TPU v7x, 32 devices: a whole 2x2x4 slice. The times are simulated.
32 devices in a mesh: dp: 8 (over z, x), rep: 4 (over y, core).
Axes of the slice: x: 2, y: 2, z: 4, core: 2. Of those that a mesh axis runs over, the one named last changes fastest.
Arguments:
- tokens: bfloat16 [4, 4096, 768], P('rep', 'dp'), may hold values from -6 to 6
- cotangent: bfloat16 [4, 4096, 768], P('rep', 'dp'), may hold values from -6 to 6
- padding: int32 [4, 4096], P('rep', 'dp'), may hold values from 0 to 1, as said below
- opening: int32 [4, 4096], P('rep', 'dp'), may hold values from 0 to 1, as said below
- w_in: float32 [768, 4992], P(('dp', 'rep')), may hold values from -0.21875 to 0.21875
- w_out: float32 [2304, 768], P(('dp', 'rep')), may hold values from -0.21875 to 0.21875
- vectors: float32 [2304], replicated, may hold values from -0.5 to 11, as said below
- m_in: float32 [768, 4992], P(('dp', 'rep')), may hold values from -0.0068359375 to 0.0068359375
- v_in: float32 [768, 4992], P(('dp', 'rep')), may hold values from 9.765625e-08 to 3.90625e-07
- m_out: float32 [2304, 768], P(('dp', 'rep')), may hold values from -0.0068359375 to 0.0068359375
- v_out: float32 [2304, 768], P(('dp', 'rep')), may hold values from 9.765625e-08 to 3.90625e-07
- m_vec: float32 [2304], replicated, may hold values from -0.0068359375 to 0.0068359375
- v_vec: float32 [2304], replicated, may hold values from 9.765625e-08 to 3.90625e-07
- counter: int32 [1], replicated, may hold values from 1 to 3
Outputs:
- block_out: bfloat16 [4, 4096, 768], P('rep', 'dp')
- d_tokens: float32 [4, 4096, 768], P('rep', 'dp')
- grad_in: float32 [768, 4992], P(('dp', 'rep'))
- new_in: float32 [768, 4992], P(('dp', 'rep'))
- first_in: float32 [768, 4992], P(('dp', 'rep'))
- second_in: float32 [768, 4992], P(('dp', 'rep'))
- copy_in: bfloat16 [768, 4992], P(('dp', 'rep'))
- grad_out: float32 [2304, 768], P(('dp', 'rep'))
- new_out: float32 [2304, 768], P(('dp', 'rep'))
- first_out: float32 [2304, 768], P(('dp', 'rep'))
- second_out: float32 [2304, 768], P(('dp', 'rep'))
- copy_out: bfloat16 [2304, 768], P(('dp', 'rep'))
- grad_vec: float32 [2304], replicated
- grad_bias: float32 [384], replicated
- update_vec: float32 [2304], replicated
- first_vec: float32 [2304], replicated
- second_vec: float32 [2304], replicated
Inputs may be any that keep to these rules, and one draw needn't show every extreme that they name: Each group's slots fall into aligned blocks of 4096; each block holds buckets of 4096, 2048 or 1024 slots, each starting at a multiple of its own length; opening is 1 exactly on each bucket's first slot. In each bucket, padding is 1 on its first slots and 0 after them; at least a quarter of each bucket's slots are 1. `vectors`: the gains and the forget biases are positive.
All inputs are finite; a program needn't handle non-finite values.
Results may differ from a plain program's by a relative error of at most 0.013.
The roundings to bfloat16 on the way count: a program that leaves them out, or rounds other values in their place, can miss the bound.
Values may be sent and summed in bfloat16 or wider, within the bound.
A program may use at most 320 MiB of HBM per device.

v0:
```python
import jax
import jax.numpy as jnp
from jax import lax
from jax.sharding import PartitionSpec as P

D = 768
CH = 384
FF = 1536


NORM_EPSILON = 1e-06
LEARN_RATE = 0.05
BETA_ONE = 0.9
BETA_TWO = 0.999
ADAM_EPSILON = 1e-08
WEIGHT_DECAY = 0.1


def complex_product(left_real, left_imag, right_real, right_imag):
    return (
        left_real * right_real - left_imag * right_imag,
        left_real * right_imag + left_imag * right_real,
    )


def compose(earlier, later):
    product = complex_product(later[0], later[1], earlier[0], earlier[1])
    carried = complex_product(later[0], later[1], earlier[2], earlier[3])
    return (product[0], product[1], carried[0] + later[2], carried[1] + later[3])


def normalize(values, gains):
    scaling = lax.rsqrt(jnp.mean(values * values, axis=-1, keepdims=True) + NORM_EPSILON)
    return (values * scaling * gains, scaling)


def normalize_back(values, scaling, gains, gradient):
    scaled = gradient * gains
    return scaling * scaled - values * scaling**3 * jnp.mean(
        values * scaled, axis=-1, keepdims=True
    )


def silu_slope(values):
    logistic = jax.nn.sigmoid(values)
    return logistic * (1.0 + values * (1.0 - logistic))


def adam_update(master, gradient, first, second, steps, decay):
    first_new = BETA_ONE * first + (1.0 - BETA_ONE) * gradient
    second_new = BETA_TWO * second + (1.0 - BETA_TWO) * gradient * gradient
    corrected = (
        first_new
        / (1.0 - BETA_ONE**steps)
        / (jnp.sqrt(second_new / (1.0 - BETA_TWO**steps)) + ADAM_EPSILON)
    )
    change = -LEARN_RATE * (corrected + decay * master)
    return (master + change, first_new, second_new, change)


def body(
    tokens,
    cotangent,
    padding,
    opening,
    w_in,
    w_out,
    vectors,
    m_in,
    v_in,
    m_out,
    v_out,
    m_vec,
    v_vec,
    counter,
):
    groups = lax.axis_size("dp")
    share = CH // groups
    mixer_cols = CH + 2 * D
    inputs = tokens[0].astype(jnp.float32)
    length = inputs.shape[0]
    filled = padding[0].astype(jnp.float32)
    starting = opening[0] == 1
    gains_one = vectors[:D]
    gains_two = vectors[D : 2 * D]
    phases = vectors[2 * D : 2 * D + CH]
    biases = vectors[2 * D + CH :]
    full_in, full_out = (
        lax.all_gather(w_in.astype(jnp.bfloat16), ("dp", "rep"), axis=0, tiled=True),
        lax.all_gather(w_out.astype(jnp.bfloat16), ("dp", "rep"), axis=0, tiled=True),
    )
    normed, scaling_one = normalize(inputs, gains_one)
    normed_low = normed.astype(jnp.bfloat16)
    pre_mix = jnp.einsum(
        "dc,td->ct", full_in[:, :mixer_cols], normed_low, preferred_element_type=jnp.float32
    )
    forget = jax.nn.sigmoid(-(pre_mix[:CH] + biases[:, None]))
    driver_pre = pre_mix[CH : CH + D]
    driver = jax.nn.silu(driver_pre)
    gate_pre = pre_mix[CH + D :]
    forget_both = jnp.concatenate([forget, forget], axis=0)
    packed = jnp.concatenate(
        [jnp.where(starting[None, :], 1.0, forget), forget_both * driver], axis=0
    ).astype(jnp.bfloat16)
    arrived = lax.all_to_all(
        packed.reshape(3, groups, share, length), "dp", split_axis=1, concat_axis=3, tiled=True
    )[:, 0].astype(jnp.float32)
    own_phase = lax.dynamic_slice_in_dim(phases, lax.axis_index("dp") * share, share)
    cosine = jnp.cos(own_phase)[:, None]
    sine = jnp.sin(own_phase)[:, None]
    retain = 1.0 - arrived[0]
    step_real = retain * cosine
    step_imag = retain * sine
    scanned = lax.associative_scan(compose, (step_real, step_imag, arrived[1], arrived[2]), axis=1)
    state_real = scanned[2]
    state_imag = scanned[3]
    outgoing = jnp.stack([state_real, state_imag]).astype(jnp.bfloat16)[:, None]
    recurrent = (
        lax.all_to_all(outgoing, "dp", split_axis=3, concat_axis=1, tiled=True)
        .reshape(2 * CH, length)
        .astype(jnp.float32)
    )
    gate_act = jax.nn.silu(gate_pre)
    masked = recurrent * filled[None, :]
    gated_rows = (masked * gate_act).astype(jnp.bfloat16)
    middle = inputs + jnp.einsum(
        "dt,de->te", gated_rows, full_out[:D], preferred_element_type=jnp.float32
    )
    normed_two, scaling_two = normalize(middle, gains_two)
    normed_two_low = normed_two.astype(jnp.bfloat16)
    glu_pre = jnp.dot(normed_two_low, full_in[:, mixer_cols:], preferred_element_type=jnp.float32)
    gate_glu = glu_pre[:, :FF]
    up_glu = glu_pre[:, FF:]
    hidden = (jax.nn.silu(gate_glu) * up_glu).astype(jnp.bfloat16)
    block_out = middle + jnp.dot(hidden, full_out[D:], preferred_element_type=jnp.float32)
    upstream = cotangent[0].astype(jnp.float32) * filled[:, None]
    upstream_low = upstream.astype(jnp.bfloat16)
    grad_down = jnp.einsum("tf,te->fe", hidden, upstream_low, preferred_element_type=jnp.float32)
    d_hidden = jnp.einsum(
        "te,fe->tf", upstream_low, full_out[D:], preferred_element_type=jnp.float32
    )
    d_glu = jnp.concatenate(
        [d_hidden * up_glu * silu_slope(gate_glu), d_hidden * jax.nn.silu(gate_glu)], axis=1
    ).astype(jnp.bfloat16)
    grad_glu = jnp.einsum("td,tc->dc", normed_two_low, d_glu, preferred_element_type=jnp.float32)
    d_normed_two = jnp.einsum(
        "tc,dc->td", d_glu, full_in[:, mixer_cols:], preferred_element_type=jnp.float32
    )
    grad_gains_two = jnp.sum(d_normed_two * middle * scaling_two, axis=0)
    d_middle = upstream + normalize_back(middle, scaling_two, gains_two, d_normed_two)
    d_mixed_low = d_middle.astype(jnp.bfloat16)
    grad_mixer_out = jnp.einsum(
        "dt,te->de", gated_rows, d_mixed_low, preferred_element_type=jnp.float32
    )
    d_gated = jnp.einsum("te,de->dt", d_mixed_low, full_out[:D], preferred_element_type=jnp.float32)
    d_recurrent = (d_gated * gate_act * filled[None, :]).astype(jnp.bfloat16)
    d_gate_pre = d_gated * masked * silu_slope(gate_pre)
    incoming = lax.all_to_all(
        d_recurrent.reshape(2, groups, share, length), "dp", split_axis=1, concat_axis=3, tiled=True
    )[:, 0].astype(jnp.float32)
    edge_zero = jnp.zeros((share, 1), jnp.float32)
    next_real = jnp.concatenate([step_real[:, 1:], edge_zero], axis=1)
    next_imag = jnp.concatenate([step_imag[:, 1:], edge_zero], axis=1)
    adjoint = lax.associative_scan(
        compose, (next_real, -next_imag, incoming[0], incoming[1]), axis=1, reverse=True
    )
    adjoint_real = adjoint[2]
    adjoint_imag = adjoint[3]
    prior_real = jnp.concatenate([edge_zero, state_real[:, :-1]], axis=1)
    prior_imag = jnp.concatenate([edge_zero, state_imag[:, :-1]], axis=1)
    turned_real = cosine * prior_real - sine * prior_imag
    turned_imag = sine * prior_real + cosine * prior_imag
    d_retain = adjoint_real * turned_real + adjoint_imag * turned_imag
    d_phase_own = jnp.sum(
        retain * (adjoint_imag * turned_real - adjoint_real * turned_imag), axis=1
    )
    d_phase = lax.dynamic_update_slice_in_dim(
        jnp.zeros((CH,), jnp.float32), d_phase_own, lax.axis_index("dp") * share, 0
    )
    leaving = jnp.stack([-d_retain, adjoint_real, adjoint_imag]).astype(jnp.bfloat16)[:, None]
    d_packed = (
        lax.all_to_all(leaving, "dp", split_axis=3, concat_axis=1, tiled=True)
        .reshape(3 * CH, length)
        .astype(jnp.float32)
    )
    d_decay = d_packed[:CH]
    d_input = d_packed[CH:]
    d_forget = jnp.where(starting[None, :], 0.0, d_decay) + jnp.sum(
        (d_input * driver).reshape(2, CH, length), axis=0
    )
    d_forget_pre = -forget * (1.0 - forget) * d_forget
    d_driver_pre = d_input * forget_both * silu_slope(driver_pre)
    d_mix = jnp.concatenate([d_forget_pre, d_driver_pre, d_gate_pre], axis=0).astype(jnp.bfloat16)
    grad_mixer_in = jnp.einsum("td,ct->dc", normed_low, d_mix, preferred_element_type=jnp.float32)
    d_normed = jnp.einsum(
        "ct,dc->td", d_mix, full_in[:, :mixer_cols], preferred_element_type=jnp.float32
    )
    grad_gains_one = jnp.sum(d_normed * inputs * scaling_one, axis=0)
    d_tokens = d_middle + normalize_back(inputs, scaling_one, gains_one, d_normed)
    grad_biases = jnp.sum(d_forget_pre, axis=1)
    grad_vectors = jnp.concatenate([grad_gains_one, grad_gains_two, d_phase, grad_biases])
    grad_in_all = jnp.concatenate([grad_mixer_in, grad_glu], axis=1)
    grad_out_all = jnp.concatenate([grad_mixer_out, grad_down], axis=0)
    summed_in, summed_out = (
        lax.psum_scatter(grad_in_all, ("dp", "rep"), scatter_dimension=0, tiled=True),
        lax.psum_scatter(grad_out_all, ("dp", "rep"), scatter_dimension=0, tiled=True),
    )
    summed_vec, total = lax.psum((grad_vectors, jnp.sum(filled)), ("dp", "rep"))
    steps = counter[0].astype(jnp.float32)
    grad_in = summed_in / total
    grad_out = summed_out / total
    grad_vec = summed_vec / total
    new_in, first_in, second_in, change_in = adam_update(
        w_in, grad_in, m_in, v_in, steps, WEIGHT_DECAY
    )
    new_out, first_out, second_out, change_out = adam_update(
        w_out, grad_out, m_out, v_out, steps, WEIGHT_DECAY
    )
    new_vec, first_vec, second_vec, update_vec = adam_update(
        vectors, grad_vec, m_vec, v_vec, steps, 0.0
    )
    return (
        block_out.astype(jnp.bfloat16)[None],
        d_tokens[None],
        grad_in,
        new_in,
        first_in,
        second_in,
        new_in.astype(jnp.bfloat16),
        grad_out,
        new_out,
        first_out,
        second_out,
        new_out.astype(jnp.bfloat16),
        grad_vec,
        grad_vec[2 * D + CH :],
        update_vec,
        first_vec,
        second_vec,
    )


def solution(mesh):
    in_specs = (
        P("rep", "dp", None),
        P("rep", "dp", None),
        P("rep", "dp"),
        P("rep", "dp"),
        P(("dp", "rep"), None),
        P(("dp", "rep"), None),
        P(),
        P(("dp", "rep"), None),
        P(("dp", "rep"), None),
        P(("dp", "rep"), None),
        P(("dp", "rep"), None),
        P(),
        P(),
        P(),
    )
    out_specs = (
        P("rep", "dp", None),
        P("rep", "dp", None),
        P(("dp", "rep"), None),
        P(("dp", "rep"), None),
        P(("dp", "rep"), None),
        P(("dp", "rep"), None),
        P(("dp", "rep"), None),
        P(("dp", "rep"), None),
        P(("dp", "rep"), None),
        P(("dp", "rep"), None),
        P(("dp", "rep"), None),
        P(("dp", "rep"), None),
        P(),
        P(),
        P(),
        P(),
        P(),
    )
    return jax.shard_map(body, mesh=mesh, in_specs=in_specs, out_specs=out_specs, check_vma=False)
```

profile of v0, /device:TPU:3, one launch (start us, length us, event | category | flops | bytes accessed | tf_op | source)
XLA Modules:
  0.0 1829.2 jit_solution(9027815124984937742)
XLA Ops:
  12.4 75.4 %all-gather.3.cloned.1.call-done = bf16[768,4992]{1,0:T(8,128)(2,1)} async-done(((bf16[24,4992]{1,0:T(8,128)(2,1)}), bf16[768,4992]{1,0:T(8,128)(2,1)}) %all-gather.3.cloned.1.call-update) | async-done | bytes 7667728 | tf_op jit(solution)/shard_map/all_gather | solution.py:89
  101.2 28.5 %all-to-all-done = bf16[3,8,48,512]{3,2,0,1:T(8,128)(2,1)S(1)} async-done(((bf16[3,8,48,512]{3,2,0,1:T(8,128)(2,1)}), bf16[3,8,48,512]{3,2,0,1:T(8,128)(2,1)S(1)}, u32[]{:S(2)}, u32[]{:S(2)}) %all-to-all-start) | async-done | bytes 1179680 | tf_op jit(solution)/shard_map/all_to_all | solution.py:105
  131.0 13.8 slice.1434
  144.7 13.8 slice.1267
  158.5 13.8 slice.1258
  173.0 14.0 slice.1432
  186.9 13.8 slice.1259
  200.7 13.8 slice.1255
  214.8 14.2 slice.1261
  229.0 13.8 slice.1254
  242.7 13.8 slice.1253
  256.5 13.9 slice.1428
  270.4 13.8 slice.1262
  284.2 13.8 slice.1256
  555.5 8.9 pad.339
  568.3 13.3 pad.342
  582.8 14.7 pad.340
  597.5 16.1 pad.341
  613.6 15.9 pad.343
  637.5 8.8 reshape.229
  655.3 15.1 all-to-all-done.1
  670.3 9.3 reshape.230
  726.2 15.0 slice.1460
  741.3 14.7 slice.1447
  755.9 14.7 slice.1445
  770.6 13.9 slice.1630
  784.5 13.2 slice.1462
  797.7 13.8 slice.1452
  828.5 8.6 slice.1448
  868.8 13.2 slice.1468
  882.0 13.8 slice.1455
  897.9 15.1 slice.1457
  913.0 14.7 slice.1449
  941.8 8.5 slice.1450
  1266.1 13.8 slice.1640
  1279.9 14.8 slice.1635
  1451.1 8.9 pad.387
  1464.8 14.7 pad.390
  1479.5 14.8 pad.389
  1494.4 14.8 pad.391
  1510.7 11.0 rev.5
  1522.7 14.7 pad.388
  1539.8 15.8 rev.4
  1577.8 8.8 fusion.12
  1586.5 18.8 %all-to-all-done.3 = bf16[8,2,36864]{2,1,0:T(2,128)(2,1)S(1)} async-done(((bf16[8,2,36864]{2,1,0:T(2,128)(2,1)}), bf16[8,2,36864]{2,1,0:T(2,128)(2,1)S(1)}, u32[]{:S(2)}, u32[]{:S(2)}) %all-to-all-start.3) | async-done | bytes 1179680 | tf_op jit(solution)/shard_map/all_to_all | solution.py:182
  1642.0 9.9 pad_maximum_fusion
  1662.8 38.6 %all-reduce.101 = (f32[]{:T(128)}, f32[2304]{0:T(1024)S(1)}) all-reduce(f32[]{:T(128)} %convert_reduce_fusion, f32[2304]{0:T(1024)S(1)} %pad_maximum_fusion.56), channel_id=1, replica_groups=mesh['dp'=8,'rep'=4] {'dp','rep'}, use_global_device_ids=true, to_apply=%region_7.8 | all-reduce | flops 2305 | bytes 18440 | tf_op jit(solution)/shard_map/psum | solution.py:208
  1709.1 110.2 %reduce-scatter.7.cloned.1.call-done = f32[24,4992]{1,0:T(8,128)} async-done(((f32[768,4992]{1,0:T(8,128)}), f32[24,4992]{1,0:T(8,128)}) %reduce-scatter.7.cloned.1.call-update) | async-done | bytes 479248
  (816 shorter events, 970.5 us)
Async XLA Ops:
  7.2 80.6 %copy-start.7 = (bf16[1,512,768]{2,1,0:T(8,128)(2,1)S(1)}, bf16[1,512,768]{2,1,0:T(8,128)(2,1)}, u32[]{:S(2)}) copy-start(bf16[1,512,768]{2,1,0:T(8,128)(2,1)} %param.14) | copy-start | bytes 2359300
  7.2 80.6 %all-gather.3.cloned.1.call-start = ((), (), s32[]{:S(2)}) async-start(), calls=%async_computation.6 | async-start | bytes 7907328 | tf_op jit(solution)/shard_map/all_gather | solution.py:89
  9.8 81.7 %copy-start.108 = (pred[512]{0:T(512)(128)(4,1)}, pred[512]{0:T(512)(128)(4,1)S(1)}, u32[]{:S(2)}) copy-start(pred[512]{0:T(512)(128)(4,1)S(1)} %compare_reduce_fusion) | copy-start | bytes 1540
  95.3 34.4 %all-to-all-start = ((bf16[3,8,48,512]{3,2,0,1:T(8,128)(2,1)}), bf16[3,8,48,512]{3,2,0,1:T(8,128)(2,1)S(1)}, u32[]{:S(2)}, u32[]{:S(2)}) async-start(bf16[3,8,48,512]{3,2,0,1:T(8,128)(2,1)} %copy.202), calls=%async_computation | async-start | bytes 2359296 | tf_op jit(solution)/shard_map/all_to_all | solution.py:105
  99.5 594.5 %all-gather.5.cloned.1.call-start = ((), (), s32[]{:S(2)}) async-start(), calls=%async_computation.7 | async-start | bytes 3649536 | tf_op jit(solution)/shard_map/all_gather | solution.py:90
  100.4 591.2 %copy-start.99 = (f32[1,512]{1,0:T(1,128)}, f32[1,512]{1,0:T(1,128)S(1)}, u32[]{:S(2)}) copy-start(f32[1,512]{1,0:T(1,128)S(1)} %convert_element_type.138) | copy-start | bytes 6148
  101.2 113.4 %copy-start.110 = (f32[48]{0:T(128)}, f32[48]{0:T(128)S(1)}, u32[]{:S(2)}) copy-start(f32[48]{0:T(128)S(1)} %get-tuple-element.252) | copy-start | bytes 580
  101.2 113.4 %copy-start.112 = (f32[48]{0:T(128)}, f32[48]{0:T(128)S(1)}, u32[]{:S(2)}) copy-start(f32[48]{0:T(128)S(1)} %get-tuple-element.253) | copy-start | bytes 580
  214.5 14.4 copy-start.5
  347.6 45.0 %copy-start.43 = (f32[48,1024]{1,0:T(8,128)S(1)}, f32[48,1024]{1,0:T(8,128)}, u32[]{:S(2)}) copy-start(f32[48,1024]{1,0:T(8,128)} %slice.1271) | copy-start | bytes 589828
  347.6 45.0 %copy-start.44 = (f32[48,1024]{1,0:T(8,128)S(1)}, f32[48,1024]{1,0:T(8,128)}, u32[]{:S(2)}) copy-start(f32[48,1024]{1,0:T(8,128)} %slice.1264) | copy-start | bytes 589828
  514.1 17.4 copy-start.45
  514.1 17.4 copy-start.46
  646.4 24.0 %all-to-all-start.1 = ((bf16[8,2,24576]{2,1,0:T(2,128)(2,1)}), bf16[8,2,24576]{2,1,0:T(2,128)(2,1)}, u32[]{:S(2)}, u32[]{:S(2)}) async-start(bf16[8,2,24576]{2,1,0:T(2,128)(2,1)} %reshape.229), calls=%async_computation.1 | async-start | bytes 1572864 | tf_op jit(solution)/shard_map/all_to_all | solution.py:119
  718.3 148.0 %all-to-all-start.2 = ((bf16[2,8,48,512]{3,2,0,1:T(8,128)(2,1)}), bf16[2,8,48,512]{3,2,0,1:T(8,128)(2,1)}, u32[]{:S(2)}, u32[]{:S(2)}) async-start(bf16[2,8,48,512]{3,2,0,1:T(8,128)(2,1)} %copy.211), calls=%async_computation.2 | async-start | bytes 1572864 | tf_op jit(solution)/shard_map/all_to_all | solution.py:158
  722.9 983.4 %reduce-scatter.5.cloned.1.call-start = ((), (), s32[]{:S(2)}) async-start(), calls=%async_computation.8 | async-start | bytes 7299072 | tf_op jit(solution)/shard_map/reduce_scatter | solution.py:206
  726.2 44.4 %copy-start.14 = (f32[48,4096]{1,0:T(8,128)S(1)}, f32[48,4096]{1,0:T(8,128)}, u32[]{:S(2)}) copy-start(f32[48,4096]{1,0:T(8,128)} %pad_negate_fusion) | copy-start | bytes 2359300
  828.5 31.3 %copy-start.19 = (bf16[768,512]{0,1:T(8,128)(2,1)S(1)}, bf16[768,512]{0,1:T(8,128)(2,1)}, u32[]{:S(2)}) copy-start(bf16[768,512]{0,1:T(8,128)(2,1)} %copy-done.18) | copy-start | bytes 2359300
  1279.9 40.2 %copy-start.24 = (f32[48,2048]{1,0:T(8,128)S(1)}, f32[48,2048]{1,0:T(8,128)}, u32[]{:S(2)}) copy-start(f32[48,2048]{1,0:T(8,128)} %get-tuple-element.85) | copy-start | bytes 1179652
  1312.9 68.4 %copy-start.27 = (f32[48,2047]{1,0:T(8,128)S(1)}, f32[48,2047]{1,0:T(8,128)}, u32[]{:S(2)}) copy-start(f32[48,2047]{1,0:T(8,128)} %slice.1640) | copy-start | bytes 1179076
  1320.2 39.0 %copy-start.50 = (f32[48,512]{1,0:T(8,128)S(1)}, f32[48,512]{1,0:T(8,128)}, u32[]{:S(2)}) copy-start(f32[48,512]{1,0:T(8,128)} %get-tuple-element.118) | copy-start | bytes 294916
  1320.2 41.3 %copy-start.51 = (f32[48,512]{1,0:T(8,128)S(1)}, f32[48,512]{1,0:T(8,128)}, u32[]{:S(2)}) copy-start(f32[48,512]{1,0:T(8,128)} %get-tuple-element.119) | copy-start | bytes 294916
  1320.2 51.7 %copy-start.59 = (f32[48,256]{1,0:T(8,128)S(1)}, f32[48,256]{1,0:T(8,128)}, u32[]{:S(2)}) copy-start(f32[48,256]{1,0:T(8,128)} %get-tuple-element.115) | copy-start | bytes 147460
  1320.2 55.0 %copy-start.60 = (f32[48,128]{1,0:T(8,128)S(1)}, f32[48,128]{1,0:T(8,128)}, u32[]{:S(2)}) copy-start(f32[48,128]{1,0:T(8,128)} %get-tuple-element.177) | copy-start | bytes 73732
  1320.2 55.5 %copy-start.52 = (f32[48,128]{1,0:T(8,128)S(1)}, f32[48,128]{1,0:T(8,128)}, u32[]{:S(2)}) copy-start(f32[48,128]{1,0:T(8,128)} %get-tuple-element.220) | copy-start | bytes 73732
  1320.2 55.9 %copy-start.53 = (f32[48,128]{1,0:T(8,128)S(1)}, f32[48,128]{1,0:T(8,128)}, u32[]{:S(2)}) copy-start(f32[48,128]{1,0:T(8,128)} %get-tuple-element.221) | copy-start | bytes 73732
  1320.2 58.4 %copy-start.55 = (f32[48,64]{1,0:T(8,128)S(1)}, f32[48,64]{1,0:T(8,128)}, u32[]{:S(2)}) copy-start(f32[48,64]{1,0:T(8,128)} %get-tuple-element.172) | copy-start | bytes 36868
  1320.2 58.7 %copy-start.54 = (f32[48,64]{1,0:T(8,128)S(1)}, f32[48,64]{1,0:T(8,128)}, u32[]{:S(2)}) copy-start(f32[48,64]{1,0:T(8,128)} %get-tuple-element.173) | copy-start | bytes 36868
  1327.7 59.2 %copy-start.28 = (f32[48,2047]{1,0:T(8,128)S(1)}, f32[48,2047]{1,0:T(8,128)}, u32[]{:S(2)}) copy-start(f32[48,2047]{1,0:T(8,128)} %slice.1635) | copy-start | bytes 1179076
  1349.8 43.4 %copy-start.56 = (f32[48,32]{1,0:T(8,128)S(1)}, f32[48,32]{1,0:T(8,128)}, u32[]{:S(2)}) copy-start(f32[48,32]{1,0:T(8,128)} %get-tuple-element.216) | copy-start | bytes 18436
  1361.5 31.5 %copy-start.82 = (f32[48,16]{1,0:T(8,128)S(1)}, f32[48,16]{1,0:T(8,128)}, u32[]{:S(2)}) copy-start(f32[48,16]{1,0:T(8,128)} %pad_maximum_fusion.49) | copy-start | bytes 9220
  1409.8 17.4 copy-start.47
  1409.8 17.4 copy-start.48
  1464.6 14.9 copy-start.30
  1464.6 29.7 %copy-start.29 = (f32[48,2048]{1,0:T(8,128)S(1)}, f32[48,2048]{1,0:T(8,128)}, u32[]{:S(2)}) copy-start(f32[48,2048]{1,0:T(8,128)} %add.1180) | copy-start | bytes 1179652
  1537.4 18.3 copy-start.6
  1537.4 18.3 copy-start.111
  1537.4 18.3 copy-start.113
  1572.1 33.2 %all-to-all-start.3 = ((bf16[8,2,36864]{2,1,0:T(2,128)(2,1)}), bf16[8,2,36864]{2,1,0:T(2,128)(2,1)S(1)}, u32[]{:S(2)}, u32[]{:S(2)}) async-start(bf16[8,2,36864]{2,1,0:T(2,128)(2,1)} %reshape.231), calls=%async_computation.3 | async-start | bytes 2359296 | tf_op jit(solution)/shard_map/all_to_all | solution.py:182
  1577.5 241.8 %reduce-scatter.7.cloned.1.call-start = ((), (), s32[]{:S(2)}) async-start(), calls=%async_computation.9 | async-start | bytes 15814656
  1660.5 40.9 %copy-start.98 = (f32[2304]{0:T(1024)S(1)}, f32[2304]{0:T(1024)}, u32[]{:S(2)}) copy-start(f32[2304]{0:T(1024)} %param.20) | copy-start | bytes 27652
  1660.5 40.9 %copy-start.103 = (f32[2304]{0:T(1024)S(1)}, f32[2304]{0:T(1024)}, u32[]{:S(2)}) copy-start(f32[2304]{0:T(1024)} %param.26) | copy-start | bytes 27652
  1660.5 40.9 %copy-start.104 = (f32[2304]{0:T(1024)S(1)}, f32[2304]{0:T(1024)}, u32[]{:S(2)}) copy-start(f32[2304]{0:T(1024)} %param.25) | copy-start | bytes 27652
  1660.5 42.7 %copy-start.115 = (f32[512]{0:T(512)S(1)}, f32[512]{0:T(512)}, u32[]{:S(2)}) copy-start(f32[512]{0:T(512)} %get-tuple-element.20) | copy-start | bytes 6148
  1660.6 42.7 %copy-start.105 = (f32[512]{0:T(512)S(1)}, f32[512]{0:T(512)}, u32[]{:S(2)}) copy-start(f32[512]{0:T(512)} %get-tuple-element.248) | copy-start | bytes 6148
  1706.3 113.0 %copy-start.25 = (f32[24,4992]{1,0:T(8,128)S(1)}, f32[24,4992]{1,0:T(8,128)}, u32[]{:S(2)}) copy-start(f32[24,4992]{1,0:T(8,128)} %param.18) | copy-start | bytes 1437700
  1706.3 113.0 %copy-start.57 = (f32[24,4992]{1,0:T(8,128)S(1)}, f32[24,4992]{1,0:T(8,128)}, u32[]{:S(2)}) copy-start(f32[24,4992]{1,0:T(8,128)} %param.22) | copy-start | bytes 1437700
  1706.3 113.0 %copy-start.58 = (f32[24,4992]{1,0:T(8,128)S(1)}, f32[24,4992]{1,0:T(8,128)}, u32[]{:S(2)}) copy-start(f32[24,4992]{1,0:T(8,128)} %param.21) | copy-start | bytes 1437700
  (80 other events, 459.5 us)
Sparse Core Ops, SparseCore 0:
  11.4 76.2 all-gather.2
  103.8 66.8 all-gather.4
  866.5 118.9 reduce-scatter.4
  1652.1 167.1 reduce-scatter.6
where the time goes:
time: 1850 us; the launch traced here: 1830 us
  local copies, waits for them, and re-layouts  1320 us (71%)
  waiting for transfers between devices  248 us (13%)
  other arithmetic  138 us (7%)
  matrix products  43.2 us (2%)
  blocking collectives  38.6 us (2%)
  starting transfers between devices  19.2 us (1%)
    slice x146, local copies, waits for them, and re-layouts, body(): lax.associative_scan(compose, (next_real, -next_imag, incoming[0], incomi...  558 us
    slice x138, local copies, waits for them, and re-layouts, body(): lax.associative_scan(compose, (step_real, step_imag, arrived[1], arrived[...  359 us
    pad x44, local copies, waits for them, and re-layouts, body(): lax.associative_scan(compose, (next_real, -next_imag, incoming[0], incomi...  141 us
    pad x44, local copies, waits for them, and re-layouts, body(): lax.associative_scan(compose, (step_real, step_imag, arrived[1], arrived[...  119 us
    unnamed x5, waiting for transfers between devices  110 us
    all_gather x1, waiting for transfers between devices, body(): lax.all_gather(w_in.astype(jnp.bfloat16), ('dp', 'rep'), axis=0, tiled=True)  75.4 us
    unnamed x255, local copies, waits for them, and re-layouts  69.9 us
    psum x1, blocking collectives, body(): summed_vec, total = lax.psum((grad_vectors, jnp.sum(filled)), ('dp', 'rep'))  38.6 us
  transfers between devices with their start and end apart: 8, of which 5 were waited for; matrix products, arithmetic and copies ran while one was open for 80% of the time, Pallas kernels for 0%

commit v1 on v0

v1 whole, which is shorter than its diff:
```python
import jax
import jax.numpy as jnp
from jax import lax
from jax.experimental import pallas as pl
from jax.experimental.pallas import tpu as pltpu
from jax.sharding import PartitionSpec as P

D = 768
CH = 384
FF = 1536


NORM_EPSILON = 1e-06
LEARN_RATE = 0.05
BETA_ONE = 0.9
BETA_TWO = 0.999
ADAM_EPSILON = 1e-08
WEIGHT_DECAY = 0.1


LANES = 8


def rotate(real, imag, cosine, sine):
    return cosine * real - sine * imag, sine * real + cosine * imag


def turn_power(cosine, sine, doublings):
    for _ in range(doublings):
        cosine, sine = cosine * cosine - sine * sine, 2.0 * cosine * sine
    return cosine, sine


def local_forward(retain, drive_re, drive_im, turn, summary):
    steps = retain.shape[0] // LANES
    cosine, sine = turn[0:1], turn[1:2]
    zero = jnp.zeros((LANES, retain.shape[1]), jnp.float32)

    def step(i, carry):
        real, imag, product = carry
        rows = pl.ds(pl.multiple_of(LANES * i, LANES), LANES)
        r = retain[rows, :]
        turned_re, turned_im = rotate(real, imag, cosine, sine)
        return r * turned_re + drive_re[rows, :], r * turned_im + drive_im[rows, :], r * product

    real, imag, product = lax.fori_loop(0, steps, step, (zero, zero, zero + 1.0), unroll=4)
    cos_sub, sin_sub = turn_power(cosine, sine, steps.bit_length() - 1)
    total_re, total_im, total = real[0:1], imag[0:1], product[0:1]
    for j in range(1, LANES):
        turned_re, turned_im = rotate(total_re, total_im, cos_sub, sin_sub)
        total_re = product[j : j + 1] * turned_re + real[j : j + 1]
        total_im = product[j : j + 1] * turned_im + imag[j : j + 1]
        total = product[j : j + 1] * total
    summary[0:LANES] = real
    summary[LANES : 2 * LANES] = imag
    summary[2 * LANES : 3 * LANES] = product
    summary[24:25] = total_re
    summary[25:26] = total_im
    summary[26:27] = total


def whole_forward(retain, drive_re, drive_im, turn, summary, start, states):
    steps = retain.shape[0] // LANES
    cosine, sine = turn[0:1], turn[1:2]
    cos_sub, sin_sub = turn_power(cosine, sine, steps.bit_length() - 1)
    now_re, now_im = start[0:1], start[1:2]
    reals, imags = [now_re], [now_im]
    for j in range(LANES - 1):
        turned_re, turned_im = rotate(now_re, now_im, cos_sub, sin_sub)
        product = summary[2 * LANES + j : 2 * LANES + j + 1]
        now_re = product * turned_re + summary[j : j + 1]
        now_im = product * turned_im + summary[LANES + j : LANES + j + 1]
        reals.append(now_re)
        imags.append(now_im)
    carry = (jnp.concatenate(reals, axis=0), jnp.concatenate(imags, axis=0))

    def step(i, carry):
        real, imag = carry
        rows = pl.ds(pl.multiple_of(LANES * i, LANES), LANES)
        states[0, rows, :] = real
        states[1, rows, :] = imag
        r = retain[rows, :]
        turned_re, turned_im = rotate(real, imag, cosine, sine)
        return r * turned_re + drive_re[rows, :], r * turned_im + drive_im[rows, :]

    real, imag = lax.fori_loop(0, steps, step, carry, unroll=4)
    states[0, LANES * steps :, :] = real
    states[1, LANES * steps :, :] = imag


def local_backward(retain, grad_re, grad_im, turn, summary):
    steps = retain.shape[0] // LANES
    cosine, sine = turn[0:1], -turn[1:2]
    zero = jnp.zeros((LANES, retain.shape[1]), jnp.float32)

    def step(k, carry):
        real, imag, product = carry
        rows = pl.ds(pl.multiple_of(LANES * (steps - 1 - k), LANES), LANES)
        r = retain[rows, :]
        turned_re, turned_im = rotate(grad_re[rows, :] + real, grad_im[rows, :] + imag, cosine, sine)
        return r * turned_re, r * turned_im, r * product

    real, imag, product = lax.fori_loop(0, steps, step, (zero, zero, zero + 1.0), unroll=4)
    cos_sub, sin_sub = turn_power(cosine, sine, steps.bit_length() - 1)
    last = LANES - 1
    total_re, total_im, total = real[last:], imag[last:], product[last:]
    for j in range(LANES - 2, -1, -1):
        turned_re, turned_im = rotate(total_re, total_im, cos_sub, sin_sub)
        total_re = product[j : j + 1] * turned_re + real[j : j + 1]
        total_im = product[j : j + 1] * turned_im + imag[j : j + 1]
        total = product[j : j + 1] * total
    summary[0:LANES] = real
    summary[LANES : 2 * LANES] = imag
    summary[2 * LANES : 3 * LANES] = product
    summary[24:25] = total_re
    summary[25:26] = total_im
    summary[26:27] = total


def whole_backward(
    retain, grad_re, grad_im, turn, summary, start, states, d_decay, d_in_re, d_in_im, d_phase
):
    steps = retain.shape[0] // LANES
    cosine, sine = turn[0:1], turn[1:2]
    cos_sub, sin_sub = turn_power(cosine, -sine, steps.bit_length() - 1)
    now_re, now_im = start[0:1], start[1:2]
    reals, imags = [now_re], [now_im]
    for j in range(LANES - 1, 0, -1):
        turned_re, turned_im = rotate(now_re, now_im, cos_sub, sin_sub)
        product = summary[2 * LANES + j : 2 * LANES + j + 1]
        now_re = product * turned_re + summary[j : j + 1]
        now_im = product * turned_im + summary[LANES + j : LANES + j + 1]
        reals.append(now_re)
        imags.append(now_im)
    zero = jnp.zeros((LANES, retain.shape[1]), jnp.float32)
    carry = (jnp.concatenate(reals[::-1], axis=0), jnp.concatenate(imags[::-1], axis=0), zero)

    def step(k, carry):
        real, imag, phase = carry
        rows = pl.ds(pl.multiple_of(LANES * (steps - 1 - k), LANES), LANES)
        r = retain[rows, :]
        real = grad_re[rows, :] + real
        imag = grad_im[rows, :] + imag
        prior_re, prior_im = rotate(states[0, rows, :], states[1, rows, :], cosine, sine)
        d_decay[rows, :] = -(real * prior_re + imag * prior_im)
        d_in_re[rows, :] = real
        d_in_im[rows, :] = imag
        phase = phase + r * (imag * prior_re - real * prior_im)
        turned_re, turned_im = rotate(real, imag, cosine, -sine)
        return r * turned_re, r * turned_im, phase

    _, _, phase = lax.fori_loop(0, steps, step, carry, unroll=4)
    d_phase[...] = jnp.sum(phase, axis=0, keepdims=True)


def stripe(rows):
    count, columns = rows.shape
    return rows.reshape(LANES, count // LANES, columns).swapaxes(0, 1).reshape(count, columns)


def unstripe(rows):
    count, columns = rows.shape
    return rows.reshape(count // LANES, LANES, columns).swapaxes(0, 1).reshape(count, columns)


def local_call(kernel, outs, *args):
    return pl.pallas_call(
        kernel,
        out_shape=[jax.ShapeDtypeStruct(shape, jnp.float32) for shape in outs],
        compiler_params=pltpu.CompilerParams(vmem_limit_bytes=32 * 1024 * 1024),
    )(*args)


def carry_in(summary, turn, length, reverse):
    every = lax.all_gather(summary[24:27], "dp", axis=0)
    cosine, sine = turn_power(
        turn[0], -turn[1] if reverse else turn[1], length.bit_length() - 1
    )
    count = every.shape[0]
    me = lax.axis_index("dp")
    real = jnp.zeros_like(cosine)
    imag = jnp.zeros_like(cosine)
    order = range(count - 1, 0, -1) if reverse else range(count - 1)
    for j in order:
        use = (j > me) if reverse else (j < me)
        turned_re, turned_im = rotate(real, imag, cosine, sine)
        real = jnp.where(use, every[j, 2] * turned_re + every[j, 0], real)
        imag = jnp.where(use, every[j, 2] * turned_im + every[j, 1], imag)
    return jnp.stack([real, imag])


def normalize(values, gains):
    scaling = lax.rsqrt(jnp.mean(values * values, axis=-1, keepdims=True) + NORM_EPSILON)
    return (values * scaling * gains, scaling)


def normalize_back(values, scaling, gains, gradient):
    scaled = gradient * gains
    return scaling * scaled - values * scaling**3 * jnp.mean(
        values * scaled, axis=-1, keepdims=True
    )


def silu_slope(values):
    logistic = jax.nn.sigmoid(values)
    return logistic * (1.0 + values * (1.0 - logistic))


def adam_update(master, gradient, first, second, steps, decay):
    first_new = BETA_ONE * first + (1.0 - BETA_ONE) * gradient
    second_new = BETA_TWO * second + (1.0 - BETA_TWO) * gradient * gradient
    corrected = (
        first_new
        / (1.0 - BETA_ONE**steps)
        / (jnp.sqrt(second_new / (1.0 - BETA_TWO**steps)) + ADAM_EPSILON)
    )
    change = -LEARN_RATE * (corrected + decay * master)
    return (master + change, first_new, second_new, change)


def body(
    tokens,
    cotangent,
    padding,
    opening,
    w_in,
    w_out,
    vectors,
    m_in,
    v_in,
    m_out,
    v_out,
    m_vec,
    v_vec,
    counter,
):
    low = jnp.bfloat16
    wide = jnp.float32
    mixer_cols = CH + 2 * D
    length = tokens.shape[1]
    inputs = stripe(tokens[0]).astype(wide)
    filled = stripe(padding[0][:, None]).astype(wide)
    starting = stripe(opening[0][:, None]) == 1
    gains_one = vectors[:D]
    gains_two = vectors[D : 2 * D]
    phases = vectors[2 * D : 2 * D + CH]
    biases = vectors[2 * D + CH :]
    turn = jnp.stack([jnp.cos(phases), jnp.sin(phases)])
    full_in = lax.all_gather(w_in.astype(low), ("dp", "rep"), axis=0, tiled=True)
    full_out = lax.all_gather(w_out.astype(low), ("dp", "rep"), axis=0, tiled=True)
    normed, scaling_one = normalize(inputs, gains_one)
    normed_low = normed.astype(low)
    pre_mix = jnp.dot(normed_low, full_in[:, :mixer_cols], preferred_element_type=wide)
    forget = jax.nn.sigmoid(-(pre_mix[:, :CH] + biases))
    driver_pre = pre_mix[:, CH : CH + D]
    driver = jax.nn.silu(driver_pre)
    gate_pre = pre_mix[:, CH + D :]
    forget_both = jnp.concatenate([forget, forget], axis=1)
    decay = jnp.where(starting, 1.0, forget).astype(low).astype(wide)
    retain = 1.0 - decay
    drive = (forget_both * driver).astype(low).astype(wide)
    drive_re, drive_im = drive[:, :CH], drive[:, CH:]
    summary = local_call(local_forward, [(32, CH)], retain, drive_re, drive_im, turn)[0]
    start = carry_in(summary, turn, length, False)
    states = local_call(
        whole_forward, [(2, length + 8, CH)], retain, drive_re, drive_im, turn, summary, start
    )[0]
    recurrent = jnp.concatenate([states[0, LANES:], states[1, LANES:]], axis=1)
    recurrent = recurrent.astype(low).astype(wide)
    gate_act = jax.nn.silu(gate_pre)
    masked = recurrent * filled
    gated_rows = (masked * gate_act).astype(low)
    middle = inputs + jnp.dot(gated_rows, full_out[:D], preferred_element_type=wide)
    normed_two, scaling_two = normalize(middle, gains_two)
    normed_two_low = normed_two.astype(low)
    glu_pre = jnp.dot(normed_two_low, full_in[:, mixer_cols:], preferred_element_type=wide)
    gate_glu = glu_pre[:, :FF]
    up_glu = glu_pre[:, FF:]
    hidden = (jax.nn.silu(gate_glu) * up_glu).astype(low)
    block_out = middle + jnp.dot(hidden, full_out[D:], preferred_element_type=wide)
    upstream = stripe(cotangent[0]).astype(wide) * filled
    upstream_low = upstream.astype(low)
    grad_down = jnp.einsum("tf,te->fe", hidden, upstream_low, preferred_element_type=wide)
    d_hidden = jnp.einsum("te,fe->tf", upstream_low, full_out[D:], preferred_element_type=wide)
    d_glu = jnp.concatenate(
        [d_hidden * up_glu * silu_slope(gate_glu), d_hidden * jax.nn.silu(gate_glu)], axis=1
    ).astype(low)
    grad_glu = jnp.einsum("td,tc->dc", normed_two_low, d_glu, preferred_element_type=wide)
    d_normed_two = jnp.einsum(
        "tc,dc->td", d_glu, full_in[:, mixer_cols:], preferred_element_type=wide
    )
    grad_gains_two = jnp.sum(d_normed_two * middle * scaling_two, axis=0)
    d_middle = upstream + normalize_back(middle, scaling_two, gains_two, d_normed_two)
    d_mixed_low = d_middle.astype(low)
    grad_mixer_out = jnp.einsum("td,te->de", gated_rows, d_mixed_low, preferred_element_type=wide)
    d_gated = jnp.einsum("te,de->td", d_mixed_low, full_out[:D], preferred_element_type=wide)
    d_recurrent = (d_gated * gate_act * filled).astype(low).astype(wide)
    d_gate_pre = d_gated * masked * silu_slope(gate_pre)
    grad_re, grad_im = d_recurrent[:, :CH], d_recurrent[:, CH:]
    summary_back = local_call(local_backward, [(32, CH)], retain, grad_re, grad_im, turn)[0]
    start_back = carry_in(summary_back, turn, length, True)
    d_decay, d_in_re, d_in_im, d_phase = local_call(
        whole_backward,
        [(length, CH)] * 3 + [(1, CH)],
        retain,
        grad_re,
        grad_im,
        turn,
        summary_back,
        start_back,
        states,
    )
    d_decay = d_decay.astype(low).astype(wide)
    d_input = jnp.concatenate([d_in_re, d_in_im], axis=1).astype(low).astype(wide)
    pulled = d_input * driver
    d_forget = jnp.where(starting, 0.0, d_decay) + pulled[:, :CH] + pulled[:, CH:]
    d_forget_pre = -forget * (1.0 - forget) * d_forget
    d_driver_pre = d_input * forget_both * silu_slope(driver_pre)
    d_mix = jnp.concatenate([d_forget_pre, d_driver_pre, d_gate_pre], axis=1).astype(low)
    grad_mixer_in = jnp.einsum("td,tc->dc", normed_low, d_mix, preferred_element_type=wide)
    d_normed = jnp.einsum(
        "tc,dc->td", d_mix, full_in[:, :mixer_cols], preferred_element_type=wide
    )
    grad_gains_one = jnp.sum(d_normed * inputs * scaling_one, axis=0)
    d_tokens = d_middle + normalize_back(inputs, scaling_one, gains_one, d_normed)
    grad_biases = jnp.sum(d_forget_pre, axis=0)
    grad_vectors = jnp.concatenate([grad_gains_one, grad_gains_two, d_phase[0], grad_biases])
    grad_in_all = jnp.concatenate([grad_mixer_in, grad_glu], axis=1)
    grad_out_all = jnp.concatenate([grad_mixer_out, grad_down], axis=0)
    summed_in, summed_out = (
        lax.psum_scatter(grad_in_all, ("dp", "rep"), scatter_dimension=0, tiled=True),
        lax.psum_scatter(grad_out_all, ("dp", "rep"), scatter_dimension=0, tiled=True),
    )
    summed_vec, total = lax.psum((grad_vectors, jnp.sum(filled)), ("dp", "rep"))
    steps = counter[0].astype(jnp.float32)
    grad_in = summed_in / total
    grad_out = summed_out / total
    grad_vec = summed_vec / total
    new_in, first_in, second_in, change_in = adam_update(
        w_in, grad_in, m_in, v_in, steps, WEIGHT_DECAY
    )
    new_out, first_out, second_out, change_out = adam_update(
        w_out, grad_out, m_out, v_out, steps, WEIGHT_DECAY
    )
    new_vec, first_vec, second_vec, update_vec = adam_update(
        vectors, grad_vec, m_vec, v_vec, steps, 0.0
    )
    return (
        unstripe(block_out.astype(jnp.bfloat16))[None],
        unstripe(d_tokens)[None],
        grad_in,
        new_in,
        first_in,
        second_in,
        new_in.astype(jnp.bfloat16),
        grad_out,
        new_out,
        first_out,
        second_out,
        new_out.astype(jnp.bfloat16),
        grad_vec,
        grad_vec[2 * D + CH :],
        update_vec,
        first_vec,
        second_vec,
    )


def solution(mesh):
    in_specs = (
        P("rep", "dp", None),
        P("rep", "dp", None),
        P("rep", "dp"),
        P("rep", "dp"),
        P(("dp", "rep"), None),
        P(("dp", "rep"), None),
        P(),
        P(("dp", "rep"), None),
        P(("dp", "rep"), None),
        P(("dp", "rep"), None),
        P(("dp", "rep"), None),
        P(),
        P(),
        P(),
    )
    out_specs = (
        P("rep", "dp", None),
        P("rep", "dp", None),
        P(("dp", "rep"), None),
        P(("dp", "rep"), None),
        P(("dp", "rep"), None),
        P(("dp", "rep"), None),
        P(("dp", "rep"), None),
        P(("dp", "rep"), None),
        P(("dp", "rep"), None),
        P(("dp", "rep"), None),
        P(("dp", "rep"), None),
        P(("dp", "rep"), None),
        P(),
        P(),
        P(),
        P(),
        P(),
    )
    return jax.shard_map(body, mesh=mesh, in_specs=in_specs, out_specs=out_specs, check_vma=False)
```

time: 1850 us -> 480 us (0.26)
  local copies, waits for them, and re-layouts: 1320 us -> 8.94 us
  other arithmetic: 138 us -> 28.4 us
  blocking collectives: 38.6 us -> 92.7 us
  waiting for transfers between devices: 248 us -> 286 us
  starting transfers between devices: 19.2 us -> 0.16 us
    slice x294 -> x6, local copies, waits for them, and re-layouts: 929 us -> 0.45 us  [the longest x4 0.24 us: carry_in(): real = jnp.where(use, every[j, 2] * turned_re + every[j, 0], real)]
    pad x88 -> x0, local copies, waits for them, and re-layouts: 260 us -> none  [the longest x44 141 us: body(): lax.associative_scan(compose, (next_real, -next_imag, incoming[0], incomi...]
    unnamed x255 -> x72, local copies, waits for them, and re-layouts: 69.9 us -> 3.5 us
    unnamed x5, waiting for transfers between devices: 110 us -> 173 us
    all_to_all x4 -> x0, waiting for transfers between devices: 62.3 us -> none  [the longest x1 28.5 us: body(): lax.all_to_all(packed.reshape(3, groups, share, length), 'dp', split_axis...]
    add x84 -> x0, other arithmetic: 52.1 us -> none  [the longest x35 24.8 us: compose(): carried[1] + later[3]]
    all_gather x0 -> x2, blocking collectives: none -> 46.4 us  [carry_in(): every = lax.all_gather(summary[24:27], 'dp', axis=0)]
    all_gather x2, waiting for transfers between devices: 75.4 us -> 103 us  [the longest x1 72.8 us: body(): lax.all_gather(w_in.astype(low), ('dp', 'rep'), axis=0, tiled=True)]
  transfers between devices with their start and end apart: 8 -> 4, of which waited for: 5 -> 4; matrix products, arithmetic and copies ran while one was open for 80% -> 10% of each run, Pallas kernels for 0% -> 1%
where the time goes in v1:
time: 480 us; the launch traced here: 477 us
  waiting for transfers between devices  286 us (60%)
  blocking collectives  92.7 us (19%)
  matrix products  43.3 us (9%)
  other arithmetic  28.4 us (6%)
  between operations  15.2 us (3%)
  local copies, waits for them, and re-layouts  8.94 us (2%)
    unnamed x5, waiting for transfers between devices  173 us
    all_gather x1, waiting for transfers between devices, body(): lax.all_gather(w_in.astype(low), ('dp', 'rep'), axis=0, tiled=True)  72.8 us
    all_gather x2, blocking collectives, carry_in(): every = lax.all_gather(summary[24:27], 'dp', axis=0)  46.4 us
    psum x1, blocking collectives, body(): summed_vec, total = lax.psum((grad_vectors, jnp.sum(filled)), ('dp', 'rep'))  46.3 us
    all_gather x1, waiting for transfers between devices, body(): lax.all_gather(w_out.astype(low), ('dp', 'rep'), axis=0, tiled=True)  30.5 us
  transfers between devices with their start and end apart: 4, of which 4 were waited for; matrix products, arithmetic and copies ran while one was open for 10% of the time, Pallas kernels for 1%

profile of v1, /device:TPU:3, one launch (start us, length us, event | category | flops | bytes accessed | tf_op | source)
XLA Modules:
  0.0 477.3 jit_solution(8275433630572928249)
XLA Ops:
  7.3 1.8 convert_element_type.126
  9.1 1.6 convert_element_type.137
  10.8 0.7 compare_reduce_fusion
  11.6 0.2 multiply_reduce_fusion.3
  11.9 0.6 convert_reduce_fusion
  13.5 1.4 convert.43
  15.0 72.8 %all-gather.7.cloned.1.call-done = bf16[768,4992]{1,0:T(8,128)(2,1)} async-done(((bf16[24,4992]{1,0:T(8,128)(2,1)}), bf16[768,4992]{1,0:T(8,128)(2,1)}) %all-gather.7.cloned.1.call-update) | async-done | bytes 7667728 | tf_op jit(solution)/shard_map/all_gather | solution.py:249
  87.8 4.2 fusion.7
  92.0 0.2 convert_subtract_fusion
  92.3 0.4 fusion.40
  92.7 1.2 copy-done.7
  94.0 0.5 shard_map.269.summary
  94.5 23.3 %all-gather.2 = f32[8,3,384]{2,1,0:T(4,128)S(1)} all-gather(f32[1,3,384]{2,1,0:T(4,128)S(1)} %slice_bitcast_fusion.3), channel_id=2, replica_groups=mesh['dp'=8,'rep'=4] {'dp'}, dimensions={0}, use_global_device_ids=true | all-gather | bytes 41472 | tf_op jit(solution)/shard_map/all_gather | solution.py:175
  118.0 0.5 shard_map.270.states
  118.6 1.0 slice_bitcast_fusion.1
  119.6 30.5 %all-gather.9.cloned.1.call-done = bf16[2304,768]{1,0:T(8,128)(2,1)} async-done(((bf16[72,768]{1,0:T(8,128)(2,1)}), bf16[2304,768]{1,0:T(8,128)(2,1)}) %all-gather.9.cloned.1.call-update) | async-done | bytes 3538960 | tf_op jit(solution)/shard_map/all_gather | solution.py:250
  150.1 4.2 multiply_reduce_fusion.2
  154.4 5.4 %fusion.2 = f32[512,3072]{1,0:T(8,128)S(1)} fusion(bf16[768,4992]{1,0:T(8,128)(2,1)} %all-gather.7.cloned.1.call-done, f32[512,768]{1,0:T(8,128)S(1)} %get-tuple-element.131, f32[768]{0:T(1024)S(1)} %get-tuple-element.122, f32[512]{0:T(512)S(1)} %get-tuple-element.129), kind=kOutput, calls=%fused_computation.4 | convolution fusion | flops 2417098752 | bytes 12588032 | tf_op jit(solution)/shard_map/dot_general | solution.py:276
  159.8 3.1 multiply_convert_fusion.1
  163.0 2.8 multiply_reduce_fusion
  165.9 1.1 subtract_add_fusion
  167.0 3.0 fusion.46
  170.0 2.0 fusion.55
  172.1 3.3 pad_maximum_fusion.1
  175.5 3.6 fusion.39
  179.2 0.5 shard_map.271.summary
  179.7 23.1 %all-gather.3 = f32[8,3,384]{2,1,0:T(4,128)S(1)} all-gather(f32[1,3,384]{2,1,0:T(4,128)S(1)} %slice_bitcast_fusion.2), channel_id=3, replica_groups=mesh['dp'=8,'rep'=4] {'dp'}, dimensions={0}, use_global_device_ids=true | all-gather | bytes 41472 | tf_op jit(solution)/shard_map/all_gather | solution.py:175
  203.1 1.1 shard_map.272
  204.4 2.3 convert_multiply_fusion.1
  206.7 0.3 fusion.65
  207.0 0.7 copy-done.11
  207.8 0.6 copy-done.1
  208.3 2.5 fusion.38
  210.8 2.7 fusion.13
  213.6 5.7 %pad_maximum_fusion = f32[768,4992]{1,0:T(8,128)} fusion(f32[768,3072]{1,0:T(8,128)S(1)} %fusion.13, f32[768,1920]{1,0:T(8,128)S(1)} %fusion.38), kind=kLoop, calls=%fused_computation | loop fusion | flops 3833856 | bytes 30670848 | tf_op jit(solution)/shard_map/concatenate | solution.py:328
  220.3 5.6 %fusion.26 = (f32[768]{0:T(1024)S(1)}, f32[512]{0:T(512)S(1)}, f32[512,768]{1,0:T(8,128)}) fusion(f32[8,64,768]{2,1,0:T(8,128)S(1)} %copy-done.1, f32[512]{0:T(512)S(1)} %rsqrt.26, f32[768]{0:T(1024)S(1)} %get-tuple-element.123, bf16[768,4992]{1,0:T(8,128)(2,1)} %all-gather.7.cloned.1.call-done, bf16[512,768]{1,0:T(8,128)(2,1)} %copy-done.19, ...), kind=kOutput, calls=%fused_computation.43 | convolution fusion | flops 1518205696 | bytes 8071168 | tf_op jit(solution)/shard_map/tc,dc->td/dot_general | solution.py:321
  225.9 46.3 %all-reduce.1 = (f32[]{:T(128)}, f32[2304]{0:T(1024)S(1)}) all-reduce(f32[]{:T(128)} %get-tuple-element.71, f32[2304]{0:T(1024)S(1)} %pad_maximum_fusion.11), channel_id=1, replica_groups=mesh['dp'=8,'rep'=4] {'dp','rep'}, use_global_device_ids=true, to_apply=%region_6.7 | all-reduce | flops 2305 | bytes 18440 | tf_op jit(solution)/shard_map/psum | solution.py:334
  272.2 4.1 fusion.32
  276.3 1.0 copy.52
  277.3 0.7 copy-done.4
  278.0 1.0 fusion.23
  279.1 1.6 copy.54
  280.8 1.3 add_multiply_fusion
  282.1 0.6 slice.345
  282.7 9.4 %reduce-scatter.5.cloned.1.call-done = f32[72,768]{1,0:T(8,128)} async-done(((f32[2304,768]{1,0:T(8,128)}), f32[72,768]{1,0:T(8,128)}) %reduce-scatter.5.cloned.1.call-update) | async-done | bytes 221200 | tf_op jit(solution)/shard_map/reduce_scatter | solution.py:332
  292.0 2.5 fusion.61
  294.5 173.2 %reduce-scatter.7.cloned.1.call-done = f32[24,4992]{1,0:T(8,128)} async-done(((f32[768,4992]{1,0:T(8,128)}), f32[24,4992]{1,0:T(8,128)}) %reduce-scatter.7.cloned.1.call-update) | async-done | bytes 479248
  467.7 3.0 fusion.63
  (121 shorter events, 2.6 us)
Async XLA Ops:
  7.2 4.4 copy-start.8
  7.2 4.7 copy-start.31
  7.2 5.6 %copy-start.27 = (f32[2304]{0:T(1024)S(1)}, f32[2304]{0:T(1024)}, u32[]{:S(2)}) copy-start(f32[2304]{0:T(1024)} %param.20) | copy-start | bytes 27652
  7.2 80.6 %all-gather.7.cloned.1.call-start = ((), (), s32[]{:S(2)}) async-start(), calls=%async_computation.2 | async-start | bytes 7907328 | tf_op jit(solution)/shard_map/all_gather | solution.py:249
  9.1 141.0 %all-gather.9.cloned.1.call-start = ((), (), s32[]{:S(2)}) async-start(), calls=%async_computation.3 | async-start | bytes 3649536 | tf_op jit(solution)/shard_map/all_gather | solution.py:250
  10.8 281.3 %reduce-scatter.5.cloned.1.call-start = ((), (), s32[]{:S(2)}) async-start(), calls=%async_computation.4 | async-start | bytes 7299072 | tf_op jit(solution)/shard_map/reduce_scatter | solution.py:332
  11.6 1.9 copy-start.20
  13.5 78.5 %copy-start = (f32[8,64,768]{2,1,0:T(8,128)}, f32[8,64,768]{2,1,0:T(8,128)S(1)}, u32[]{:S(2)}) copy-start(f32[8,64,768]{2,1,0:T(8,128)S(1)} %convert.48) | copy-start | bytes 4718596
  92.0 1.9 copy-start.7
  154.3 11.5 %copy-start.5 = (f32[512,768]{1,0:T(8,128)}, f32[512,768]{1,0:T(8,128)S(1)}, u32[]{:S(2)}) copy-start(f32[512,768]{1,0:T(8,128)S(1)} %get-tuple-element.131) | copy-start | bytes 4718596
  154.4 5.4 %copy-start.2 = (f32[8,64,768]{2,1,0:T(8,128)S(1)}, f32[8,64,768]{2,1,0:T(8,128)}, u32[]{:S(2)}) copy-start(f32[8,64,768]{2,1,0:T(8,128)} %convert.43) | copy-start | bytes 4718596
  154.4 5.4 %copy-start.32 = (bf16[2304,768]{1,0:T(8,128)(2,1)S(1)}, bf16[2304,768]{1,0:T(8,128)(2,1)}, u32[]{:S(2)}) copy-start(bf16[2304,768]{1,0:T(8,128)(2,1)} %all-gather.9.cloned.1.call-done) | copy-start | bytes 10616836
  154.4 8.6 %slice-start = ((s8[7667712]{0:T(1024)(128)(4,1)}), s8[4194304]{0:T(1024)(128)(4,1)S(1)}, s32[]{:S(2)}) async-start(s8[7667712]{0:T(1024)(128)(4,1)} %bitcast.80), calls=%async_computation.6 | async-start | bytes 8388608
  159.8 3.2 slice-start.1
  162.9 2.9 copy-start.14
  163.0 2.9 copy-start.16
  163.0 7.0 %copy-start.9 = (bf16[512,1536]{1,0:T(8,128)(2,1)}, bf16[512,1536]{1,0:T(8,128)(2,1)S(1)}, u32[]{:S(2)}) copy-start(bf16[512,1536]{1,0:T(8,128)(2,1)S(1)} %get-tuple-element.109) | copy-start | bytes 4718596
  165.8 1.1 copy-start.23
  165.9 1.1 copy-start.24
  167.0 3.0 copy-start.3
  175.4 292.3 %reduce-scatter.7.cloned.1.call-start = ((), (), s32[]{:S(2)}) async-start(), calls=%async_computation.5 | async-start | bytes 15814656
  179.1 27.9 %copy-start.19 = (bf16[512,768]{1,0:T(8,128)(2,1)}, bf16[512,768]{1,0:T(8,128)(2,1)S(1)}, u32[]{:S(2)}) copy-start(bf16[512,768]{1,0:T(8,128)(2,1)S(1)} %get-tuple-element.111) | copy-start | bytes 2359300
  206.7 1.6 copy-start.1
  207.0 0.8 copy-start.11
  208.3 2.5 copy-start.6
  208.3 2.5 copy-start.15
  208.3 2.5 copy-start.17
  219.3 1.0 copy-start.12
  272.2 5.2 %copy-start.13 = (f32[512,768]{1,0:T(8,128)S(1)}, f32[512,768]{1,0:T(8,128)}, u32[]{:S(2)}) copy-start(f32[512,768]{1,0:T(8,128)} %get-tuple-element.133) | copy-start | bytes 4718596
  276.3 1.7 copy-start.4
  279.1 1.7 copy-start.29
  279.1 1.7 copy-start.30
  279.1 13.0 %copy-start.18 = (f32[72,768]{1,0:T(8,128)S(1)}, f32[72,768]{1,0:T(8,128)}, u32[]{:S(2)}) copy-start(f32[72,768]{1,0:T(8,128)} %param.19) | copy-start | bytes 663556
  279.1 12.9 %copy-start.25 = (f32[72,768]{1,0:T(8,128)S(1)}, f32[72,768]{1,0:T(8,128)}, u32[]{:S(2)}) copy-start(f32[72,768]{1,0:T(8,128)} %param.24) | copy-start | bytes 663556
  279.1 12.9 %copy-start.26 = (f32[72,768]{1,0:T(8,128)S(1)}, f32[72,768]{1,0:T(8,128)}, u32[]{:S(2)}) copy-start(f32[72,768]{1,0:T(8,128)} %param.23) | copy-start | bytes 663556
  280.7 187.0 %copy-start.10 = (f32[24,4992]{1,0:T(8,128)S(1)}, f32[24,4992]{1,0:T(8,128)}, u32[]{:S(2)}) copy-start(f32[24,4992]{1,0:T(8,128)} %param.18) | copy-start | bytes 1437700
  280.7 187.0 %copy-start.21 = (f32[24,4992]{1,0:T(8,128)S(1)}, f32[24,4992]{1,0:T(8,128)}, u32[]{:S(2)}) copy-start(f32[24,4992]{1,0:T(8,128)} %param.22) | copy-start | bytes 1437700
  280.7 187.0 %copy-start.22 = (f32[24,4992]{1,0:T(8,128)S(1)}, f32[24,4992]{1,0:T(8,128)}, u32[]{:S(2)}) copy-start(f32[24,4992]{1,0:T(8,128)} %param.21) | copy-start | bytes 1437700
  282.1 188.7 %copy-start.28 = (f32[2304]{0:T(1024)}, f32[2304]{0:T(1024)S(1)}, u32[]{:S(2)}) copy-start(f32[2304]{0:T(1024)S(1)} %get-tuple-element.78) | copy-start | bytes 27652
Sparse Core Ops, SparseCore 0:
  11.5 76.2 all-gather.6
  91.3 58.8 all-gather.8
  175.6 116.4 reduce-scatter.4
  299.1 168.5 reduce-scatter.6

commit v2 on v1

--- a/solution.py
+++ b/solution.py
@@ -1,3 +1,5 @@
+import functools
+
 import jax
 import jax.numpy as jnp
 from jax import lax
@@ -216,6 +218,506 @@
     )
     change = -LEARN_RATE * (corrected + decay * master)
     return (master + change, first_new, second_new, change)
+
+
+MESH = pl.DeviceIdType.MESH
+LOW = jnp.bfloat16
+WIDE = jnp.float32
+PLANES = 4
+SIDE = 2
+IN_ROWS = 24
+OUT_ROWS = 72
+MIX = CH + 2 * D
+MIX_HALF = 1024
+TILE = 128
+VMEM_BYTES = 60 * 1024 * 1024
+
+
+class Piece:
+    def __init__(self, matrix, rows, columns, starts, overlap=0):
+        self.matrix, self.rows, self.columns = matrix, rows, columns
+        self.starts, self.overlap = starts, overlap
+
+    def shape(self):
+        return (2, PLANES, SIDE, SIDE, 2 * self.rows, self.columns)
+
+
+def piece_list():
+    half = MIX_HALF // 2
+    second = MIX - MIX_HALF
+    mix = [
+        Piece("in", IN_ROWS, half, (0, second), TILE),
+        Piece("in", IN_ROWS, half, (half, second + half)),
+    ]
+    out = [Piece("out", OUT_ROWS, D // 2, (0, D // 2))]
+    wide = FF // 4
+    glu = [
+        Piece("in", IN_ROWS, wide, (MIX + wide * k, MIX + FF + wide * k)) for k in range(4)
+    ]
+    return mix + out + glu
+
+
+PIECES = piece_list()
+
+
+class Place:
+    def __init__(self):
+        dp, rep = lax.axis_index("dp"), lax.axis_index("rep")
+        self.z, self.x = dp // SIDE, dp % SIDE
+        self.y, self.core = rep // 2, rep % 2
+
+    def at(self, z, x, y, core):
+        return (z * SIDE + x, y * 2 + core)
+
+    def sibling(self):
+        return self.at(self.z, self.x, self.y, 1 - self.core)
+
+    def plane(self, z):
+        return self.at(z, self.x, self.y, self.core)
+
+    def near(self, core):
+        if core == 0:
+            return self.at(self.z, 1 - self.x, self.y, self.core)
+        return self.at(self.z, self.x, 1 - self.y, self.core)
+
+    def far(self, core):
+        return self.near(1 - core)
+
+    def turn(self, step):
+        return lax.rem(self.z + step, PLANES)
+
+    def sides(self, core):
+        return (self.x, self.y) if core == 0 else (self.y, self.x)
+
+    def by_core(self, run):
+        for core in range(2):
+            pl.when(self.core == core)(functools.partial(run, core))
+
+    def greet(self):
+        barrier = pltpu.get_barrier_semaphore()
+        partners = [self.sibling(), self.near(0), self.near(1)]
+        partners += [self.plane(self.turn(step)) for step in (1, 2, 3)]
+        for partner in partners:
+            pl.semaphore_signal(barrier, inc=1, device_id=partner, device_id_type=MESH)
+        return lambda: pl.semaphore_wait(barrier, len(partners))
+
+
+def block_of(ref, core, z, near, far):
+    return ref.at[core, z, near, far] if core == 0 else ref.at[core, z, far, near]
+
+
+def pair_of(ref, core, z, far):
+    return ref.at[core, z, :, far] if core == 0 else ref.at[core, z, far]
+
+
+def remote(source, target, sent, received, device):
+    return pltpu.make_async_remote_copy(
+        src_ref=source,
+        dst_ref=target,
+        send_sem=sent,
+        recv_sem=received,
+        device_id=device,
+        device_id_type=MESH,
+    )
+
+
+GATHER_SEMS = 4 * 2
+STEPS_AWAY = (1, 3, 2)
+
+
+class Gather:
+    def __init__(self, place, masters, buffers, staging, sems):
+        self.place, self.masters, self.buffers, self.staging = place, masters, buffers, staging
+        self.local, self.sent0, self.got0 = sems[:3]
+        self.sems = sems[3:]
+
+    @staticmethod
+    def scratch():
+        n = len(PIECES)
+        dma = pltpu.SemaphoreType.DMA
+        return (
+            [pltpu.VMEM(p.shape(), LOW) for p in PIECES]
+            + [pltpu.VMEM((2 * p.rows, p.columns), WIDE) for p in PIECES]
+            + [dma((n,))] * 3
+            + [dma((n, PLANES))] * GATHER_SEMS
+        )
+
+    def part(self, p, half):
+        piece = PIECES[p]
+        start = piece.starts[0] + half * (piece.starts[1] - piece.starts[0])
+        return self.masters[piece.matrix].at[:, pl.ds(pl.multiple_of(start, TILE), piece.columns)]
+
+    def own_rows(self, p):
+        rows = PIECES[p].rows
+        return self.staging[p].at[pl.ds(pl.multiple_of(self.place.core * rows, 8), rows)]
+
+    def to_sibling(self, p):
+        return remote(
+            self.part(p, 1 - self.place.core),
+            self.own_rows(p),
+            self.sent0.at[p],
+            self.got0.at[p],
+            self.place.sibling(),
+        )
+
+    def to_self(self, p):
+        return pltpu.make_async_copy(
+            self.part(p, self.place.core), self.own_rows(p), self.local.at[p]
+        )
+
+    def along_z(self, p, z, target):
+        place = self.place
+        block = self.buffers[p].at[place.core, z, place.x, place.y]
+        return remote(
+            block, block, self.sems[0].at[p, target], self.sems[1].at[p, z], place.plane(target)
+        )
+
+    def along_near(self, p, z, core):
+        block = block_of(self.buffers[p], core, z, *self.place.sides(core))
+        return remote(
+            block, block, self.sems[2].at[p, z], self.sems[3].at[p, z], self.place.near(core)
+        )
+
+    def along_far(self, p, z, core):
+        pair = pair_of(self.buffers[p], core, z, self.place.sides(core)[1])
+        return remote(
+            pair, pair, self.sems[4].at[p, z], self.sems[5].at[p, z], self.place.far(core)
+        )
+
+    def in_chip(self, p, z, core):
+        plane = self.buffers[p].at[core, z]
+        return remote(
+            plane, plane, self.sems[6].at[p, z], self.sems[7].at[p, z], self.place.sibling()
+        )
+
+    def begin(self):
+        for p in range(len(PIECES)):
+            self.to_sibling(p).start()
+            self.to_self(p).start()
+
+    def stage0(self, p):
+        place = self.place
+        self.to_self(p).wait()
+        self.to_sibling(p).wait_recv()
+        self.buffers[p][place.core, place.z, place.x, place.y] = self.staging[p][...].astype(LOW)
+        for step in STEPS_AWAY:
+            self.along_z(p, place.z, place.turn(step)).start()
+        place.by_core(lambda core: self.along_near(p, place.z, core).start())
+
+    def stage1(self, p):
+        place = self.place
+        for step in STEPS_AWAY:
+            z = place.turn(step)
+            self.along_z(p, z, place.z).wait_recv()
+            place.by_core(lambda core: self.along_near(p, z, core).start())
+
+    def stage2(self, p):
+        def run(core):
+            for step in (0,) + STEPS_AWAY:
+                z = self.place.turn(step)
+                self.along_near(p, z, core).wait_recv()
+                self.along_far(p, z, core).start()
+
+        self.place.by_core(run)
+
+    def stage3(self, p):
+        def run(core):
+            for step in (0,) + STEPS_AWAY:
+                z = self.place.turn(step)
+                self.along_far(p, z, core).wait_recv()
+                self.in_chip(p, z, core).start()
+
+        self.place.by_core(run)
+
+    def stage4(self, p):
+        for step in (0,) + STEPS_AWAY:
+            z = self.place.turn(step)
+            self.in_chip(p, z, 1 - self.place.core).wait_recv()
+
+    def drain(self, p):
+        self.to_sibling(p).wait_send()
+        for step in STEPS_AWAY:
+            self.along_z(p, self.place.z, self.place.turn(step)).wait_send()
+
+        def run(core):
+            for z in range(PLANES):
+                self.along_near(p, z, core).wait_send()
+                self.along_far(p, z, core).wait_send()
+                self.in_chip(p, z, core).wait_send()
+
+        self.place.by_core(run)
+
+
+class Reduce:
+    ORDER = STEPS_AWAY + (0,)
+
+    def __init__(self, place, grads, refs, results):
+        n = len(PIECES)
+        self.place, self.grads, self.results = place, grads, results
+        self.chip, self.far, self.near, self.planes, self.final = (
+            refs[k * n : (k + 1) * n] for k in range(5)
+        )
+        self.sems = refs[5 * n :]
+
+    @staticmethod
+    def scratch():
+        n = len(PIECES)
+        dma = pltpu.SemaphoreType.DMA
+        shapes = [p.shape() for p in PIECES]
+        return (
+            [pltpu.VMEM(s[1:], LOW) for s in shapes]
+            + [pltpu.VMEM((PLANES, SIDE) + s[4:], LOW) for s in shapes]
+            + [pltpu.VMEM((PLANES,) + s[4:], LOW) for s in shapes] * 2
+            + [pltpu.VMEM(s[4:], WIDE) for s in shapes]
+            + [dma((n, PLANES))] * 8
+            + [dma((n,))] * 2
+        )
+
+    def in_chip(self, p, z, core):
+        return remote(
+            self.grads[p].at[1 - core, z],
+            self.chip[p].at[z],
+            self.sems[0].at[p, z],
+            self.sems[1].at[p, z],
+            self.place.sibling(),
+        )
+
+    def along_far(self, p, z, core):
+        return remote(
+            pair_of(self.grads[p], core, z, 1 - self.place.sides(core)[1]),
+            self.far[p].at[z],
+            self.sems[2].at[p, z],
+            self.sems[3].at[p, z],
+            self.place.far(core),
+        )
+
+    def along_near(self, p, z, core):
+        near, far = self.place.sides(core)
+        return remote(
+            block_of(self.grads[p], core, z, 1 - near, far),
+            self.near[p].at[z],
+            self.sems[4].at[p, z],
+            self.sems[5].at[p, z],
+            self.place.near(core),
+        )
+
+    def along_z(self, p, z, sender, core):
+        return remote(
+            block_of(self.grads[p], core, z, *self.place.sides(core)),
+            self.planes[p].at[sender],
+            self.sems[6].at[p, z],
+            self.sems[7].at[p, sender],
+            self.place.plane(z),
+        )
+
+    def result(self, p, core):
+        piece = PIECES[p]
+        skip = piece.overlap * core
+        start, width = piece.starts[core] + skip, piece.columns - skip
+        return self.results[piece.matrix].at[:, pl.ds(start, width)], pl.ds(skip, width)
+
+    def to_sibling(self, p, core):
+        rows = PIECES[p].rows
+        target, columns = self.result(p, core)
+        return remote(
+            self.final[p].at[pl.ds(rows * (1 - core), rows), columns],
+            target,
+            self.sems[8].at[p],
+            self.sems[9].at[p],
+            self.place.sibling(),
+        )
+
+    @staticmethod
+    def add(target, source):
+        target[...] = (target[...].astype(WIDE) + source[...].astype(WIDE)).astype(LOW)
+
+    def stage0(self, p):
+        def run(core):
+            for step in self.ORDER:
+                self.in_chip(p, self.place.turn(step), core).start()
+
+        self.place.by_core(run)
+
+    def stage1(self, p):
+        def run(core):
+            for step in self.ORDER:
+                z = self.place.turn(step)
+                self.in_chip(p, z, core).wait_recv()
+                self.add(self.grads[p].at[core, z], self.chip[p].at[z])
+                self.along_far(p, z, core).start()
+
+        self.place.by_core(run)
+
+    def stage2(self, p):
+        def run(core):
+            for step in self.ORDER:
+                z = self.place.turn(step)
+                self.along_far(p, z, core).wait_recv()
+                own = pair_of(self.grads[p], core, z, self.place.sides(core)[1])
+                self.add(own, self.far[p].at[z])
+                self.along_near(p, z, core).start()
+
+        self.place.by_core(run)
+
+    def stage3(self, p):
+        def run(core):
+            for step in self.ORDER:
+                z = self.place.turn(step)
+                self.along_near(p, z, core).wait_recv()
+                own = block_of(self.grads[p], core, z, *self.place.sides(core))
+                self.add(own, self.near[p].at[z])
+                if step:
+                    self.along_z(p, z, self.place.z, core).start()
+
+        self.place.by_core(run)
+
+    def stage4(self, p):
+        rows = PIECES[p].rows
+
+        def run(core):
+            z = self.place.z
+            for step in STEPS_AWAY:
+                self.along_z(p, z, self.place.turn(step), core).wait_recv()
+            total = block_of(self.grads[p], core, z, *self.place.sides(core))[...].astype(WIDE)
+            for step in STEPS_AWAY:
+                total = total + self.planes[p][self.place.turn(step)].astype(WIDE)
+            self.final[p][...] = total
+            self.to_sibling(p, core).start()
+            target, columns = self.result(p, core)
+            target[...] = self.final[p][pl.ds(rows * core, rows), columns]
+
+        self.place.by_core(run)
+
+    def drain(self, p):
+        def run(core):
+            self.to_sibling(p, 1 - core).wait_recv()
+            self.to_sibling(p, core).wait_send()
+            for step in self.ORDER:
+                z = self.place.turn(step)
+                self.in_chip(p, z, core).wait_send()
+                self.along_far(p, z, core).wait_send()
+                self.along_near(p, z, core).wait_send()
+                if step:
+                    self.along_z(p, z, self.place.z, core).wait_send()
+
+        self.place.by_core(run)
+
+
+def stagger(stages, count):
+    for tick in range(count + len(stages) - 1):
+        for lag, stage in enumerate(stages):
+            if 0 <= tick - lag < count:
+                stage(tick - lag)
+
+
+def gather_kernel(w_in, w_out, *refs):
+    n = len(PIECES)
+    results, (buffers, staging, rest) = refs[:n], (refs[n : 2 * n], refs[2 * n : 3 * n], refs[3 * n :])
+    done, sems = rest[-1], rest[:-1]
+    place = Place()
+    gather = Gather(place, {"in": w_in, "out": w_out}, buffers, staging, sems)
+    place.greet()()
+    gather.begin()
+    stagger([gather.stage0, gather.stage1, gather.stage2, gather.stage3, gather.stage4], n)
+    copies = [pltpu.make_async_copy(buffers[p], results[p], done.at[p]) for p in range(n)]
+    for copy in copies:
+        copy.start()
+    for p in range(n):
+        gather.drain(p)
+    for copy in copies:
+        copy.wait()
+
+
+def gather_call(w_in, w_out):
+    n = len(PIECES)
+    anywhere = pl.BlockSpec(memory_space=pl.ANY)
+    return pl.pallas_call(
+        gather_kernel,
+        out_shape=[jax.ShapeDtypeStruct(p.shape(), LOW) for p in PIECES],
+        in_specs=[anywhere] * 2,
+        out_specs=[anywhere] * n,
+        scratch_shapes=Gather.scratch() + [pltpu.SemaphoreType.DMA((n,))],
+        compiler_params=pltpu.CompilerParams(
+            collective_id=0, has_side_effects=True, vmem_limit_bytes=VMEM_BYTES
+        ),
+    )(w_in, w_out)
+
+
+def reduce_kernel(*refs):
+    n = len(PIECES)
+    sources, results, grads = refs[:n], refs[n : n + 2], refs[n + 2 : 2 * n + 2]
+    loaded, rest = refs[2 * n + 2], refs[2 * n + 3 :]
+    place = Place()
+    reduce = Reduce(place, grads, rest, {"in": results[0], "out": results[1]})
+    entered = place.greet()
+    copies = [pltpu.make_async_copy(sources[p], grads[p], loaded.at[p]) for p in range(n)]
+    for copy in copies:
+        copy.start()
+    entered()
+    for copy in copies:
+        copy.wait()
+    stagger([reduce.stage0, reduce.stage1, reduce.stage2, reduce.stage3, reduce.stage4], n)
+    for p in range(n):
+        reduce.drain(p)
+
+
+def reduce_call(pieces):
+    n = len(PIECES)
+    return pl.pallas_call(
+        reduce_kernel,
+        out_shape=[
+            jax.ShapeDtypeStruct((IN_ROWS, MIX + 2 * FF), WIDE),
+            jax.ShapeDtypeStruct((OUT_ROWS, D), WIDE),
+        ],
+        in_specs=[pl.BlockSpec(memory_space=pl.ANY)] * n,
+        out_specs=[pl.BlockSpec(memory_space=pltpu.VMEM)] * 2,
+        scratch_shapes=[pltpu.VMEM(p.shape(), LOW) for p in PIECES]
+        + [pltpu.SemaphoreType.DMA((n,))]
+        + Reduce.scratch(),
+        compiler_params=pltpu.CompilerParams(
+            collective_id=1, has_side_effects=True, vmem_limit_bytes=VMEM_BYTES
+        ),
+    )(*pieces)
+
+
+def routed(w_in, w_out):
+    sizes = (lax.axis_size("dp"), lax.axis_size("rep"))
+    return sizes == (PLANES * SIDE, SIDE * 2) and (w_in.shape[0], w_out.shape[0]) == (
+        IN_ROWS,
+        OUT_ROWS,
+    )
+
+
+def gather_weights(w_in, w_out):
+    if not routed(w_in, w_out):
+        axes = ("dp", "rep")
+        return (
+            lax.all_gather(w_in.astype(LOW), axes, axis=0, tiled=True),
+            lax.all_gather(w_out.astype(LOW), axes, axis=0, tiled=True),
+        )
+    got = gather_call(w_in, w_out)
+    parts = [[g[half].reshape(-1, g.shape[-1]) for g in got] for half in range(2)]
+    mix = parts[0][:2] + [parts[1][0][:, TILE:], parts[1][1]]
+    full_in = jnp.concatenate(mix + parts[0][3:] + parts[1][3:], axis=1)
+    return full_in, jnp.concatenate([parts[0][2], parts[1][2]], axis=1)
+
+
+def reduce_grads(grad_in, grad_out, shard_in, shard_out):
+    if not routed(shard_in, shard_out):
+        axes = ("dp", "rep")
+        return (
+            lax.psum_scatter(grad_in, axes, scatter_dimension=0, tiled=True),
+            lax.psum_scatter(grad_out, axes, scatter_dimension=0, tiled=True),
+        )
+    whole = {"in": grad_in.astype(LOW), "out": grad_out.astype(LOW)}
+    pieces = []
+    for piece in PIECES:
+        halves = [
+            whole[piece.matrix][:, start : start + piece.columns].reshape(piece.shape()[1:])
+            for start in piece.starts
+        ]
+        pieces.append(jnp.stack(halves))
+    return reduce_call(pieces)
 
 
 def body(
@@ -246,8 +748,7 @@
     phases = vectors[2 * D : 2 * D + CH]
     biases = vectors[2 * D + CH :]
     turn = jnp.stack([jnp.cos(phases), jnp.sin(phases)])
-    full_in = lax.all_gather(w_in.astype(low), ("dp", "rep"), axis=0, tiled=True)
-    full_out = lax.all_gather(w_out.astype(low), ("dp", "rep"), axis=0, tiled=True)
+    full_in, full_out = gather_weights(w_in, w_out)
     normed, scaling_one = normalize(inputs, gains_one)
     normed_low = normed.astype(low)
     pre_mix = jnp.dot(normed_low, full_in[:, :mixer_cols], preferred_element_type=wide)
@@ -327,10 +828,7 @@
     grad_vectors = jnp.concatenate([grad_gains_one, grad_gains_two, d_phase[0], grad_biases])
     grad_in_all = jnp.concatenate([grad_mixer_in, grad_glu], axis=1)
     grad_out_all = jnp.concatenate([grad_mixer_out, grad_down], axis=0)
-    summed_in, summed_out = (
-        lax.psum_scatter(grad_in_all, ("dp", "rep"), scatter_dimension=0, tiled=True),
-        lax.psum_scatter(grad_out_all, ("dp", "rep"), scatter_dimension=0, tiled=True),
-    )
+    summed_in, summed_out = reduce_grads(grad_in_all, grad_out_all, w_in, w_out)
     summed_vec, total = lax.psum((grad_vectors, jnp.sum(filled)), ("dp", "rep"))
     steps = counter[0].astype(jnp.float32)
     grad_in = summed_in / total

time: 480 us -> 348 us (0.72)
  waiting for transfers between devices: 286 us -> 0 us
  Pallas kernels: 2.56 us -> 146 us
  local copies, waits for them, and re-layouts: 8.94 us -> 26.9 us
  between operations: 15.2 us -> 2.51 us
  blocking collectives: 92.7 us -> 98.8 us
    unnamed x5 -> x0, waiting for transfers between devices: 173 us -> none
    pallas_call x0 -> x2, Pallas kernels: none -> 143 us  [the longest x1 73.4 us: reduce_call(): pl.pallas_call(reduce_kernel, out_shape=[jax.ShapeDtypeStruct((IN_ROWS, M...]
    all_gather x2 -> x0, waiting for transfers between devices: 103 us -> none  [the longest x1 72.8 us: body(): lax.all_gather(w_in.astype(low), ('dp', 'rep'), axis=0, tiled=True)]
    unnamed x72 -> x127, local copies, waits for them, and re-layouts: 3.5 us -> 14.9 us
    another operation x3 -> x10, other arithmetic: 0.18 us -> 9.6 us  [the longest x7 9.42 us: reduce_grads(): pieces.append(jnp.stack(halves))]
    reduce_scatter x1 -> x0, waiting for transfers between devices: 9.38 us -> none  [body(): lax.psum_scatter(grad_out_all, ('dp', 'rep'), scatter_dimension=0, tiled=...]
    slice x0 -> x7, local copies, waits for them, and re-layouts: none -> 7.27 us  [the longest x4 5.62 us: gather_weights(): g[half].reshape(-1, g.shape[-1])]
    concatenate x1 -> x0, other arithmetic: 5.68 us -> none  [body(): grad_in_all = jnp.concatenate([grad_mixer_in, grad_glu], axis=1)]
  transfers between devices with their start and end apart: 4 -> 0, of which waited for: 4 -> 0; matrix products, arithmetic and copies ran while one was open for 10% -> 0% of each run, Pallas kernels for 1% -> 0%
where the time goes in v2:
time: 348 us; the launch traced here: 342 us
  Pallas kernels  146 us (42%)
  blocking collectives  98.8 us (28%)
  matrix products  41.2 us (12%)
  local copies, waits for them, and re-layouts  26.9 us (8%)
  other arithmetic  26.9 us (8%)
    pallas_call x1, Pallas kernels, reduce_call(): pl.pallas_call(reduce_kernel, out_shape=[jax.ShapeDtypeStruct((IN_ROWS, M...  73.4 us
    pallas_call x1, Pallas kernels, gather_call(): pl.pallas_call(gather_kernel, out_shape=[jax.ShapeDtypeStruct(p.shape(),...  70 us
    psum x1, blocking collectives, body(): summed_vec, total = lax.psum((grad_vectors, jnp.sum(filled)), ('dp', 'rep'))  50.7 us
    all_gather x2, blocking collectives, carry_in(): every = lax.all_gather(summary[24:27], 'dp', axis=0)  48.1 us
    unnamed x127, local copies, waits for them, and re-layouts  14.9 us
    another operation x7, other arithmetic, reduce_grads(): pieces.append(jnp.stack(halves))  9.42 us

profile of v2, /device:TPU:3, one launch (start us, length us, event | category | flops | bytes accessed | tf_op | source)
XLA Modules:
  0.0 341.9 jit_solution(3448910341750528282)
XLA Ops:
  0.7 70.0 %shard_map.269 = (bf16[2,4,2,2,48,512]{5,4,3,2,1,0:T(8,128)(2,1)}, bf16[2,4,2,2,48,512]{5,4,3,2,1,0:T(8,128)(2,1)}, bf16[2,4,2,2,144,384]{5,4,3,2,1,0:T(8,128)(2...) custom-call(f32[24,4992]{1,0:T(8,128)} %w_in.1, ...), custom_call_target="tpu_custom_call" | custom-call | tf_op jit(solution)/shard_map/pallas_call | solution.py:634
  70.6 3.0 fusion.60
  73.6 0.9 slice.408
  74.5 0.8 copy-done.16
  76.0 5.6 %fusion.28 = f32[512,1920]{1,0:T(8,128)} fusion(bf16[768,512]{1,0:T(8,128)(2,1)S(1)} %bitcast.138, bf16[768,384]{1,0:T(8,128)(2,1)} %slice.408, bf16[768,512]{1,0:T(8,128)(2,1)} %bitcast.140, bf16[768,512]{1,0:T(8,128)(2,1)S(1)} %bitcast.136, f32[8,64,768]{2,1,0:T(8,128)S(1)} %convert.68, f32[768]{0:T(1024)S(1)} %get-tuple-element.169, f32[512]{0:T(512)S(1)} %rsqrt.26), kind=kOutput, calls=%fused_computation.81 | convolution fusion | flops 1522925568 | bytes 8459264 | tf_op jit(solution)/shard_map/dot_general | solution.py:754
  82.1 1.4 convert_subtract_fusion
  83.5 2.1 fusion.23
  86.2 23.9 %all-gather.2 = f32[8,3,384]{2,1,0:T(4,128)S(1)} all-gather(f32[1,3,384]{2,1,0:T(4,128)S(1)} %slice_bitcast_fusion.3), channel_id=2, replica_groups=mesh['dp'=8,'rep'=4] {'dp'}, dimensions={0}, use_global_device_ids=true | all-gather | bytes 41472 | tf_op jit(solution)/shard_map/all_gather | solution.py:177
  110.4 1.1 copy-done.1
  112.2 2.1 copy-done.15
  114.3 2.1 fusion.56
  117.3 4.2 %multiply_reduce_fusion.2 = (f32[512]{0:T(512)S(1)}, f32[512,768]{1,0:T(8,128)S(1)}) fusion(bf16[2304,384]{1,0:T(8,128)(2,1)} %bitcast.131, bf16[2304,384]{1,0:T(8,128)(2,1)} %bitcast.127, f32[512]{0:T(512)S(1)} %convert_element_type.130, bf16[512,384]{1,0:T(8,128)(2,1)S(1)} %get-tuple-element.165, bf16[512,384]{1,0:T(8,128)(2,1)S(1)} %get-tuple-element.164, ...), kind=kOutput, calls=%fused_computation.49 | convolution fusion | flops 611843584 | bytes 9048064 | tf_op jit(solution)/shard_map/dot_general | solution.py:774
  122.0 1.3 copy-done.23
  124.8 2.7 fusion.44
  127.7 1.3 copy-done.18
  129.0 5.1 %multiply_convert_fusion.1 = (bf16[512,1536]{1,0:T(8,128)(2,1)S(1)}, bf16[512,1536]{1,0:T(8,128)(2,1)S(1)}, bf16[512,1536]{1,0:T(8,128)(2,1)}) fusion(f32[512,3072]{1,0:T(8,128)S(1)} %fusion.44, bf16[2304,384]{1,0:T(8,128)(2,1)S(1)} %bitcast.132, bf16[2304,384]{1,0:T(8,128)(2,1)S(1)} %bitcast.128, f32[8,64,768]{2,1,0:T(8,128)S(1)} %convert.59, ...), kind=kOutput, calls=%fused_computation.8 | convolution fusion | flops 1225261056 | bytes 16123904 | tf_op jit(solution)/shard_map/te,fe->tf/dot_general | solution.py:785
  134.1 2.8 multiply_reduce_fusion
  137.0 1.1 subtract_add_fusion
  138.2 4.1 %fusion.22 = (f32[512,768]{1,0:T(8,128)S(1)}, bf16[512,768]{1,0:T(8,128)(2,1)}) fusion(f32[512]{0:T(512)S(1)} %convert_element_type.130, f32[512,1920]{1,0:T(8,128)} %fusion.28, bf16[512,384]{1,0:T(8,128)(2,1)S(1)} %get-tuple-element.165, bf16[512,384]{1,0:T(8,128)(2,1)S(1)} %get-tuple-element.164, bf16[2304,384]{1,0:T(8,128)(2,1)S(1)} %bitcast.133, ...), kind=kOutput, calls=%fused_computation.67 | convolution fusion | flops 614596608 | bytes 9832448 | tf_op jit(solution)/shard_map/te,de->td/dot_general | solution.py:797
  142.9 0.9 copy-done.2
  143.8 24.2 %all-gather.3 = f32[8,3,384]{2,1,0:T(4,128)S(1)} all-gather(f32[1,3,384]{2,1,0:T(4,128)S(1)} %slice_bitcast_fusion.2), channel_id=3, replica_groups=mesh['dp'=8,'rep'=4] {'dp'}, dimensions={0}, use_global_device_ids=true | all-gather | bytes 41472 | tf_op jit(solution)/shard_map/all_gather | solution.py:177
  168.3 1.1 copy-done.3
  169.4 0.9 shard_map.273
  170.4 1.0 copy-done.5
  171.4 2.4 convert_multiply_fusion.1
  174.7 0.9 copy-done.7
  176.1 3.5 %fusion.15 = (f32[768]{0:T(1024)S(1)}, f32[512]{0:T(512)S(1)}, f32[512,768]{1,0:T(8,128)}) fusion(f32[8,64,768]{2,1,0:T(8,128)S(1)} %copy-done.7, f32[512]{0:T(512)S(1)} %rsqrt.26, f32[768]{0:T(1024)S(1)} %get-tuple-element.169, bf16[768,512]{1,0:T(8,128)(2,1)S(1)} %bitcast.139, bf16[768,384]{1,0:T(8,128)(2,1)S(1)} %copy-done.36, ...), kind=kOutput, calls=%fused_computation.41 | convolution fusion | flops 1530002176 | bytes 8071168 | tf_op jit(solution)/shard_map/tc,dc->td/dot_general | solution.py:822
  179.7 50.7 %all-reduce = (f32[]{:T(128)}, f32[2304]{0:T(1024)S(1)}) all-reduce(f32[]{:T(128)} %get-tuple-element.89, f32[2304]{0:T(1024)S(1)} %pad_maximum_fusion.24), channel_id=1, replica_groups=mesh['dp'=8,'rep'=4] {'dp','rep'}, use_global_device_ids=true, to_apply=%region_5.6 | all-reduce | flops 2305 | bytes 18440 | tf_op jit(solution)/shard_map/psum | solution.py:832
  231.2 1.2 add_multiply_fusion
  233.0 4.6 %convolution_convert_fusion = bf16[768,3072]{1,0:T(8,128)(2,1)S(1)} fusion(bf16[512,1536]{1,0:T(8,128)(2,1)} %copy-done.58, bf16[512,1536]{1,0:T(8,128)(2,1)} %copy-done.57, f32[512,768]{1,0:T(8,128)S(1)} %copy-done.13, f32[768]{0:T(1024)S(1)} %get-tuple-element.168, f32[512]{0:T(512)S(1)} %get-tuple-element.175), kind=kOutput, calls=%fused_computation | convolution fusion | flops 2425749504 | bytes 9442304 | tf_op jit(solution)/shard_map/td,tc->dc/dot_general | solution.py:789
  238.1 1.2 pad_maximum_fusion.15.refs_6_
  239.3 1.2 pad_maximum_fusion.14.refs_5_
  240.4 1.2 pad_maximum_fusion.13.refs_4_
  241.6 1.1 pad_maximum_fusion.12.refs_3_
  243.6 2.6 convolution_convert_fusion.3
  246.3 2.1 convolution_convert_fusion.2
  248.7 2.2 pad_maximum_fusion.refs_2_
  250.9 2.5 convolution_convert_fusion.1
  253.6 1.3 pad_maximum_fusion.10.refs_1_
  255.0 1.3 pad_maximum_fusion.9.refs_0_
  256.3 73.4 %shard_map.274 = (f32[24,4992]{1,0:T(8,128)}, f32[72,768]{1,0:T(8,128)}) custom-call(bf16[2,4,2,2,48,512]{5,4,3,2,1,0:T(8,128)(2,1)} %pad_maximum_fusion.9.refs_0_, bf16[2,4,2,2,48,512]{5,4,3,2,1,0:T(8,128)(2,1)} %pad_maximum_fusion.10.refs_1_, bf16[2,4,2,2,144,384]{5,4,3,2,1,0:T(8,128)(2,1)} %pad_maximum_fusion.refs_2_, ...), custom_call_target="tpu_custom_call" | custom-call | tf_op jit(solution)/shard_map/pallas_call | solution.py:666
  329.7 2.6 fusion.48
  332.3 3.2 fusion.50
  335.5 1.1 fusion.12
  336.7 1.6 copy.54
  338.3 1.0 copy-done.54
  339.3 1.4 fusion.19
  340.7 1.0 copy.52
  (177 shorter events, 10.5 us)
Async XLA Ops:
  73.6 2.4 copy-start.28
  73.6 2.4 copy-start.30
  75.4 6.2 %copy-start.6 = (f32[8,64,768]{2,1,0:T(8,128)}, f32[8,64,768]{2,1,0:T(8,128)S(1)}, u32[]{:S(2)}) copy-start(f32[8,64,768]{2,1,0:T(8,128)S(1)} %convert.68) | copy-start | bytes 4718596
  76.0 5.7 %copy-start.51 = (s32[1,512]{1,0:T(1,128)S(1)}, s32[1,512]{1,0:T(1,128)}, u32[]{:S(2)}) copy-start(s32[1,512]{1,0:T(1,128)} %param.17) | copy-start | bytes 6148
  83.4 2.1 copy-start.4
  85.7 24.6 %copy-start = (f32[512,384]{1,0:T(8,128)}, f32[512,384]{1,0:T(8,128)S(1)}, u32[]{:S(2)}) copy-start(f32[512,384]{1,0:T(8,128)S(1)} %get-tuple-element.151.drive_re) | copy-start | bytes 2359300
  112.0 2.3 copy-start.15
  112.2 26.0 %copy-start.41 = (bf16[512,384]{1,0:T(8,128)(2,1)}, bf16[512,384]{1,0:T(8,128)(2,1)S(1)}, u32[]{:S(2)}) copy-start(bf16[512,384]{1,0:T(8,128)(2,1)S(1)} %get-tuple-element.164) | copy-start | bytes 1179652
  112.2 26.0 %copy-start.43 = (bf16[512,384]{1,0:T(8,128)(2,1)}, bf16[512,384]{1,0:T(8,128)(2,1)S(1)}, u32[]{:S(2)}) copy-start(bf16[512,384]{1,0:T(8,128)(2,1)S(1)} %get-tuple-element.165) | copy-start | bytes 1179652
  114.3 2.2 copy-start.52
  117.3 4.2 %copy-start.25 = (bf16[2,4,2,2,48,384]{5,4,3,2,1,0:T(8,128)(2,1)S(1)}, bf16[2,4,2,2,48,384]{5,4,3,2,1,0:T(8,128)(2,1)}, u32[]{:S(2)}) copy-start(bf16[2,4,2,2,48,384]{5,4,3,2,1,0:T(8,128)(2,1)} %get-tuple-element.33) | copy-start | bytes 3538948
  117.3 4.2 %copy-start.26 = (bf16[2,4,2,2,48,384]{5,4,3,2,1,0:T(8,128)(2,1)S(1)}, bf16[2,4,2,2,48,384]{5,4,3,2,1,0:T(8,128)(2,1)}, u32[]{:S(2)}) copy-start(bf16[2,4,2,2,48,384]{5,4,3,2,1,0:T(8,128)(2,1)} %get-tuple-element.34) | copy-start | bytes 3538948
  121.5 15.5 %copy-start.12 = (f32[512,768]{1,0:T(8,128)}, f32[512,768]{1,0:T(8,128)S(1)}, u32[]{:S(2)}) copy-start(f32[512,768]{1,0:T(8,128)S(1)} %get-tuple-element.177) | copy-start | bytes 4718596
  121.8 1.9 copy-start.24
  124.8 2.7 copy-start.33
  124.8 2.9 copy-start.20
  129.0 8.0 %copy-start.8 = (f32[8,64,768]{2,1,0:T(8,128)}, f32[8,64,768]{2,1,0:T(8,128)S(1)}, u32[]{:S(2)}) copy-start(f32[8,64,768]{2,1,0:T(8,128)S(1)} %convert.59) | copy-start | bytes 4718596
  134.1 2.8 copy-start.57
  134.1 2.8 copy-start.58
  138.2 4.1 %copy-start.10 = (f32[512,768]{1,0:T(8,128)}, f32[512,768]{1,0:T(8,128)S(1)}, u32[]{:S(2)}) copy-start(f32[512,768]{1,0:T(8,128)S(1)} %subtract_add_fusion) | copy-start | bytes 4718596
  171.4 3.3 copy-start.32
  171.4 3.3 copy-start.36
  171.4 3.3 copy-start.55
  173.9 1.8 copy-start.7
  173.9 2.0 copy-start.29
  173.9 2.2 copy-start.31
  174.2 5.5 %copy-start.39 = (bf16[512,384]{1,0:T(8,128)(2,1)}, bf16[512,384]{1,0:T(8,128)(2,1)S(1)}, u32[]{:S(2)}) copy-start(bf16[512,384]{1,0:T(8,128)(2,1)S(1)} %get-tuple-element.108) | copy-start | bytes 1179652
  176.1 55.0 %copy-start.49 = (f32[2304]{0:T(1024)S(1)}, f32[2304]{0:T(1024)}, u32[]{:S(2)}) copy-start(f32[2304]{0:T(1024)} %param.26) | copy-start | bytes 27652
  176.1 55.0 %copy-start.50 = (f32[2304]{0:T(1024)S(1)}, f32[2304]{0:T(1024)}, u32[]{:S(2)}) copy-start(f32[2304]{0:T(1024)} %param.25) | copy-start | bytes 27652
  176.1 56.8 %copy-start.13 = (f32[512,768]{1,0:T(8,128)S(1)}, f32[512,768]{1,0:T(8,128)}, u32[]{:S(2)}) copy-start(f32[512,768]{1,0:T(8,128)} %copy-done.12) | copy-start | bytes 4718596
  232.4 5.2 %copy-start.48 = (f32[2304]{0:T(1024)}, f32[2304]{0:T(1024)S(1)}, u32[]{:S(2)}) copy-start(f32[2304]{0:T(1024)S(1)} %get-tuple-element.96) | copy-start | bytes 27652
  241.6 1.9 copy-start.42
  241.6 2.0 copy-start.44
  243.6 2.6 copy-start.9
  243.6 2.6 copy-start.53
  248.7 2.2 copy-start.35
  248.7 2.2 copy-start.40
  248.7 2.2 copy-start.56
  256.3 73.4 %copy-start.27 = (f32[72,768]{1,0:T(8,128)S(1)}, f32[72,768]{1,0:T(8,128)}, u32[]{:S(2)}) copy-start(f32[72,768]{1,0:T(8,128)} %w_out.1) | copy-start | bytes 663556
  256.3 73.4 %copy-start.45 = (f32[72,768]{1,0:T(8,128)S(1)}, f32[72,768]{1,0:T(8,128)}, u32[]{:S(2)}) copy-start(f32[72,768]{1,0:T(8,128)} %param.24) | copy-start | bytes 663556
  256.3 73.4 %copy-start.46 = (f32[72,768]{1,0:T(8,128)S(1)}, f32[72,768]{1,0:T(8,128)}, u32[]{:S(2)}) copy-start(f32[72,768]{1,0:T(8,128)} %param.23) | copy-start | bytes 663556
  329.6 2.7 copy-start.17
  329.7 2.6 copy-start.37
  329.7 2.6 copy-start.38
  332.3 3.2 copy-start.22
  335.5 2.8 copy-start.19
  335.5 2.8 copy-start.21
  336.6 2.6 copy-start.54
  (11 other events, 14.1 us)

commit v3 on v2

--- a/solution.py
+++ b/solution.py
@@ -56,9 +56,7 @@
     summary[0:LANES] = real
     summary[LANES : 2 * LANES] = imag
     summary[2 * LANES : 3 * LANES] = product
-    summary[24:25] = total_re
-    summary[25:26] = total_im
-    summary[26:27] = total
+    summary[24:32] = jnp.concatenate([total_re, total_im, total, zero[3:]], axis=0)
 
 
 def whole_forward(retain, drive_re, drive_im, turn, summary, start, states):
@@ -114,9 +112,7 @@
     summary[0:LANES] = real
     summary[LANES : 2 * LANES] = imag
     summary[2 * LANES : 3 * LANES] = product
-    summary[24:25] = total_re
-    summary[25:26] = total_im
-    summary[26:27] = total
+    summary[24:32] = jnp.concatenate([total_re, total_im, total, zero[3:]], axis=0)
 
 
 def whole_backward(
@@ -173,22 +169,23 @@
     )(*args)
 
 
-def carry_in(summary, turn, length, reverse):
-    every = lax.all_gather(summary[24:27], "dp", axis=0)
-    cosine, sine = turn_power(
-        turn[0], -turn[1] if reverse else turn[1], length.bit_length() - 1
-    )
+def carry_chain(every, turn, me, length, reverse):
+    sine = -turn[1:2] if reverse else turn[1:2]
+    cosine, sine = turn_power(turn[0:1], sine, length.bit_length() - 1)
     count = every.shape[0]
-    me = lax.axis_index("dp")
     real = jnp.zeros_like(cosine)
     imag = jnp.zeros_like(cosine)
-    order = range(count - 1, 0, -1) if reverse else range(count - 1)
-    for j in order:
+    for j in range(count - 1, 0, -1) if reverse else range(count - 1):
         use = (j > me) if reverse else (j < me)
         turned_re, turned_im = rotate(real, imag, cosine, sine)
-        real = jnp.where(use, every[j, 2] * turned_re + every[j, 0], real)
-        imag = jnp.where(use, every[j, 2] * turned_im + every[j, 1], imag)
-    return jnp.stack([real, imag])
+        real = jnp.where(use, every[j, 2:3] * turned_re + every[j, 0:1], real)
+        imag = jnp.where(use, every[j, 2:3] * turned_im + every[j, 1:2], imag)
+    return jnp.concatenate([real, imag], axis=0)
+
+
+def carry_in(summary, turn, length, reverse):
+    every = lax.all_gather(summary[24:32], "dp", axis=0)
+    return carry_chain(every, turn, lax.axis_index("dp"), length, reverse)
 
 
 def normalize(values, gains):
@@ -229,8 +226,14 @@
 OUT_ROWS = 72
 MIX = CH + 2 * D
 MIX_HALF = 1024
+CHUNK = 512
+CHUNKS = FF // CHUNK
+OUT = 2
 TILE = 128
-VMEM_BYTES = 60 * 1024 * 1024
+VMEM_BYTES = 63 * 1024 * 1024
+SLOTS = 512
+ROWS = 64
+RUN = SLOTS // LANES
 
 
 class Piece:
@@ -250,9 +253,8 @@
         Piece("in", IN_ROWS, half, (half, second + half)),
     ]
     out = [Piece("out", OUT_ROWS, D // 2, (0, D // 2))]
-    wide = FF // 4
     glu = [
-        Piece("in", IN_ROWS, wide, (MIX + wide * k, MIX + FF + wide * k)) for k in range(4)
+        Piece("in", IN_ROWS, CHUNK, (MIX + CHUNK * k, MIX + FF + CHUNK * k)) for k in range(CHUNKS)
     ]
     return mix + out + glu
 
@@ -296,7 +298,9 @@
     def greet(self):
         barrier = pltpu.get_barrier_semaphore()
         partners = [self.sibling(), self.near(0), self.near(1)]
-        partners += [self.plane(self.turn(step)) for step in (1, 2, 3)]
+        for step in (1, 2, 3):
+            partners.append(self.plane(self.turn(step)))
+            partners.append(self.at(self.turn(step), 1 - self.x, self.y, self.core))
         for partner in partners:
             pl.semaphore_signal(barrier, inc=1, device_id=partner, device_id_type=MESH)
         return lambda: pl.semaphore_wait(barrier, len(partners))
@@ -454,59 +458,53 @@
     def __init__(self, place, grads, refs, results):
         n = len(PIECES)
         self.place, self.grads, self.results = place, grads, results
-        self.chip, self.far, self.near, self.planes, self.final = (
-            refs[k * n : (k + 1) * n] for k in range(5)
-        )
-        self.sems = refs[5 * n :]
+        self.far, self.near, self.planes, self.final = (refs[k * n : (k + 1) * n] for k in range(4))
+        self.sems = refs[4 * n :]
 
     @staticmethod
     def scratch():
         n = len(PIECES)
         dma = pltpu.SemaphoreType.DMA
-        shapes = [p.shape() for p in PIECES]
+        blocks = [p.shape()[4:] for p in PIECES]
         return (
-            [pltpu.VMEM(s[1:], LOW) for s in shapes]
-            + [pltpu.VMEM((PLANES, SIDE) + s[4:], LOW) for s in shapes]
-            + [pltpu.VMEM((PLANES,) + s[4:], LOW) for s in shapes] * 2
-            + [pltpu.VMEM(s[4:], WIDE) for s in shapes]
-            + [dma((n, PLANES))] * 8
+            [pltpu.VMEM((PLANES, SIDE) + s, LOW) for s in blocks]
+            + [pltpu.VMEM((PLANES,) + s, LOW) for s in blocks] * 2
+            + [pltpu.VMEM(s, WIDE) for s in blocks]
+            + [dma((n, PLANES))] * 6
             + [dma((n,))] * 2
         )
 
-    def in_chip(self, p, z, core):
+    def block(self, p, z, near, far, core):
+        return self.grads[p].at[z, near, far] if core == 0 else self.grads[p].at[z, far, near]
+
+    def pair(self, p, z, far, core):
+        return self.grads[p].at[z, :, far] if core == 0 else self.grads[p].at[z, far]
+
+    def along_far(self, p, z, core):
         return remote(
-            self.grads[p].at[1 - core, z],
-            self.chip[p].at[z],
+            self.pair(p, z, 1 - self.place.sides(core)[1], core),
+            self.far[p].at[z],
             self.sems[0].at[p, z],
             self.sems[1].at[p, z],
-            self.place.sibling(),
-        )
-
-    def along_far(self, p, z, core):
-        return remote(
-            pair_of(self.grads[p], core, z, 1 - self.place.sides(core)[1]),
-            self.far[p].at[z],
-            self.sems[2].at[p, z],
-            self.sems[3].at[p, z],
             self.place.far(core),
         )
 
     def along_near(self, p, z, core):
         near, far = self.place.sides(core)
         return remote(
-            block_of(self.grads[p], core, z, 1 - near, far),
+            self.block(p, z, 1 - near, far, core),
             self.near[p].at[z],
-            self.sems[4].at[p, z],
-            self.sems[5].at[p, z],
+            self.sems[2].at[p, z],
+            self.sems[3].at[p, z],
             self.place.near(core),
         )
 
     def along_z(self, p, z, sender, core):
         return remote(
-            block_of(self.grads[p], core, z, *self.place.sides(core)),
+            self.block(p, z, *self.place.sides(core), core),
             self.planes[p].at[sender],
-            self.sems[6].at[p, z],
-            self.sems[7].at[p, sender],
+            self.sems[4].at[p, z],
+            self.sems[5].at[p, sender],
             self.place.plane(z),
         )
 
@@ -522,8 +520,8 @@
         return remote(
             self.final[p].at[pl.ds(rows * (1 - core), rows), columns],
             target,
-            self.sems[8].at[p],
-            self.sems[9].at[p],
+            self.sems[6].at[p],
+            self.sems[7].at[p],
             self.place.sibling(),
         )
 
@@ -534,7 +532,7 @@
     def stage0(self, p):
         def run(core):
             for step in self.ORDER:
-                self.in_chip(p, self.place.turn(step), core).start()
+                self.along_far(p, self.place.turn(step), core).start()
 
         self.place.by_core(run)
 
@@ -542,9 +540,9 @@
         def run(core):
             for step in self.ORDER:
                 z = self.place.turn(step)
-                self.in_chip(p, z, core).wait_recv()
-                self.add(self.grads[p].at[core, z], self.chip[p].at[z])
-                self.along_far(p, z, core).start()
+                self.along_far(p, z, core).wait_recv()
+                self.add(self.pair(p, z, self.place.sides(core)[1], core), self.far[p].at[z])
+                self.along_near(p, z, core).start()
 
         self.place.by_core(run)
 
@@ -552,33 +550,21 @@
         def run(core):
             for step in self.ORDER:
                 z = self.place.turn(step)
-                self.along_far(p, z, core).wait_recv()
-                own = pair_of(self.grads[p], core, z, self.place.sides(core)[1])
-                self.add(own, self.far[p].at[z])
-                self.along_near(p, z, core).start()
-
-        self.place.by_core(run)
-
-    def stage3(self, p):
-        def run(core):
-            for step in self.ORDER:
-                z = self.place.turn(step)
                 self.along_near(p, z, core).wait_recv()
-                own = block_of(self.grads[p], core, z, *self.place.sides(core))
-                self.add(own, self.near[p].at[z])
+                self.add(self.block(p, z, *self.place.sides(core), core), self.near[p].at[z])
                 if step:
                     self.along_z(p, z, self.place.z, core).start()
 
         self.place.by_core(run)
 
-    def stage4(self, p):
+    def stage3(self, p):
         rows = PIECES[p].rows
 
         def run(core):
             z = self.place.z
             for step in STEPS_AWAY:
                 self.along_z(p, z, self.place.turn(step), core).wait_recv()
-            total = block_of(self.grads[p], core, z, *self.place.sides(core))[...].astype(WIDE)
+            total = self.block(p, z, *self.place.sides(core), core)[...].astype(WIDE)
             for step in STEPS_AWAY:
                 total = total + self.planes[p][self.place.turn(step)].astype(WIDE)
             self.final[p][...] = total
@@ -594,7 +580,6 @@
             self.to_sibling(p, core).wait_send()
             for step in self.ORDER:
                 z = self.place.turn(step)
-                self.in_chip(p, z, core).wait_send()
                 self.along_far(p, z, core).wait_send()
                 self.along_near(p, z, core).wait_send()
                 if step:
@@ -603,139 +588,647 @@
         self.place.by_core(run)
 
 
-def stagger(stages, count):
-    for tick in range(count + len(stages) - 1):
+def tiled(column, count):
+    return jnp.concatenate([column] * count, axis=1)
+
+
+def some(index, size=ROWS):
+    return pl.ds(pl.multiple_of(index * size, size), size)
+
+
+def each_block(run, size=ROWS, count=SLOTS):
+    lax.fori_loop(0, count // size, lambda i, _: (run(some(i, size)), 0)[1], 0)
+
+
+def inner(left, right, dims=((1,), (0,))):
+    return lax.dot_general(left, right, (dims, ((), ())), preferred_element_type=WIDE)
+
+
+def across(left, right):
+    return inner(left, right, ((1,), (1,)))
+
+
+def along(left, right):
+    return inner(left, right, ((0,), (0,)))
+
+
+def out_segments(start, count):
+    size, runs, stop = 2 * OUT_ROWS, [], start + count
+    while start < stop:
+        chip, first = divmod(start, size)
+        last = min(size, first + stop - start)
+        runs.append((chip // 4, chip // 2 % 2, chip % 2, first, last))
+        start += last - first
+    return runs
+
+
+def row_norm(values):
+    return lax.rsqrt(jnp.mean(values * values, axis=1, keepdims=True) + NORM_EPSILON)
+
+
+def eights(values):
+    return jnp.sum(values.reshape(values.shape[0] // 8, 8, values.shape[1]), axis=0)
+
+
+def block_scratch():
+    vmem, dma = pltpu.VMEM, pltpu.SemaphoreType.DMA
+    rows = (SLOTS, D)
+    both = (2 * SLOTS, D)
+    return dict(
+        arrivals=dma((2,)),
+        departures=dma((2,)),
+        perm=vmem((SLOTS, SLOTS), LOW),
+        live=vmem((SLOTS, TILE), WIDE),
+        opens=vmem((SLOTS, TILE), WIDE),
+        params=vmem((8, D), WIDE),
+        tokens=vmem(rows, LOW),
+        upstream=vmem((2, SLOTS, D // 2), LOW),
+        upstream_got=vmem((SLOTS, D // 2), LOW),
+        normed=vmem(both, LOW),
+        normed_two=vmem(both, LOW),
+        gated=vmem(both, LOW),
+        hidden=vmem((CHUNKS, 2 * SLOTS, CHUNK), LOW),
+        d_glu=vmem((CHUNKS, 2, SLOTS, CHUNK), LOW),
+        d_glu_got=vmem((CHUNKS, SLOTS, CHUNK), LOW),
+        d_out=vmem((2, SLOTS, D // 2), LOW),
+        d_out_got=vmem((SLOTS, D // 2), LOW),
+        d_mix=vmem((2, 2, SLOTS, MIX_HALF // 2), LOW),
+        d_mix_got=vmem((2, SLOTS, MIX_HALF // 2), LOW),
+        pre_mix=vmem((SLOTS, MIX), WIDE),
+        glu=vmem((3, SLOTS // 2, CHUNK), WIDE),
+        retain=vmem((SLOTS, CH), WIDE),
+        drive=vmem(rows, WIDE),
+        states=vmem((2, SLOTS + LANES, CH), WIDE),
+        summaries=vmem((2, 32, CH), WIDE),
+        every=vmem((2, PLANES * SIDE, 8, CH), WIDE),
+        middle=vmem(rows, WIDE),
+        d_normed=vmem(rows, WIDE),
+        total=vmem(rows, WIDE),
+        block_out=vmem(rows, LOW),
+        sums=vmem((3, 8, D), WIDE),
+        vector=vmem((8, VEC_ROWS, TILE), WIDE),
+        pair_sent=dma((PAIRS,)),
+        pair_got=dma((PAIRS,)),
+        carry_sent=dma((2, PLANES * SIDE)),
+        carry_got=dma((2, PLANES * SIDE)),
+        vector_sent=dma((6,)),
+        vector_got=dma((6,)),
+    )
+
+
+VEC_ROWS = 24
+VEC_COUNT = 18
+PAIRS = 16
+
+
+class Block:
+    def __init__(self, place, buffers, grads, refs):
+        self.place, self.weights, self.grads = place, buffers, grads
+        for name, ref in refs.items():
+            setattr(self, name, ref)
+        self.me = place.z * SIDE + place.x
+
+
+    def swaps(self):
+        own, got = pl.ds(0, SLOTS), pl.ds(SLOTS, SLOTS)
+        other = 1 - self.place.core
+        pairs = dict(
+            normed=(self.normed.at[own], self.normed.at[got]),
+            normed_two=(self.normed_two.at[own], self.normed_two.at[got]),
+            gated=(self.gated.at[own], self.gated.at[got]),
+            upstream=(self.upstream.at[other], self.upstream_got),
+            d_out=(self.d_out.at[other], self.d_out_got),
+        )
+        for k in range(CHUNKS):
+            pairs["hidden", k] = (self.hidden.at[k, own], self.hidden.at[k, got])
+            pairs["d_glu", k] = (self.d_glu.at[k, other], self.d_glu_got.at[k])
+        for m in range(2):
+            pairs["d_mix", m] = (self.d_mix.at[other, m], self.d_mix_got.at[m])
+        return pairs
+
+    def swap(self, name):
+        pairs = self.swaps()
+        slot = list(pairs).index(name)
+        sems = self.pair_sent.at[slot], self.pair_got.at[slot]
+        return remote(*pairs[name], *sems, self.place.sibling())
+
+    def give(self, *names):
+        for name in names:
+            self.swap(name).start()
+
+    def take(self, *names):
+        for name in names:
+            self.swap(name).wait_recv()
+
+    def settle(self):
+        for name in self.swaps():
+            self.swap(name).wait_send()
+
+
+    def mix_weight(self, half, m):
+        return self.weights[m][half].reshape(D, MIX_HALF // 2)
+
+    def glu_weight(self, k):
+        parts = [self.weights[OUT + 1 + k][half].reshape(D, CHUNK) for half in range(2)]
+        return jnp.concatenate(parts, axis=1)
+
+    def out_weight(self, start, count):
+        halves = []
+        for half in range(2):
+            ref = self.weights[OUT]
+            parts = [
+                ref[half, z, x, y, first:last] for z, x, y, first, last in out_segments(start, count)
+            ]
+            halves.append(jnp.concatenate(parts, axis=0))
+        return jnp.concatenate(halves, axis=1)
+
+    def put_in(self, p, value):
+        self.grads[p][...] = value.astype(LOW).reshape(self.grads[p].shape)
+
+    def put_out(self, start, value):
+        value, done = value.astype(LOW), 0
+        for z, x, y, first, last in out_segments(start, value.shape[0]):
+            count = last - first
+            self.grads[OUT][z, x, y, first:last] = value[done : done + count]
+            done += count
+
+
+    def prepare(self, padding, opening, vectors):
+        row = lax.broadcasted_iota(jnp.int32, (SLOTS, SLOTS), 0)
+        column = lax.broadcasted_iota(jnp.int32, (SLOTS, SLOTS), 1)
+        perm = (column == row % LANES * RUN + row // LANES).astype(WIDE)
+        self.perm[...] = perm.astype(LOW)
+        ones = jnp.ones((SLOTS, TILE), LOW)
+        self.live[...] = inner((perm * padding[...].astype(WIDE)).astype(LOW), ones)
+        self.opens[...] = inner((perm * opening[...].astype(WIDE)).astype(LOW), ones)
+
+        def line(first, count):
+            return jnp.concatenate([vectors[first + i : first + i + 1] for i in range(count)], axis=1)
+
+        phase = line(12, 3)
+        self.params[0:1] = line(0, 6)
+        self.params[1:2] = line(6, 6)
+        self.params[2:3] = jnp.concatenate([jnp.cos(phase), jnp.sin(phase)], axis=1)
+        self.params[3:4] = jnp.concatenate([line(15, 3)] * 2, axis=1)
+        self.sums[...] = jnp.zeros_like(self.sums)
+
+    def turn(self):
+        return jnp.concatenate([self.params[2:3, :CH], self.params[2:3, CH:]], axis=0)
+
+    def first_norm(self, raw):
+        self.tokens[...] = inner(self.perm[...], raw[...]).astype(LOW)
+
+        def run(rows):
+            values = self.tokens[rows, :].astype(WIDE)
+            self.normed[rows, :] = (values * row_norm(values) * self.params[0:1]).astype(LOW)
+
+        each_block(run)
+
+    def mask_upstream(self, raw):
+        striped = inner(self.perm[...], raw[...]) * tiled(self.live[...], D // TILE)
+        self.upstream[0] = striped[:, : D // 2].astype(LOW)
+        self.upstream[1] = striped[:, D // 2 :].astype(LOW)
+
+    def mix(self, m):
+        normed, width = self.normed[0:SLOTS, :], MIX_HALF // 2
+        piece = PIECES[m]
+        for half in range(2):
+            skip = piece.overlap * half
+            start = piece.starts[half] + skip
+            product = inner(normed, self.mix_weight(half, m))
+            self.pre_mix[:, start : start + width - skip] = product[:, skip:]
+
+    def drives(self):
+        def run(rows):
+            forget = jax.nn.sigmoid(-(self.pre_mix[rows, :CH] + self.params[3:4, :CH]))
+            pre = self.pre_mix[rows, CH : CH + D]
+            driver = pre * jax.nn.sigmoid(pre)
+            opens = tiled(self.opens[rows, :], CH // TILE)
+            decay = jnp.where(opens > 0.5, 1.0, forget).astype(LOW).astype(WIDE)
+            self.retain[rows, :] = 1.0 - decay
+            drive = jnp.concatenate([forget, forget], axis=1) * driver
+            self.drive[rows, :] = drive.astype(LOW).astype(WIDE)
+
+        each_block(run)
+
+    def parts(self):
+        return self.drive.at[:, pl.ds(0, CH)], self.drive.at[:, pl.ds(CH, CH)]
+
+    def others(self):
+        place = self.place
+        for step in range(PLANES):
+            for flip in range(SIDE):
+                if step or flip:
+                    z = place.turn(step)
+                    x = 1 - place.x if flip else place.x
+                    yield z * SIDE + x, place.at(z, x, place.y, place.core)
+
+    def carry_copy(self, way, other, device, sender):
+        return remote(
+            self.summaries.at[way, pl.ds(24, 8)],
+            self.every.at[way, sender],
+            self.carry_sent.at[way, other],
+            self.carry_got.at[way, sender],
+            device,
+        )
+
+    def scan_own(self, way):
+        run = local_backward if way else local_forward
+        run(self.retain, *self.parts(), self.turn(), self.summaries.at[way])
+        self.every[way, self.me] = self.summaries[way, 24:32]
+        for other, device in self.others():
+            self.carry_copy(way, other, device, self.me).start()
+
+    def carried(self, way):
+        for other, device in self.others():
+            self.carry_copy(way, other, device, other).wait_recv()
+        turn = self.turn()
+        return carry_chain(self.every.at[way], turn, self.me, SLOTS, way == 1)
+
+    def scan_states(self):
+        start = self.carried(0)
+        run = whole_forward
+        run(self.retain, *self.parts(), self.turn(), self.summaries.at[0], start, self.states)
+
+    def recurrent(self, rows):
+        after = pl.ds(pl.multiple_of(rows.start + LANES, LANES), rows.size)
+        both = jnp.concatenate([self.states[0, after, :], self.states[1, after, :]], axis=1)
+        return both.astype(LOW).astype(WIDE)
+
+    def gate_rows(self):
+        def run(rows):
+            pre = self.pre_mix[rows, CH + D :]
+            masked = self.recurrent(rows) * tiled(self.live[rows, :], D // TILE)
+            self.gated[rows, :] = (masked * (pre * jax.nn.sigmoid(pre))).astype(LOW)
+
+        each_block(run)
+
+    def second_norm(self):
+        self.middle[...] = inner(self.gated[0:SLOTS, :], self.out_weight(0, D))
+
+        def run(rows):
+            middle = self.tokens[rows, :].astype(WIDE) + self.middle[rows, :]
+            self.middle[rows, :] = middle
+            self.normed_two[rows, :] = (middle * row_norm(middle) * self.params[1:2]).astype(LOW)
+
+        each_block(run)
+
+    def glu_forward(self, k):
+        weight = self.glu_weight(k)
+        down = self.out_weight(D + CHUNK * k, CHUNK)
+        half = SLOTS // 2
+        for part in range(2):
+            rows = slice(part * half, (part + 1) * half)
+            pre = inner(self.normed_two[rows, :], weight)
+            self.glu[0] = pre[:, :CHUNK]
+            self.glu[1] = pre[:, CHUNK:]
+            upstream = jnp.concatenate([self.upstream[0, rows], self.upstream[1, rows]], axis=1)
+            self.glu[2] = across(upstream, down)
+
+            def run(block):
+                gate, up, d_hidden = (self.glu[i, block, :] for i in range(3))
+                own = pl.ds(pl.multiple_of(block.start + part * half, ROWS), ROWS)
+                logistic = jax.nn.sigmoid(gate)
+                active = gate * logistic
+                slope = logistic * (1.0 + gate * (1.0 - logistic))
+                self.hidden[k, own, :] = (active * up).astype(LOW)
+                self.d_glu[k, 0, own, :] = (d_hidden * up * slope).astype(LOW)
+                self.d_glu[k, 1, own, :] = (d_hidden * active).astype(LOW)
+
+            each_block(run, count=half)
+
+    def glu_back(self, k):
+        down = self.out_weight(D + CHUNK * k, CHUNK)
+        share = inner(self.hidden[k, 0:SLOTS, :], down)
+        d_glu = jnp.concatenate([self.d_glu[k, 0], self.d_glu[k, 1]], axis=1)
+        d_share = across(d_glu, self.glu_weight(k))
+        if k == 0:
+            self.total[...] = self.middle[...] + share
+            self.d_normed[...] = d_share
+        else:
+            self.total[...] += share
+            self.d_normed[...] += d_share
+        if k == CHUNKS - 1:
+            self.block_out[...] = self.total[...].astype(LOW)
+
+    def own_half(self, ref, got):
+        return jnp.concatenate([ref[self.place.core], got], axis=0)
+
+    def glu_grads(self, k):
+        d_glu = jnp.concatenate([self.d_glu[k, self.place.core], self.d_glu_got[k]], axis=0)
+        self.put_in(OUT + 1 + k, along(self.normed_two[...], d_glu))
+        upstream = self.own_half(self.upstream, self.upstream_got[...])
+        self.put_out(D + CHUNK * k, along(self.hidden[k], upstream))
+
+    def add_sum(self, index, values):
+        self.sums[index, :, : values.shape[1]] += eights(values)
+
+    def middle_back(self):
+        def run(rows):
+            middle, d_normed = self.middle[rows, :], self.d_normed[rows, :]
+            scaling = row_norm(middle)
+            self.add_sum(1, d_normed * middle * scaling)
+            scaled = d_normed * self.params[1:2]
+            mean = jnp.mean(middle * scaled, axis=1, keepdims=True)
+            upstream = jnp.concatenate([self.upstream[0, rows], self.upstream[1, rows]], axis=1)
+            d_middle = upstream.astype(WIDE) + scaling * scaled - middle * (scaling**3 * mean)
+            self.middle[rows, :] = d_middle
+            self.d_out[0, rows] = d_middle[:, : D // 2].astype(LOW)
+            self.d_out[1, rows] = d_middle[:, D // 2 :].astype(LOW)
+
+        each_block(run)
+
+    def gate_back(self):
+        d_out = jnp.concatenate([self.d_out[0], self.d_out[1]], axis=1)
+        self.total[...] = across(d_out, self.out_weight(0, D))
+
+        def run(rows):
+            pre, d_gated = self.pre_mix[rows, CH + D :], self.total[rows, :]
+            logistic = jax.nn.sigmoid(pre)
+            d_live = d_gated * tiled(self.live[rows, :], D // TILE)
+            self.drive[rows, :] = (d_live * (pre * logistic)).astype(LOW).astype(WIDE)
+            slope = logistic * (1.0 + pre * (1.0 - logistic))
+            d_gate = (d_live * self.recurrent(rows) * slope).astype(LOW)
+            self.d_mix[1, 0, rows, 2 * TILE :] = d_gate[:, : 2 * TILE]
+            self.d_mix[1, 1, rows, :] = d_gate[:, 2 * TILE :]
+
+        each_block(run)
+
+    def mixer_out_grad(self):
+        d_out = self.own_half(self.d_out, self.d_out_got[...])
+        self.put_out(0, along(self.gated[...], d_out))
+
+    def scan_back(self):
+        start = self.carried(1)
+        real, imag = self.parts()
+        whole_backward(
+            self.retain,
+            real,
+            imag,
+            self.turn(),
+            self.summaries.at[1],
+            start,
+            self.states,
+            self.retain,
+            real,
+            imag,
+            self.sums.at[2, pl.ds(0, 1), pl.ds(0, CH)],
+        )
+
+    def drives_back(self):
+        def run(rows):
+            forget = jax.nn.sigmoid(-(self.pre_mix[rows, :CH] + self.params[3:4, :CH]))
+            pre = self.pre_mix[rows, CH : CH + D]
+            logistic = jax.nn.sigmoid(pre)
+            d_decay = self.retain[rows, :].astype(LOW).astype(WIDE)
+            d_input = self.drive[rows, :].astype(LOW).astype(WIDE)
+            pulled = d_input * (pre * logistic)
+            opens = tiled(self.opens[rows, :], CH // TILE)
+            d_forget = jnp.where(opens > 0.5, 0.0, d_decay) + pulled[:, :CH] + pulled[:, CH:]
+            d_first = -forget * (1.0 - forget) * d_forget
+            self.sums[2, :, CH:] += eights(d_first)
+            slope = logistic * (1.0 + pre * (1.0 - logistic))
+            d_driver = d_input * jnp.concatenate([forget, forget], axis=1) * slope
+            d_pre = jnp.concatenate([d_first, d_driver], axis=1).astype(LOW)
+            half = MIX_HALF // 2
+            self.d_mix[0, 0, rows, :] = d_pre[:, :half]
+            self.d_mix[0, 1, rows, :] = d_pre[:, half : 2 * half]
+            self.d_mix[1, 0, rows, : 2 * TILE] = d_pre[:, MIX_HALF - TILE :]
+
+        each_block(run)
+
+    def mix_grads(self, m):
+        d_mix = jnp.concatenate([self.d_mix[self.place.core, m], self.d_mix_got[m]], axis=0)
+        self.put_in(m, along(self.normed[...], d_mix))
+
+    def first_back(self):
+        lefts, rights = [], []
+        for half in range(2):
+            for m in range(2):
+                skip = PIECES[m].overlap * half
+                lefts.append(self.d_mix[half, m][:, skip:])
+                rights.append(self.mix_weight(half, m)[:, skip:])
+        product = across(jnp.concatenate(lefts, axis=1), jnp.concatenate(rights, axis=1))
+        self.d_normed[...] = product
+
+        def run(rows):
+            values, d_normed = self.tokens[rows, :].astype(WIDE), self.d_normed[rows, :]
+            scaling = row_norm(values)
+            self.add_sum(0, d_normed * values * scaling)
+            scaled = d_normed * self.params[0:1]
+            mean = jnp.mean(values * scaled, axis=1, keepdims=True)
+            self.middle[rows, :] += scaling * scaled - values * (scaling**3 * mean)
+
+        each_block(run)
+
+
+    def gather_vector(self):
+        lines = [
+            jnp.sum(self.sums[0], axis=0, keepdims=True),
+            jnp.sum(self.sums[1], axis=0, keepdims=True),
+            jnp.concatenate(
+                [self.sums[2, 0:1, :CH], jnp.sum(self.sums[2, :, CH:], axis=0, keepdims=True)], axis=1
+            ),
+        ]
+        for i, line in enumerate(lines):
+            for j in range(D // TILE):
+                row = i * (D // TILE) + j
+                self.vector[0, row : row + 1] = line[:, j * TILE : (j + 1) * TILE]
+        filled = jnp.sum(self.live[...], axis=0, keepdims=True)
+        rest = jnp.zeros((VEC_ROWS - VEC_COUNT - 1, TILE), WIDE)
+        self.vector[0, VEC_COUNT:] = jnp.concatenate([filled, rest], axis=0)
+
+    def vector_copy(self, stage):
+        place = self.place
+        device = (place.sibling(), place.near(0), place.near(1))[stage]
+        source = self.vector.at[stage]
+        target = self.vector.at[4 + stage]
+        return remote(source, target, self.vector_sent.at[stage], self.vector_got.at[stage], device)
+
+    def vector_step(self, stage):
+        if stage:
+            self.vector_copy(stage - 1).wait_recv()
+            self.vector[stage] = self.vector[stage - 1] + self.vector[3 + stage]
+        if stage < 3:
+            self.vector_copy(stage).start()
+
+    def vector_plane(self, planes, step, sender):
+        place = self.place
+        return remote(
+            self.vector.at[3],
+            planes.at[sender],
+            self.vector_sent.at[2 + step],
+            self.vector_got.at[2 + step],
+            place.plane(place.turn(step)),
+        )
+
+
+def block_kernel(tokens, cotangent, padding, opening, w_in, w_out, vectors, *refs):
+    n = len(PIECES)
+    block_out, d_tokens, sum_in, sum_out, planes = refs[:5]
+    refs = refs[5:]
+    count = len(Gather.scratch())
+    gather_refs, refs = refs[:count], refs[count:]
+    buffers, staging, gather_sems = gather_refs[:n], gather_refs[n : 2 * n], gather_refs[2 * n :]
+    grads, refs = refs[:n], refs[n:]
+    count = len(Reduce.scratch())
+    reduce_refs, refs = refs[:count], refs[count:]
+    place = Place()
+    gather = Gather(place, {"in": w_in, "out": w_out}, buffers, staging, gather_sems)
+    reduce = Reduce(place, grads, reduce_refs, {"in": sum_in, "out": sum_out})
+    block = Block(place, buffers, grads, dict(zip(block_scratch(), refs, strict=True)))
+
+    entered = place.greet()
+    raw_tokens, raw_upstream = block.gated.at[pl.ds(0, SLOTS)], block.block_out
+    loads = [
+        pltpu.make_async_copy(tokens.at[0], raw_tokens, block.arrivals.at[0]),
+        pltpu.make_async_copy(cotangent.at[0], raw_upstream, block.arrivals.at[1]),
+    ]
+    for load in loads:
+        load.start()
+    block.prepare(padding, opening, vectors)
+    entered()
+    gather.begin()
+    loads[0].wait()
+    block.first_norm(raw_tokens)
+    loads[1].wait()
+    block.mask_upstream(raw_upstream)
+    block.give("normed", "upstream")
+
+    stages = (gather.stage0, gather.stage1, gather.stage2, gather.stage3, gather.stage4)
+
+    def tick(now):
         for lag, stage in enumerate(stages):
-            if 0 <= tick - lag < count:
-                stage(tick - lag)
-
-
-def gather_kernel(w_in, w_out, *refs):
-    n = len(PIECES)
-    results, (buffers, staging, rest) = refs[:n], (refs[n : 2 * n], refs[2 * n : 3 * n], refs[3 * n :])
-    done, sems = rest[-1], rest[:-1]
-    place = Place()
-    gather = Gather(place, {"in": w_in, "out": w_out}, buffers, staging, sems)
-    place.greet()()
-    gather.begin()
-    stagger([gather.stage0, gather.stage1, gather.stage2, gather.stage3, gather.stage4], n)
-    copies = [pltpu.make_async_copy(buffers[p], results[p], done.at[p]) for p in range(n)]
-    for copy in copies:
-        copy.start()
+            if 0 <= now - lag < n:
+                stage(now - lag)
+
+    for now in range(5):
+        tick(now)
+    block.mix(0)
+    tick(5)
+    block.mix(1)
+    block.drives()
+    block.scan_own(0)
+    tick(6)
+    block.scan_states()
+    block.gate_rows()
+    block.give("gated")
+    block.second_norm()
+    block.give("normed_two")
+    block.take("upstream", "normed_two")
+
+    def glu(k):
+        block.glu_forward(k)
+        block.give(("hidden", k), ("d_glu", k))
+        block.glu_back(k)
+        block.take(("hidden", k), ("d_glu", k))
+        block.glu_grads(k)
+        reduce.stage0(OUT + 1 + k)
+
+    tick(7)
+    glu(0)
+    tick(8)
+    reduce.stage1(OUT + 1)
+    glu(1)
+    tick(9)
+    reduce.stage2(OUT + 1)
+    reduce.stage1(OUT + 2)
+    glu(2)
+    leave_out = pltpu.make_async_copy(block.block_out, block_out, block.departures.at[0])
+    leave_out.start()
+    block.middle_back()
+    block.give("d_out")
+    reduce.stage3(OUT + 1)
+    reduce.stage2(OUT + 2)
+    reduce.stage1(OUT + 3)
+    block.gate_back()
+    block.scan_own(1)
+    block.take("gated", "d_out")
+    block.mixer_out_grad()
+    reduce.stage0(OUT)
+    block.scan_back()
+    reduce.stage3(OUT + 2)
+    reduce.stage2(OUT + 3)
+    block.drives_back()
+    block.give(("d_mix", 0), ("d_mix", 1))
+    reduce.stage1(OUT)
+    block.take("normed", ("d_mix", 0), ("d_mix", 1))
+    block.mix_grads(0)
+    reduce.stage0(0)
+    block.mix_grads(1)
+    reduce.stage0(1)
+    reduce.stage3(OUT + 3)
+    block.first_back()
+    leave_tokens = pltpu.make_async_copy(block.middle, d_tokens, block.departures.at[1])
+    leave_tokens.start()
+    block.gather_vector()
+    block.vector_step(0)
+    reduce.stage2(OUT)
+    reduce.stage1(0)
+    block.vector_step(1)
+    reduce.stage1(1)
+    reduce.stage3(OUT)
+    block.vector_step(2)
+    reduce.stage2(0)
+    reduce.stage2(1)
+    block.vector_step(3)
+    for step in (1, 2, 3):
+        block.vector_plane(planes, step, place.z).start()
+    planes[place.z] = block.vector[3]
+    reduce.stage3(0)
+    reduce.stage3(1)
+
+    for step in (1, 2, 3):
+        block.vector_plane(planes, step, place.z).wait_send()
+        block.vector_plane(planes, step, place.turn(4 - step)).wait_recv()
+    for stage in range(3):
+        block.vector_copy(stage).wait_send()
+    for way in range(2):
+        for other, device in block.others():
+            block.carry_copy(way, other, device, block.me).wait_send()
+    block.settle()
     for p in range(n):
         gather.drain(p)
-    for copy in copies:
-        copy.wait()
-
-
-def gather_call(w_in, w_out):
-    n = len(PIECES)
+        reduce.drain(p)
+    leave_out.wait()
+    leave_tokens.wait()
+
+
+def block_routed(tokens, cotangent, padding, opening, w_in, w_out, vectors):
+    vmem = pl.BlockSpec(memory_space=pltpu.VMEM)
     anywhere = pl.BlockSpec(memory_space=pl.ANY)
-    return pl.pallas_call(
-        gather_kernel,
-        out_shape=[jax.ShapeDtypeStruct(p.shape(), LOW) for p in PIECES],
-        in_specs=[anywhere] * 2,
-        out_specs=[anywhere] * n,
-        scratch_shapes=Gather.scratch() + [pltpu.SemaphoreType.DMA((n,))],
+    out_shape = [
+        jax.ShapeDtypeStruct((SLOTS, D), LOW),
+        jax.ShapeDtypeStruct((SLOTS, D), WIDE),
+        jax.ShapeDtypeStruct(w_in.shape, WIDE),
+        jax.ShapeDtypeStruct(w_out.shape, WIDE),
+        jax.ShapeDtypeStruct((PLANES, VEC_ROWS, TILE), WIDE),
+    ]
+    grads = [pltpu.VMEM(p.shape()[1:], LOW) for p in PIECES]
+    block_out, d_tokens, sum_in, sum_out, planes = pl.pallas_call(
+        block_kernel,
+        out_shape=out_shape,
+        in_specs=[anywhere, anywhere, vmem, vmem, anywhere, anywhere, vmem],
+        out_specs=[anywhere, anywhere, vmem, vmem, vmem],
+        scratch_shapes=Gather.scratch()
+        + grads
+        + Reduce.scratch()
+        + list(block_scratch().values()),
         compiler_params=pltpu.CompilerParams(
             collective_id=0, has_side_effects=True, vmem_limit_bytes=VMEM_BYTES
         ),
-    )(w_in, w_out)
-
-
-def reduce_kernel(*refs):
-    n = len(PIECES)
-    sources, results, grads = refs[:n], refs[n : n + 2], refs[n + 2 : 2 * n + 2]
-    loaded, rest = refs[2 * n + 2], refs[2 * n + 3 :]
-    place = Place()
-    reduce = Reduce(place, grads, rest, {"in": results[0], "out": results[1]})
-    entered = place.greet()
-    copies = [pltpu.make_async_copy(sources[p], grads[p], loaded.at[p]) for p in range(n)]
-    for copy in copies:
-        copy.start()
-    entered()
-    for copy in copies:
-        copy.wait()
-    stagger([reduce.stage0, reduce.stage1, reduce.stage2, reduce.stage3, reduce.stage4], n)
-    for p in range(n):
-        reduce.drain(p)
-
-
-def reduce_call(pieces):
-    n = len(PIECES)
-    return pl.pallas_call(
-        reduce_kernel,
-        out_shape=[
-            jax.ShapeDtypeStruct((IN_ROWS, MIX + 2 * FF), WIDE),
-            jax.ShapeDtypeStruct((OUT_ROWS, D), WIDE),
-        ],
-        in_specs=[pl.BlockSpec(memory_space=pl.ANY)] * n,
-        out_specs=[pl.BlockSpec(memory_space=pltpu.VMEM)] * 2,
-        scratch_shapes=[pltpu.VMEM(p.shape(), LOW) for p in PIECES]
-        + [pltpu.SemaphoreType.DMA((n,))]
-        + Reduce.scratch(),
-        compiler_params=pltpu.CompilerParams(
-            collective_id=1, has_side_effects=True, vmem_limit_bytes=VMEM_BYTES
-        ),
-    )(*pieces)
-
-
-def routed(w_in, w_out):
+    )(tokens, cotangent, padding, opening, w_in, w_out, vectors.reshape(VEC_COUNT, TILE))
+    sums = jnp.sum(planes, axis=0)
+    return block_out, d_tokens, sum_in, sum_out, sums[:VEC_COUNT].reshape(-1), sums[VEC_COUNT, 0]
+
+
+def routed(tokens, w_in, w_out):
     sizes = (lax.axis_size("dp"), lax.axis_size("rep"))
-    return sizes == (PLANES * SIDE, SIDE * 2) and (w_in.shape[0], w_out.shape[0]) == (
-        IN_ROWS,
-        OUT_ROWS,
-    )
-
-
-def gather_weights(w_in, w_out):
-    if not routed(w_in, w_out):
-        axes = ("dp", "rep")
-        return (
-            lax.all_gather(w_in.astype(LOW), axes, axis=0, tiled=True),
-            lax.all_gather(w_out.astype(LOW), axes, axis=0, tiled=True),
-        )
-    got = gather_call(w_in, w_out)
-    parts = [[g[half].reshape(-1, g.shape[-1]) for g in got] for half in range(2)]
-    mix = parts[0][:2] + [parts[1][0][:, TILE:], parts[1][1]]
-    full_in = jnp.concatenate(mix + parts[0][3:] + parts[1][3:], axis=1)
-    return full_in, jnp.concatenate([parts[0][2], parts[1][2]], axis=1)
-
-
-def reduce_grads(grad_in, grad_out, shard_in, shard_out):
-    if not routed(shard_in, shard_out):
-        axes = ("dp", "rep")
-        return (
-            lax.psum_scatter(grad_in, axes, scatter_dimension=0, tiled=True),
-            lax.psum_scatter(grad_out, axes, scatter_dimension=0, tiled=True),
-        )
-    whole = {"in": grad_in.astype(LOW), "out": grad_out.astype(LOW)}
-    pieces = []
-    for piece in PIECES:
-        halves = [
-            whole[piece.matrix][:, start : start + piece.columns].reshape(piece.shape()[1:])
-            for start in piece.starts
-        ]
-        pieces.append(jnp.stack(halves))
-    return reduce_call(pieces)
-
-
-def body(
-    tokens,
-    cotangent,
-    padding,
-    opening,
-    w_in,
-    w_out,
-    vectors,
-    m_in,
-    v_in,
-    m_out,
-    v_out,
-    m_vec,
-    v_vec,
-    counter,
-):
+    shards = (tokens.shape[1], w_in.shape[0], w_out.shape[0])
+    return sizes == (PLANES * SIDE, SIDE * 2) and shards == (SLOTS, IN_ROWS, OUT_ROWS)
+
+
+def block_anywhere(tokens, cotangent, padding, opening, w_in, w_out, vectors):
     low = jnp.bfloat16
     wide = jnp.float32
     mixer_cols = CH + 2 * D
@@ -748,7 +1241,9 @@
     phases = vectors[2 * D : 2 * D + CH]
     biases = vectors[2 * D + CH :]
     turn = jnp.stack([jnp.cos(phases), jnp.sin(phases)])
-    full_in, full_out = gather_weights(w_in, w_out)
+    axes = ("dp", "rep")
+    full_in = lax.all_gather(w_in.astype(low), axes, axis=0, tiled=True)
+    full_out = lax.all_gather(w_out.astype(low), axes, axis=0, tiled=True)
     normed, scaling_one = normalize(inputs, gains_one)
     normed_low = normed.astype(low)
     pre_mix = jnp.dot(normed_low, full_in[:, :mixer_cols], preferred_element_type=wide)
@@ -828,8 +1323,32 @@
     grad_vectors = jnp.concatenate([grad_gains_one, grad_gains_two, d_phase[0], grad_biases])
     grad_in_all = jnp.concatenate([grad_mixer_in, grad_glu], axis=1)
     grad_out_all = jnp.concatenate([grad_mixer_out, grad_down], axis=0)
-    summed_in, summed_out = reduce_grads(grad_in_all, grad_out_all, w_in, w_out)
-    summed_vec, total = lax.psum((grad_vectors, jnp.sum(filled)), ("dp", "rep"))
+    summed_in = lax.psum_scatter(grad_in_all, axes, scatter_dimension=0, tiled=True)
+    summed_out = lax.psum_scatter(grad_out_all, axes, scatter_dimension=0, tiled=True)
+    summed_vec, total = lax.psum((grad_vectors, jnp.sum(filled)), axes)
+    return block_out.astype(low), d_tokens, summed_in, summed_out, summed_vec, total
+
+
+def body(
+    tokens,
+    cotangent,
+    padding,
+    opening,
+    w_in,
+    w_out,
+    vectors,
+    m_in,
+    v_in,
+    m_out,
+    v_out,
+    m_vec,
+    v_vec,
+    counter,
+):
+    run = block_routed if routed(tokens, w_in, w_out) else block_anywhere
+    block_out, d_tokens, summed_in, summed_out, summed_vec, total = run(
+        tokens, cotangent, padding, opening, w_in, w_out, vectors
+    )
     steps = counter[0].astype(jnp.float32)
     grad_in = summed_in / total
     grad_out = summed_out / total
@@ -844,7 +1363,7 @@
         vectors, grad_vec, m_vec, v_vec, steps, 0.0
     )
     return (
-        unstripe(block_out.astype(jnp.bfloat16))[None],
+        unstripe(block_out)[None],
         unstripe(d_tokens)[None],
         grad_in,
         new_in,

time: 348 us -> 170 us (0.49); the launches traced: 342 us -> 168 us
  blocking collectives: 98.8 us -> 0 us
  matrix products: 41.2 us -> 0 us
  local copies, waits for them, and re-layouts: 26.9 us -> 5.07 us
  other arithmetic: 26.9 us -> 6.92 us
  Pallas kernels: 146 us -> 155 us
    psum x1 -> x0, blocking collectives: 50.7 us -> none  [body(): summed_vec, total = lax.psum((grad_vectors, jnp.sum(filled)), ('dp', 'rep'))]
    all_gather x2 -> x0, blocking collectives: 48.1 us -> none  [carry_in(): every = lax.all_gather(summary[24:27], 'dp', axis=0)]
    dot_general x12 -> x0, matrix products: 41.2 us -> none  [the longest x1 5.58 us: body(): jnp.dot(normed_low, full_in[:, :mixer_cols], preferred_element_type=wide)]
    unnamed x127 -> x26, local copies, waits for them, and re-layouts: 14.9 us -> 0.06 us
    another operation x13 -> x0, other arithmetic: 9.63 us -> none  [the longest x7 9.42 us: reduce_grads(): pieces.append(jnp.stack(halves))]
    pallas_call x6 -> x1, Pallas kernels: 146 us -> 155 us  [block_routed(): pl.pallas_call(block_kernel, out_shape=out_shape, in_specs=[anywhere, any...]
    slice x14 -> x1, local copies, waits for them, and re-layouts: 7.71 us -> 0.54 us  [block_routed(): sums[VEC_COUNT, 0]]
where the time goes in v3:
time: 170 us; the launch traced here: 168 us
  Pallas kernels  155 us (91%)
  other arithmetic  6.92 us (4%)
  local copies, waits for them, and re-layouts  5.07 us (3%)
    pallas_call x1, Pallas kernels, block_routed(): pl.pallas_call(block_kernel, out_shape=out_shape, in_specs=[anywhere, any...  155 us
    transpose x2, local copies, waits for them, and re-layouts, unstripe(): rows.reshape(count // LANES, LANES, columns).swapaxes(0, 1)  3.89 us

profile of v3, /device:TPU:3, one launch (start us, length us, event | category | flops | bytes accessed | tf_op | source)
XLA Modules:
  0.0 168.2 jit_solution(3072055052323649434)
XLA Ops:
  0.7 154.7 %shard_map.269 = (bf16[512,768]{1,0:T(8,128)(2,1)}, f32[512,768]{1,0:T(8,128)}, f32[24,4992]{1,0:T(8,128)}, f32[72,768]{1,0:T(8,128)}, f32[4,24,128]{2,1,0:T(8,128)}) custom-call(bf16[1,512,768]{2,1,0:T(8,128)(2,1)} %tokens.1, bf16[1,512,768]{2,1,0:T(8,128)(2,1)} %cotangent.1, s32[1,512]{1,0:T(1,128)} %padding.1, s32[1,512]{1,0:T(1,128)} %opening.1, ...), custom_call_target="tpu_custom_call" | custom-call | tf_op jit(solution)/shard_map/pallas_call | solution.py:1208
  155.3 0.0 copy-start.1
  155.4 2.3 %copy.31 = bf16[8,64,768]{2,1,0:T(8,128)(2,1)} copy(bf16[8,64,768]{2,0,1:T(8,128)(2,1)} %bitcast.20) | data formatting | bytes 1572864 | tf_op jit(solution)/shard_map/transpose | solution.py:161
  157.6 0.0 copy-done.1
  157.6 0.0 copy-start.10
  157.6 0.0 copy-start
  157.6 0.0 copy-start.3
  157.6 0.0 copy-start.4
  157.6 0.0 copy-start.5
  157.7 1.6 copy.32
  160.0 0.0 copy-done.10
  160.0 0.5 slice.16
  160.6 0.0 copy-done
  160.6 0.0 copy-done.3
  160.6 0.0 copy-done.4
  160.6 0.0 copy-done.5
  160.6 0.0 copy-start.2
  160.6 0.0 copy-start.6
  160.6 0.0 copy-start.7
  160.6 0.0 copy-start.8
  160.6 2.1 %fusion.6 = (bf16[24,4992]{1,0:T(8,128)(2,1)}, f32[24,4992]{1,0:T(8,128)}, f32[24,4992]{1,0:T(8,128)}, f32[24,4992]{1,0:T(8,128)}, f32[24,4992]{1,0:T(8,128)}) fusion(f32[24,4992]{1,0:T(8,128)S(1)} %copy-done, f32[]{:T(128)} %bitcast.9, f32[]{:T(128)} %bitcast.8, f32[24,4992]{1,0:T(8,128)S(1)} %copy-done.3, f32[24,4992]{1,0:T(8,128)S(1)} %copy-done.4, ...), kind=kLoop, calls=%fused_computation.17 | loop fusion | flops 2036736 | bytes 4073484 | tf_op jit(solution)/shard_map/convert_element_type | solution.py:1372
  162.8 0.0 copy-start.9
  162.8 0.0 copy-start.11
  162.8 0.0 copy-start.12
  162.8 0.0 copy-done.2
  162.8 0.0 copy-done.6
  162.8 0.0 copy-done.7
  162.8 0.0 copy-done.8
  162.8 1.6 fusion.4
  164.5 1.2 fusion.8
  165.7 0.6 slice_divide_fusion
  166.3 0.6 slice_bitcast_fusion
  166.9 0.0 copy-done.9
  166.9 0.0 copy-done.11
  166.9 0.0 copy-done.12
  166.9 1.3 add_multiply_fusion
  (1 shorter events, 0.0 us)
Async XLA Ops:
  155.3 2.3 %copy-start.1 = (f32[512,768]{1,0:T(8,128)S(1)}, f32[512,768]{1,0:T(8,128)}, u32[]{:S(2)}) copy-start(f32[512,768]{1,0:T(8,128)} %get-tuple-element.23) | copy-start | bytes 4718596
  157.6 2.4 %copy-start.10 = (f32[4,24,128]{2,1,0:T(8,128)S(1)}, f32[4,24,128]{2,1,0:T(8,128)}, u32[]{:S(2)}) copy-start(f32[4,24,128]{2,1,0:T(8,128)} %get-tuple-element.25) | copy-start | bytes 147460
  157.6 3.0 %copy-start = (f32[24,4992]{1,0:T(8,128)S(1)}, f32[24,4992]{1,0:T(8,128)}, u32[]{:S(2)}) copy-start(f32[24,4992]{1,0:T(8,128)} %w_in.1) | copy-start | bytes 1437700
  157.6 3.0 %copy-start.3 = (f32[24,4992]{1,0:T(8,128)S(1)}, f32[24,4992]{1,0:T(8,128)}, u32[]{:S(2)}) copy-start(f32[24,4992]{1,0:T(8,128)} %param.22) | copy-start | bytes 1437700
  157.6 3.0 %copy-start.4 = (f32[24,4992]{1,0:T(8,128)S(1)}, f32[24,4992]{1,0:T(8,128)}, u32[]{:S(2)}) copy-start(f32[24,4992]{1,0:T(8,128)} %param.21) | copy-start | bytes 1437700
  157.6 2.9 %copy-start.5 = (f32[24,4992]{1,0:T(8,128)S(1)}, f32[24,4992]{1,0:T(8,128)}, u32[]{:S(2)}) copy-start(f32[24,4992]{1,0:T(8,128)} %get-tuple-element.24) | copy-start | bytes 1437700
  160.6 2.2 %copy-start.2 = (f32[72,768]{1,0:T(8,128)S(1)}, f32[72,768]{1,0:T(8,128)}, u32[]{:S(2)}) copy-start(f32[72,768]{1,0:T(8,128)} %w_out.1) | copy-start | bytes 663556
  160.6 2.2 %copy-start.6 = (f32[72,768]{1,0:T(8,128)S(1)}, f32[72,768]{1,0:T(8,128)}, u32[]{:S(2)}) copy-start(f32[72,768]{1,0:T(8,128)} %param.24) | copy-start | bytes 663556
  160.6 2.2 %copy-start.7 = (f32[72,768]{1,0:T(8,128)S(1)}, f32[72,768]{1,0:T(8,128)}, u32[]{:S(2)}) copy-start(f32[72,768]{1,0:T(8,128)} %param.23) | copy-start | bytes 663556
  160.6 2.2 %copy-start.8 = (f32[72,768]{1,0:T(8,128)S(1)}, f32[72,768]{1,0:T(8,128)}, u32[]{:S(2)}) copy-start(f32[72,768]{1,0:T(8,128)} %get-tuple-element.26) | copy-start | bytes 663556
  162.8 4.1 %copy-start.9 = (f32[2304]{0:T(1024)S(1)}, f32[2304]{0:T(1024)}, u32[]{:S(2)}) copy-start(f32[2304]{0:T(1024)} %param.20) | copy-start | bytes 27652
  162.8 4.1 %copy-start.11 = (f32[2304]{0:T(1024)S(1)}, f32[2304]{0:T(1024)}, u32[]{:S(2)}) copy-start(f32[2304]{0:T(1024)} %param.26) | copy-start | bytes 27652
  162.8 4.1 %copy-start.12 = (f32[2304]{0:T(1024)S(1)}, f32[2304]{0:T(1024)}, u32[]{:S(2)}) copy-start(f32[2304]{0:T(1024)} %param.25) | copy-start | bytes 27652

commit v4 on v3

--- a/solution.py
+++ b/solution.py
@@ -225,11 +225,12 @@
 IN_ROWS = 24
 OUT_ROWS = 72
 MIX = CH + 2 * D
-MIX_HALF = 1024
 CHUNK = 512
 CHUNKS = FF // CHUNK
 OUT = 2
 TILE = 128
+OUTS = D // 2 // TILE
+GLU = OUT + OUTS
 VMEM_BYTES = 63 * 1024 * 1024
 SLOTS = 512
 ROWS = 64
@@ -246,13 +247,12 @@
 
 
 def piece_list():
-    half = MIX_HALF // 2
-    second = MIX - MIX_HALF
+    drive = (CH + D) // 2 + TILE // 2
     mix = [
-        Piece("in", IN_ROWS, half, (0, second), TILE),
-        Piece("in", IN_ROWS, half, (half, second + half)),
+        Piece("in", IN_ROWS, drive, (0, CH + D - drive), TILE),
+        Piece("in", IN_ROWS, D // 2, (CH + D, MIX - D // 2)),
     ]
-    out = [Piece("out", OUT_ROWS, D // 2, (0, D // 2))]
+    out = [Piece("out", OUT_ROWS, TILE, (TILE * k, D // 2 + TILE * k)) for k in range(OUTS)]
     glu = [
         Piece("in", IN_ROWS, CHUNK, (MIX + CHUNK * k, MIX + FF + CHUNK * k)) for k in range(CHUNKS)
     ]
@@ -327,6 +327,8 @@
 
 GATHER_SEMS = 4 * 2
 STEPS_AWAY = (1, 3, 2)
+GATHER_NEAR_FIRST = (GLU + 1, GLU + 2)
+REDUCE_NEAR_LAST = (GLU, GLU + 1)
 
 
 class Gather:
@@ -369,12 +371,15 @@
             self.part(p, self.place.core), self.own_rows(p), self.local.at[p]
         )
 
-    def along_z(self, p, z, target):
+    def along_z(self, p, z, target, core):
         place = self.place
-        block = self.buffers[p].at[place.core, z, place.x, place.y]
-        return remote(
-            block, block, self.sems[0].at[p, target], self.sems[1].at[p, z], place.plane(target)
-        )
+        near, far = place.sides(core)
+        if p in GATHER_NEAR_FIRST:
+            part = pair_of(self.buffers[p], core, z, far)
+        else:
+            part = block_of(self.buffers[p], core, z, near, far)
+        sems = self.sems[0].at[p, target], self.sems[1].at[p, z]
+        return remote(part, part, *sems, place.plane(target))
 
     def along_near(self, p, z, core):
         block = block_of(self.buffers[p], core, z, *self.place.sides(core))
@@ -399,32 +404,59 @@
             self.to_sibling(p).start()
             self.to_self(p).start()
 
-    def stage0(self, p):
+
+    def near_own(self, p):
         place = self.place
         self.to_self(p).wait()
         self.to_sibling(p).wait_recv()
         self.buffers[p][place.core, place.z, place.x, place.y] = self.staging[p][...].astype(LOW)
-        for step in STEPS_AWAY:
-            self.along_z(p, place.z, place.turn(step)).start()
         place.by_core(lambda core: self.along_near(p, place.z, core).start())
 
-    def stage1(self, p):
+    def z_own(self, p):
         place = self.place
-        for step in STEPS_AWAY:
-            z = place.turn(step)
-            self.along_z(p, z, place.z).wait_recv()
-            place.by_core(lambda core: self.along_near(p, z, core).start())
-
-    def stage2(self, p):
+
         def run(core):
-            for step in (0,) + STEPS_AWAY:
-                z = self.place.turn(step)
-                self.along_near(p, z, core).wait_recv()
+            for step in STEPS_AWAY:
+                self.along_z(p, place.z, place.turn(step), core).start()
+
+        place.by_core(run)
+
+    def far_own(self, p):
+        place = self.place
+
+        def run(core):
+            self.along_near(p, place.z, core).wait_recv()
+            self.along_far(p, place.z, core).start()
+
+        place.by_core(run)
+
+    def near(self, p):
+        place = self.place
+
+        def run(core):
+            for step in STEPS_AWAY:
+                z = place.turn(step)
+                self.along_z(p, z, place.z, core).wait_recv()
+                self.along_near(p, z, core).start()
+
+        if p not in GATHER_NEAR_FIRST:
+            place.by_core(run)
+
+    def far(self, p):
+        place = self.place
+
+        def run(core):
+            for step in STEPS_AWAY:
+                z = place.turn(step)
+                if p in GATHER_NEAR_FIRST:
+                    self.along_z(p, z, place.z, core).wait_recv()
+                else:
+                    self.along_near(p, z, core).wait_recv()
                 self.along_far(p, z, core).start()
 
-        self.place.by_core(run)
-
-    def stage3(self, p):
+        place.by_core(run)
+
+    def chip(self, p):
         def run(core):
             for step in (0,) + STEPS_AWAY:
                 z = self.place.turn(step)
@@ -433,19 +465,21 @@
 
         self.place.by_core(run)
 
-    def stage4(self, p):
+    def arrive(self, p):
         for step in (0,) + STEPS_AWAY:
             z = self.place.turn(step)
             self.in_chip(p, z, 1 - self.place.core).wait_recv()
 
     def drain(self, p):
         self.to_sibling(p).wait_send()
-        for step in STEPS_AWAY:
-            self.along_z(p, self.place.z, self.place.turn(step)).wait_send()
 
         def run(core):
-            for z in range(PLANES):
-                self.along_near(p, z, core).wait_send()
+            for step in (0,) + STEPS_AWAY:
+                z = self.place.turn(step)
+                if step:
+                    self.along_z(p, self.place.z, z, core).wait_send()
+                if p not in GATHER_NEAR_FIRST or step == 0:
+                    self.along_near(p, z, core).wait_send()
                 self.along_far(p, z, core).wait_send()
                 self.in_chip(p, z, core).wait_send()
 
@@ -458,7 +492,7 @@
     def __init__(self, place, grads, refs, results):
         n = len(PIECES)
         self.place, self.grads, self.results = place, grads, results
-        self.far, self.near, self.planes, self.final = (refs[k * n : (k + 1) * n] for k in range(4))
+        self.far_got, self.near_got, self.planes, self.final = (refs[k * n : (k + 1) * n] for k in range(4))
         self.sems = refs[4 * n :]
 
     @staticmethod
@@ -468,7 +502,11 @@
         blocks = [p.shape()[4:] for p in PIECES]
         return (
             [pltpu.VMEM((PLANES, SIDE) + s, LOW) for s in blocks]
-            + [pltpu.VMEM((PLANES,) + s, LOW) for s in blocks] * 2
+            + [pltpu.VMEM((PLANES,) + s, LOW) for s in blocks]
+            + [
+                pltpu.VMEM((PLANES,) + (SIDE,) * (p in REDUCE_NEAR_LAST) + s, LOW)
+                for p, s in enumerate(blocks)
+            ]
             + [pltpu.VMEM(s, WIDE) for s in blocks]
             + [dma((n, PLANES))] * 6
             + [dma((n,))] * 2
@@ -483,7 +521,7 @@
     def along_far(self, p, z, core):
         return remote(
             self.pair(p, z, 1 - self.place.sides(core)[1], core),
-            self.far[p].at[z],
+            self.far_got[p].at[z],
             self.sems[0].at[p, z],
             self.sems[1].at[p, z],
             self.place.far(core),
@@ -493,20 +531,20 @@
         near, far = self.place.sides(core)
         return remote(
             self.block(p, z, 1 - near, far, core),
-            self.near[p].at[z],
+            self.near_got[p].at[z],
             self.sems[2].at[p, z],
             self.sems[3].at[p, z],
             self.place.near(core),
         )
 
     def along_z(self, p, z, sender, core):
-        return remote(
-            self.block(p, z, *self.place.sides(core), core),
-            self.planes[p].at[sender],
-            self.sems[4].at[p, z],
-            self.sems[5].at[p, sender],
-            self.place.plane(z),
-        )
+        near, far = self.place.sides(core)
+        if p in REDUCE_NEAR_LAST:
+            part = self.pair(p, z, far, core)
+        else:
+            part = self.block(p, z, near, far, core)
+        sems = self.sems[4].at[p, z], self.sems[5].at[p, sender]
+        return remote(part, self.planes[p].at[sender], *sems, self.place.plane(z))
 
     def result(self, p, core):
         piece = PIECES[p]
@@ -529,50 +567,72 @@
     def add(target, source):
         target[...] = (target[...].astype(WIDE) + source[...].astype(WIDE)).astype(LOW)
 
-    def stage0(self, p):
+    def far(self, p):
         def run(core):
             for step in self.ORDER:
                 self.along_far(p, self.place.turn(step), core).start()
 
         self.place.by_core(run)
 
-    def stage1(self, p):
+    def after_far(self, p):
         def run(core):
             for step in self.ORDER:
                 z = self.place.turn(step)
                 self.along_far(p, z, core).wait_recv()
-                self.add(self.pair(p, z, self.place.sides(core)[1], core), self.far[p].at[z])
-                self.along_near(p, z, core).start()
+                self.add(self.pair(p, z, self.place.sides(core)[1], core), self.far_got[p].at[z])
+                if p not in REDUCE_NEAR_LAST:
+                    self.along_near(p, z, core).start()
+                elif step:
+                    self.along_z(p, z, self.place.z, core).start()
 
         self.place.by_core(run)
 
-    def stage2(self, p):
+    def after_near(self, p):
+        place = self.place
+
         def run(core):
+            near, far = place.sides(core)
+            if p in REDUCE_NEAR_LAST:
+                self.along_z_waits(p, core)
+                total = self.pair(p, place.z, far, core)[...].astype(WIDE)
+                for step in STEPS_AWAY:
+                    total = total + self.planes[p][place.turn(step)].astype(WIDE)
+                self.pair(p, place.z, far, core)[...] = total.astype(LOW)
+                self.along_near(p, place.z, core).start()
+                return
             for step in self.ORDER:
-                z = self.place.turn(step)
+                z = place.turn(step)
                 self.along_near(p, z, core).wait_recv()
-                self.add(self.block(p, z, *self.place.sides(core), core), self.near[p].at[z])
+                self.add(self.block(p, z, near, far, core), self.near_got[p].at[z])
                 if step:
-                    self.along_z(p, z, self.place.z, core).start()
-
-        self.place.by_core(run)
-
-    def stage3(self, p):
-        rows = PIECES[p].rows
+                    self.along_z(p, z, place.z, core).start()
+
+        place.by_core(run)
+
+    def along_z_waits(self, p, core):
+        for step in STEPS_AWAY:
+            self.along_z(p, self.place.z, self.place.turn(step), core).wait_recv()
+
+    def finish(self, p):
+        rows, place = PIECES[p].rows, self.place
 
         def run(core):
-            z = self.place.z
-            for step in STEPS_AWAY:
-                self.along_z(p, z, self.place.turn(step), core).wait_recv()
-            total = self.block(p, z, *self.place.sides(core), core)[...].astype(WIDE)
-            for step in STEPS_AWAY:
-                total = total + self.planes[p][self.place.turn(step)].astype(WIDE)
+            near, far = place.sides(core)
+            if p in REDUCE_NEAR_LAST:
+                self.along_near(p, place.z, core).wait_recv()
+                others = [self.near_got[p].at[place.z]]
+            else:
+                self.along_z_waits(p, core)
+                others = [self.planes[p].at[place.turn(step)] for step in STEPS_AWAY]
+            total = self.block(p, place.z, near, far, core)[...].astype(WIDE)
+            for other in others:
+                total = total + other[...].astype(WIDE)
             self.final[p][...] = total
             self.to_sibling(p, core).start()
             target, columns = self.result(p, core)
             target[...] = self.final[p][pl.ds(rows * core, rows), columns]
 
-        self.place.by_core(run)
+        place.by_core(run)
 
     def drain(self, p):
         def run(core):
@@ -581,7 +641,8 @@
             for step in self.ORDER:
                 z = self.place.turn(step)
                 self.along_far(p, z, core).wait_send()
-                self.along_near(p, z, core).wait_send()
+                if p not in REDUCE_NEAR_LAST or step == 0:
+                    self.along_near(p, z, core).wait_send()
                 if step:
                     self.along_z(p, z, self.place.z, core).wait_send()
 
@@ -652,8 +713,10 @@
         d_glu_got=vmem((CHUNKS, SLOTS, CHUNK), LOW),
         d_out=vmem((2, SLOTS, D // 2), LOW),
         d_out_got=vmem((SLOTS, D // 2), LOW),
-        d_mix=vmem((2, 2, SLOTS, MIX_HALF // 2), LOW),
-        d_mix_got=vmem((2, SLOTS, MIX_HALF // 2), LOW),
+        d_drive=vmem((2, SLOTS, PIECES[0].columns), LOW),
+        d_drive_got=vmem((SLOTS, PIECES[0].columns), LOW),
+        d_gate=vmem((2, SLOTS, PIECES[1].columns), LOW),
+        d_gate_got=vmem((SLOTS, PIECES[1].columns), LOW),
         pre_mix=vmem((SLOTS, MIX), WIDE),
         glu=vmem((3, SLOTS // 2, CHUNK), WIDE),
         retain=vmem((SLOTS, CH), WIDE),
@@ -698,12 +761,12 @@
             gated=(self.gated.at[own], self.gated.at[got]),
             upstream=(self.upstream.at[other], self.upstream_got),
             d_out=(self.d_out.at[other], self.d_out_got),
+            d_drive=(self.d_drive.at[other], self.d_drive_got),
+            d_gate=(self.d_gate.at[other], self.d_gate_got),
         )
         for k in range(CHUNKS):
             pairs["hidden", k] = (self.hidden.at[k, own], self.hidden.at[k, got])
             pairs["d_glu", k] = (self.d_glu.at[k, other], self.d_glu_got.at[k])
-        for m in range(2):
-            pairs["d_mix", m] = (self.d_mix.at[other, m], self.d_mix_got.at[m])
         return pairs
 
     def swap(self, name):
@@ -726,21 +789,21 @@
 
 
     def mix_weight(self, half, m):
-        return self.weights[m][half].reshape(D, MIX_HALF // 2)
+        return self.weights[m][half].reshape(D, PIECES[m].columns)
 
     def glu_weight(self, k):
-        parts = [self.weights[OUT + 1 + k][half].reshape(D, CHUNK) for half in range(2)]
+        parts = [self.weights[GLU + k][half].reshape(D, CHUNK) for half in range(2)]
         return jnp.concatenate(parts, axis=1)
 
     def out_weight(self, start, count):
-        halves = []
+        columns = []
         for half in range(2):
-            ref = self.weights[OUT]
-            parts = [
-                ref[half, z, x, y, first:last] for z, x, y, first, last in out_segments(start, count)
-            ]
-            halves.append(jnp.concatenate(parts, axis=0))
-        return jnp.concatenate(halves, axis=1)
+            for p in range(OUT, GLU):
+                ref = self.weights[p]
+                runs = out_segments(start, count)
+                parts = [ref[half, z, x, y, first:last] for z, x, y, first, last in runs]
+                columns.append(jnp.concatenate(parts, axis=0))
+        return jnp.concatenate(columns, axis=1)
 
     def put_in(self, p, value):
         self.grads[p][...] = value.astype(LOW).reshape(self.grads[p].shape)
@@ -749,7 +812,9 @@
         value, done = value.astype(LOW), 0
         for z, x, y, first, last in out_segments(start, value.shape[0]):
             count = last - first
-            self.grads[OUT][z, x, y, first:last] = value[done : done + count]
+            for k in range(OUTS):
+                part = value[done : done + count, k * TILE : (k + 1) * TILE]
+                self.grads[OUT + k][z, x, y, first:last] = part
             done += count
 
 
@@ -790,13 +855,12 @@
         self.upstream[1] = striped[:, D // 2 :].astype(LOW)
 
     def mix(self, m):
-        normed, width = self.normed[0:SLOTS, :], MIX_HALF // 2
-        piece = PIECES[m]
+        normed, piece = self.normed[0:SLOTS, :], PIECES[m]
         for half in range(2):
             skip = piece.overlap * half
             start = piece.starts[half] + skip
             product = inner(normed, self.mix_weight(half, m))
-            self.pre_mix[:, start : start + width - skip] = product[:, skip:]
+            self.pre_mix[:, start : start + piece.columns - skip] = product[:, skip:]
 
     def drives(self):
         def run(rows):
@@ -916,7 +980,7 @@
 
     def glu_grads(self, k):
         d_glu = jnp.concatenate([self.d_glu[k, self.place.core], self.d_glu_got[k]], axis=0)
-        self.put_in(OUT + 1 + k, along(self.normed_two[...], d_glu))
+        self.put_in(GLU + k, along(self.normed_two[...], d_glu))
         upstream = self.own_half(self.upstream, self.upstream_got[...])
         self.put_out(D + CHUNK * k, along(self.hidden[k], upstream))
 
@@ -949,8 +1013,8 @@
             self.drive[rows, :] = (d_live * (pre * logistic)).astype(LOW).astype(WIDE)
             slope = logistic * (1.0 + pre * (1.0 - logistic))
             d_gate = (d_live * self.recurrent(rows) * slope).astype(LOW)
-            self.d_mix[1, 0, rows, 2 * TILE :] = d_gate[:, : 2 * TILE]
-            self.d_mix[1, 1, rows, :] = d_gate[:, 2 * TILE :]
+            self.d_gate[0, rows, :] = d_gate[:, : D // 2]
+            self.d_gate[1, rows, :] = d_gate[:, D // 2 :]
 
         each_block(run)
 
@@ -990,26 +1054,26 @@
             slope = logistic * (1.0 + pre * (1.0 - logistic))
             d_driver = d_input * jnp.concatenate([forget, forget], axis=1) * slope
             d_pre = jnp.concatenate([d_first, d_driver], axis=1).astype(LOW)
-            half = MIX_HALF // 2
-            self.d_mix[0, 0, rows, :] = d_pre[:, :half]
-            self.d_mix[0, 1, rows, :] = d_pre[:, half : 2 * half]
-            self.d_mix[1, 0, rows, : 2 * TILE] = d_pre[:, MIX_HALF - TILE :]
+            piece = PIECES[0]
+            for half, start in enumerate(piece.starts):
+                self.d_drive[half, rows, :] = d_pre[:, start : start + piece.columns]
 
         each_block(run)
 
     def mix_grads(self, m):
-        d_mix = jnp.concatenate([self.d_mix[self.place.core, m], self.d_mix_got[m]], axis=0)
-        self.put_in(m, along(self.normed[...], d_mix))
+        own, got = ((self.d_drive, self.d_drive_got), (self.d_gate, self.d_gate_got))[m]
+        self.put_in(m, along(self.normed[...], self.own_half(own, got[...])))
+
+    def gate_normed(self):
+        left = jnp.concatenate([self.d_gate[0], self.d_gate[1]], axis=1)
+        right = jnp.concatenate([self.mix_weight(0, 1), self.mix_weight(1, 1)], axis=1)
+        self.d_normed[...] = across(left, right)
 
     def first_back(self):
-        lefts, rights = [], []
-        for half in range(2):
-            for m in range(2):
-                skip = PIECES[m].overlap * half
-                lefts.append(self.d_mix[half, m][:, skip:])
-                rights.append(self.mix_weight(half, m)[:, skip:])
-        product = across(jnp.concatenate(lefts, axis=1), jnp.concatenate(rights, axis=1))
-        self.d_normed[...] = product
+        skip = PIECES[0].overlap
+        left = jnp.concatenate([self.d_drive[0], self.d_drive[1][:, skip:]], axis=1)
+        right = jnp.concatenate([self.mix_weight(0, 0), self.mix_weight(1, 0)[:, skip:]], axis=1)
+        self.d_normed[...] += across(left, right)
 
         def run(rows):
             values, d_normed = self.tokens[rows, :].astype(WIDE), self.d_normed[rows, :]
@@ -1020,6 +1084,18 @@
             self.middle[rows, :] += scaling * scaled - values * (scaling**3 * mean)
 
         each_block(run)
+
+    def natural_out(self):
+        self.block_out[...] = along(self.perm[...], self.block_out[...]).astype(LOW)
+
+    def natural_tokens(self):
+        rest = self.middle[...]
+        total = jnp.zeros_like(rest)
+        for _ in range(3):
+            part = rest.astype(LOW)
+            total = total + along(self.perm[...], part)
+            rest = rest - part.astype(WIDE)
+        self.d_normed[...] = total
 
 
     def gather_vector(self):
@@ -1091,92 +1167,138 @@
     gather.begin()
     loads[0].wait()
     block.first_norm(raw_tokens)
+
+    out = range(OUT, GLU)
+    for p in (0, 1):
+        gather.near_own(p)
+        gather.z_own(p)
+    for p in range(2, n):
+        gather.near_own(p)
     loads[1].wait()
     block.mask_upstream(raw_upstream)
     block.give("normed", "upstream")
-
-    stages = (gather.stage0, gather.stage1, gather.stage2, gather.stage3, gather.stage4)
-
-    def tick(now):
-        for lag, stage in enumerate(stages):
-            if 0 <= now - lag < n:
-                stage(now - lag)
-
-    for now in range(5):
-        tick(now)
+    gather.far_own(0)
+    gather.far_own(1)
+    gather.near(0)
+    gather.z_own(2)
+    gather.far_own(2)
+    gather.far(0)
+    gather.near(1)
+    gather.z_own(3)
+    gather.far_own(3)
+    gather.chip(0)
+    gather.far(1)
+    gather.near(2)
+    gather.z_own(4)
+    gather.far_own(4)
+    gather.arrive(0)
     block.mix(0)
-    tick(5)
-    block.mix(1)
     block.drives()
     block.scan_own(0)
-    tick(6)
+    gather.chip(1)
+    gather.far(2)
+    gather.near(3)
+    gather.z_own(5)
+    gather.far_own(5)
+    gather.arrive(1)
+    block.mix(1)
+    gather.chip(2)
+    gather.far(3)
+    gather.near(4)
+    gather.far_own(6)
+    gather.z_own(6)
     block.scan_states()
     block.gate_rows()
     block.give("gated")
+    gather.chip(3)
+    gather.far(4)
+    gather.near(5)
+    gather.far_own(7)
+    gather.z_own(7)
+    gather.chip(4)
+    gather.far(5)
+    for p in out:
+        gather.arrive(p)
     block.second_norm()
     block.give("normed_two")
-    block.take("upstream", "normed_two")
-
-    def glu(k):
+    gather.chip(5)
+    gather.far(6)
+
+    def glu_chunk(k, beside):
+        gather.arrive(GLU + k)
         block.glu_forward(k)
         block.give(("hidden", k), ("d_glu", k))
+        for run, p in beside:
+            run(p)
         block.glu_back(k)
+        if k == 0:
+            block.take("upstream", "normed_two")
         block.take(("hidden", k), ("d_glu", k))
         block.glu_grads(k)
-        reduce.stage0(OUT + 1 + k)
-
-    tick(7)
-    glu(0)
-    tick(8)
-    reduce.stage1(OUT + 1)
-    glu(1)
-    tick(9)
-    reduce.stage2(OUT + 1)
-    reduce.stage1(OUT + 2)
-    glu(2)
+
+    glu_chunk(0, ((gather.chip, 6), (gather.far, 7)))
+    reduce.far(GLU)
+    glu_chunk(1, ((gather.chip, 7),))
+    reduce.far(GLU + 1)
+    glu_chunk(2, ((reduce.after_far, GLU),))
+    block.middle_back()
+    block.give("d_out")
+    block.gate_back()
+    block.scan_own(1)
+    reduce.far(GLU + 2)
+    block.give("d_gate")
+    block.take("gated", "d_out")
+    block.mixer_out_grad()
+    reduce.after_far(GLU + 1)
+    for p in out:
+        reduce.far(p)
+    block.take("normed", "d_gate")
+    block.mix_grads(1)
+    reduce.far(1)
+    block.gate_normed()
+    reduce.after_near(GLU)
+    reduce.after_far(GLU + 2)
+    block.scan_back()
+    block.drives_back()
+    block.give("d_drive")
+    reduce.after_far(OUT)
+    reduce.after_near(GLU + 1)
+    block.take("d_drive")
+    block.mix_grads(0)
+    reduce.far(0)
+    block.natural_out()
     leave_out = pltpu.make_async_copy(block.block_out, block_out, block.departures.at[0])
     leave_out.start()
-    block.middle_back()
-    block.give("d_out")
-    reduce.stage3(OUT + 1)
-    reduce.stage2(OUT + 2)
-    reduce.stage1(OUT + 3)
-    block.gate_back()
-    block.scan_own(1)
-    block.take("gated", "d_out")
-    block.mixer_out_grad()
-    reduce.stage0(OUT)
-    block.scan_back()
-    reduce.stage3(OUT + 2)
-    reduce.stage2(OUT + 3)
-    block.drives_back()
-    block.give(("d_mix", 0), ("d_mix", 1))
-    reduce.stage1(OUT)
-    block.take("normed", ("d_mix", 0), ("d_mix", 1))
-    block.mix_grads(0)
-    reduce.stage0(0)
-    block.mix_grads(1)
-    reduce.stage0(1)
-    reduce.stage3(OUT + 3)
+    reduce.after_far(OUT + 1)
+    reduce.after_near(GLU + 2)
+    reduce.finish(GLU)
     block.first_back()
-    leave_tokens = pltpu.make_async_copy(block.middle, d_tokens, block.departures.at[1])
-    leave_tokens.start()
+    reduce.after_far(OUT + 2)
+    reduce.after_near(OUT)
     block.gather_vector()
     block.vector_step(0)
-    reduce.stage2(OUT)
-    reduce.stage1(0)
+    block.natural_tokens()
+    leave_tokens = pltpu.make_async_copy(block.d_normed, d_tokens, block.departures.at[1])
+    leave_tokens.start()
+    reduce.after_far(1)
+    reduce.after_near(OUT + 1)
     block.vector_step(1)
-    reduce.stage1(1)
-    reduce.stage3(OUT)
+    reduce.finish(GLU + 1)
+    reduce.after_near(OUT + 2)
+    reduce.after_far(0)
+    reduce.finish(GLU + 2)
+    reduce.after_near(1)
     block.vector_step(2)
-    reduce.stage2(0)
-    reduce.stage2(1)
+    reduce.finish(OUT)
+    reduce.after_near(0)
     block.vector_step(3)
     for step in (1, 2, 3):
         block.vector_plane(planes, step, place.z).start()
     planes[place.z] = block.vector[3]
-    reduce.stage3(0)
-    reduce.stage3(1)
+    reduce.finish(OUT + 1)
+    reduce.finish(OUT + 2)
+    reduce.finish(1)
+    reduce.finish(0)
 
     for step in (1, 2, 3):
         block.vector_plane(planes, step, place.z).wait_send()
@@ -1218,8 +1340,78 @@
             collective_id=0, has_side_effects=True, vmem_limit_bytes=VMEM_BYTES
         ),
     )(tokens, cotangent, padding, opening, w_in, w_out, vectors.reshape(VEC_COUNT, TILE))
-    sums = jnp.sum(planes, axis=0)
-    return block_out, d_tokens, sum_in, sum_out, sums[:VEC_COUNT].reshape(-1), sums[VEC_COUNT, 0]
+    return block_out, d_tokens, sum_in, sum_out, planes
+
+
+def power(base, count):
+    return lax.fori_loop(0, count, lambda _, value: value * base, jnp.float32(1.0))
+
+
+def update_kernel(counter, planes, block_from, tokens_from, *refs):
+    ins, outs = refs[:11], refs[11:]
+    outs[0][...] = block_from[...]
+    outs[1][...] = tokens_from[...]
+    first_scale = 1.0 - power(BETA_ONE, counter[0])
+    second_scale = 1.0 - power(BETA_TWO, counter[0])
+    vectors = (planes[0] + planes[1]) + (planes[2] + planes[3])
+    total = vectors[VEC_COUNT : VEC_COUNT + 1, 0:1]
+
+    def step(summed, master, first, second, decay):
+        gradient = summed / total
+        first = BETA_ONE * first + (1.0 - BETA_ONE) * gradient
+        second = BETA_TWO * second + (1.0 - BETA_TWO) * gradient * gradient
+        corrected = first / first_scale / (jnp.sqrt(second / second_scale) + ADAM_EPSILON)
+        return gradient, -LEARN_RATE * (corrected + decay * master), first, second
+
+    for k in range(2):
+        summed, master, first, second = (ref[...] for ref in ins[4 * k : 4 * k + 4])
+        gradient, change, first, second = step(summed, master, first, second, WEIGHT_DECAY)
+        new = master + change
+        results = (gradient, new, first, second, new.astype(LOW))
+        for ref, value in zip(outs[2 + 5 * k : 7 + 5 * k], results, strict=True):
+            ref[...] = value
+    master, first, second = (ref[...] for ref in ins[8:])
+    results = step(vectors[:VEC_COUNT], master, first, second, 0.0)
+    for ref, value in zip(outs[12:], results, strict=True):
+        ref[...] = value
+
+
+UPDATE_BLOCKS = 3
+
+
+def update(counter, planes, block_out, d_tokens, sums, masters, moments, vector_state):
+    shapes = [x.shape for x in sums]
+
+    def by_columns(shape):
+        return pl.BlockSpec((shape[0], shape[1] // UPDATE_BLOCKS), lambda i: (0, i))
+
+    def whole(shape):
+        return pl.BlockSpec(shape, lambda i: (0,) * len(shape))
+
+    vector = whole((VEC_COUNT, TILE))
+    columns = [by_columns(shape) for shape in shapes]
+    types = (WIDE, WIDE, WIDE, WIDE, LOW)
+    out_shape = [
+        jax.ShapeDtypeStruct(block_out.shape, block_out.dtype),
+        jax.ShapeDtypeStruct(d_tokens.shape, d_tokens.dtype),
+    ]
+    out_shape += [jax.ShapeDtypeStruct(shape, kind) for shape in shapes for kind in types]
+    out_shape += [jax.ShapeDtypeStruct((VEC_COUNT, TILE), WIDE)] * 4
+    operands = []
+    for k in range(2):
+        operands += [sums[k], masters[k], *moments[k]]
+    return pl.pallas_call(
+        update_kernel,
+        grid=(UPDATE_BLOCKS,),
+        out_shape=out_shape,
+        in_specs=[pl.BlockSpec(memory_space=pltpu.SMEM), whole(planes.shape)]
+        + [by_columns(block_out.shape)] * 2
+        + [columns[0]] * 4
+        + [columns[1]] * 4
+        + [vector] * 3,
+        out_specs=[by_columns(block_out.shape)] * 2 + [columns[0]] * 5 + [columns[1]] * 5 + [vector] * 4,
+        compiler_params=pltpu.CompilerParams(vmem_limit_bytes=VMEM_BYTES),
+    )(counter, planes, block_out, d_tokens, *operands, *vector_state)
 
 
 def routed(tokens, w_in, w_out):
@@ -1326,7 +1518,7 @@
     summed_in = lax.psum_scatter(grad_in_all, axes, scatter_dimension=0, tiled=True)
     summed_out = lax.psum_scatter(grad_out_all, axes, scatter_dimension=0, tiled=True)
     summed_vec, total = lax.psum((grad_vectors, jnp.sum(filled)), axes)
-    return block_out.astype(low), d_tokens, summed_in, summed_out, summed_vec, total
+    return unstripe(block_out.astype(low)), unstripe(d_tokens), summed_in, summed_out, summed_vec, total
 
 
 def body(
@@ -1345,8 +1537,29 @@
     v_vec,
     counter,
 ):
-    run = block_routed if routed(tokens, w_in, w_out) else block_anywhere
-    block_out, d_tokens, summed_in, summed_out, summed_vec, total = run(
+    if routed(tokens, w_in, w_out):
+        block_out, d_tokens, sum_in, sum_out, planes = block_routed(
+            tokens, cotangent, padding, opening, w_in, w_out, vectors
+        )
+        sums, masters = (sum_in, sum_out), (w_in, w_out)
+        moments = ((m_in, v_in), (m_out, v_out))
+        lines = [x.reshape(VEC_COUNT, TILE) for x in (vectors, m_vec, v_vec)]
+        results = update(
+            counter, planes, block_out, d_tokens, sums, masters, moments, lines
+        )
+        block_out, d_tokens = results[:2]
+        grad_vec, update_vec, first_vec, second_vec = (x.reshape(-1) for x in results[12:])
+        return (
+            block_out[None],
+            d_tokens[None],
+            *results[2:12],
+            grad_vec,
+            grad_vec[2 * D + CH :],
+            update_vec,
+            first_vec,
+            second_vec,
+        )
+    block_out, d_tokens, summed_in, summed_out, summed_vec, total = block_anywhere(
         tokens, cotangent, padding, opening, w_in, w_out, vectors
     )
     steps = counter[0].astype(jnp.float32)
@@ -1363,8 +1576,8 @@
         vectors, grad_vec, m_vec, v_vec, steps, 0.0
     )
     return (
-        unstripe(block_out)[None],
-        unstripe(d_tokens)[None],
+        block_out[None],
+        d_tokens[None],
         grad_in,
         new_in,
         first_in,

time: 170 us -> 139 us (0.82)
  Pallas kernels: 155 us -> 136 us
  other arithmetic: 6.92 us -> 0 us
  local copies, waits for them, and re-layouts: 5.07 us -> 1.28 us
    pallas_call x1, Pallas kernels: 155 us -> 130 us  [block_routed(): pl.pallas_call(block_kernel, out_shape=out_shape, in_specs=[anywhere, any...]
    pallas_call x0 -> x1, Pallas kernels: none -> 5.89 us  [update(): pl.pallas_call(update_kernel, grid=(UPDATE_BLOCKS,), out_shape=out_shape,...]
    transpose x2 -> x0, local copies, waits for them, and re-layouts: 3.89 us -> none  [unstripe(): rows.reshape(count // LANES, LANES, columns).swapaxes(0, 1)]
    convert_element_type x2 -> x0, other arithmetic: 3.77 us -> none  [the longest x1 2.13 us: body(): new_in.astype(jnp.bfloat16)]
    div x2 -> x0, other arithmetic: 1.88 us -> none  [body(): grad_vec = summed_vec / total]
where the time goes in v4:
time: 139 us; the launch traced here: 138 us
  Pallas kernels  136 us (98%)
    pallas_call x1, Pallas kernels, block_routed(): pl.pallas_call(block_kernel, out_shape=out_shape, in_specs=[anywhere, any...  130 us
    pallas_call x1, Pallas kernels, update(): pl.pallas_call(update_kernel, grid=(UPDATE_BLOCKS,), out_shape=out_shape,...  5.89 us

profile of v4, /device:TPU:3, one launch (start us, length us, event | category | flops | bytes accessed | tf_op | source)
XLA Modules:
  0.0 138.3 jit_solution(460370057974659279)
XLA Ops:
  1.3 129.9 %shard_map.269 = (bf16[512,768]{1,0:T(8,128)(2,1)}, f32[512,768]{1,0:T(8,128)}, f32[24,4992]{1,0:T(8,128)}, f32[72,768]{1,0:T(8,128)}, f32[4,24,128]{2,1,0:T(8,128)}) custom-call(bf16[1,512,768]{2,1,0:T(8,128)(2,1)} %tokens.1, bf16[1,512,768]{2,1,0:T(8,128)(2,1)} %cotangent.1, s32[1,512]{1,0:T(1,128)} %padding.1, s32[1,512]{1,0:T(1,128)} %opening.1, ...), custom_call_target="tpu_custom_call" | custom-call | tf_op jit(solution)/shard_map/pallas_call | solution.py:1330
  131.2 5.9 %shard_map.270 = (bf16[512,768]{1,0:T(8,128)(2,1)}, f32[512,768]{1,0:T(8,128)}, f32[24,4992]{1,0:T(8,128)}, f32[24,4992]{1,0:T(8,128)}, f32[24,4992]{1,0:T(8,128...) custom-call(s32[1]{0:T(128)S(6)} %copy.31.counter, ...), custom_call_target="tpu_custom_call" | custom-call | tf_op jit(solution)/shard_map/pallas_call | solution.py:1403
  137.1 1.3 slice_bitcast_fusion

commit v5 on v4

--- a/solution.py
+++ b/solution.py
@@ -285,6 +285,15 @@
     def far(self, core):
         return self.near(1 - core)
 
+    def away(self):
+        return self.z % 2 + 1, (3 * self.z + 2) % 5, 3 - 3 * (self.z // 2)
+
+    def when_inner(self, run):
+        pl.when((self.z + 1) // 2 == 1)(run)
+
+    def when_end(self, run):
+        pl.when((self.z + 1) // 2 != 1)(run)
+
     def turn(self, step):
         return lax.rem(self.z + step, PLANES)
 
@@ -306,6 +315,10 @@
         return lambda: pl.semaphore_wait(barrier, len(partners))
 
 
+def always(run):
+    run()
+
+
 def block_of(ref, core, z, near, far):
     return ref.at[core, z, near, far] if core == 0 else ref.at[core, z, far, near]
 
@@ -326,9 +339,10 @@
 
 
 GATHER_SEMS = 4 * 2
-STEPS_AWAY = (1, 3, 2)
-GATHER_NEAR_FIRST = (GLU + 1, GLU + 2)
-REDUCE_NEAR_LAST = (GLU, GLU + 1)
+GATHER_NEAR_FIRST = (1, 6, 7)
+REDUCE_NEAR_LAST = (2, 4, 5, 7)
+GATHER_RELAYED = (0, 1, 2, 3, 4, 5)
+REDUCE_RELAYED = (0, 1, 2, 3, 4, 5, 6, 7)
 
 
 class Gather:
@@ -371,15 +385,20 @@
             self.part(p, self.place.core), self.own_rows(p), self.local.at[p]
         )
 
-    def along_z(self, p, z, target, core):
+    def along_z(self, p, z, target, core, sent=None):
         place = self.place
         near, far = place.sides(core)
         if p in GATHER_NEAR_FIRST:
             part = pair_of(self.buffers[p], core, z, far)
         else:
             part = block_of(self.buffers[p], core, z, near, far)
-        sems = self.sems[0].at[p, target], self.sems[1].at[p, z]
+        sems = self.sems[0].at[p, target if sent is None else sent], self.sems[1].at[p, z]
         return remote(part, part, *sems, place.plane(target))
+
+    def relay(self, p, core):
+        place = self.place
+        last = place.away()[2]
+        return self.along_z(p, last, 3 - last, core, sent=place.z)
 
     def along_near(self, p, z, core):
         block = block_of(self.buffers[p], core, z, *self.place.sides(core))
@@ -412,14 +431,27 @@
         self.buffers[p][place.core, place.z, place.x, place.y] = self.staging[p][...].astype(LOW)
         place.by_core(lambda core: self.along_near(p, place.z, core).start())
 
+    def z_targets(self, p):
+        first, second, third = self.place.away()
+        relayed = self.place.when_inner if p in GATHER_RELAYED else always
+        return (first, always), (second, always), (third, relayed)
+
     def z_own(self, p):
         place = self.place
 
         def run(core):
-            for step in STEPS_AWAY:
-                self.along_z(p, place.z, place.turn(step), core).start()
+            for z, when in self.z_targets(p):
+                when(lambda: self.along_z(p, place.z, z, core).start())
 
         place.by_core(run)
+
+    def from_z(self, p, index, core):
+        place = self.place
+        z = place.away()[index]
+        self.along_z(p, z, place.z, core).wait_recv()
+        if index == 2 and p in GATHER_RELAYED:
+            place.when_inner(lambda: self.relay(p, core).start())
+        return z
 
     def far_own(self, p):
         place = self.place
@@ -430,55 +462,55 @@
 
         place.by_core(run)
 
-    def near(self, p):
+    def near(self, p, *indices):
         place = self.place
 
         def run(core):
-            for step in STEPS_AWAY:
-                z = place.turn(step)
-                self.along_z(p, z, place.z, core).wait_recv()
+            for index in indices or range(3):
+                z = self.from_z(p, index, core)
                 self.along_near(p, z, core).start()
 
         if p not in GATHER_NEAR_FIRST:
             place.by_core(run)
 
-    def far(self, p):
+    def far(self, p, *indices):
         place = self.place
 
         def run(core):
-            for step in STEPS_AWAY:
-                z = place.turn(step)
+            for index in indices or range(3):
+                z = place.away()[index]
                 if p in GATHER_NEAR_FIRST:
-                    self.along_z(p, z, place.z, core).wait_recv()
+                    self.from_z(p, index, core)
                 else:
                     self.along_near(p, z, core).wait_recv()
                 self.along_far(p, z, core).start()
 
         place.by_core(run)
 
-    def chip(self, p):
+    def chip(self, p, *indices):
         def run(core):
-            for step in (0,) + STEPS_AWAY:
-                z = self.place.turn(step)
+            for index in indices or range(4):
+                z = (self.place.z, *self.place.away())[index]
                 self.along_far(p, z, core).wait_recv()
                 self.in_chip(p, z, core).start()
 
         self.place.by_core(run)
 
     def arrive(self, p):
-        for step in (0,) + STEPS_AWAY:
-            z = self.place.turn(step)
+        for z in (self.place.z, *self.place.away()):
             self.in_chip(p, z, 1 - self.place.core).wait_recv()
 
     def drain(self, p):
         self.to_sibling(p).wait_send()
 
         def run(core):
-            for step in (0,) + STEPS_AWAY:
-                z = self.place.turn(step)
-                if step:
-                    self.along_z(p, self.place.z, z, core).wait_send()
-                if p not in GATHER_NEAR_FIRST or step == 0:
+            place = self.place
+            for z, when in self.z_targets(p):
+                when(lambda: self.along_z(p, place.z, z, core).wait_send())
+            if p in GATHER_RELAYED:
+                place.when_inner(lambda: self.relay(p, core).wait_send())
+            for index, z in enumerate((place.z, *place.away())):
+                if p not in GATHER_NEAR_FIRST or index == 0:
                     self.along_near(p, z, core).wait_send()
                 self.along_far(p, z, core).wait_send()
                 self.in_chip(p, z, core).wait_send()
@@ -487,8 +519,6 @@
 
 
 class Reduce:
-    ORDER = STEPS_AWAY + (0,)
-
     def __init__(self, place, grads, refs, results):
         n = len(PIECES)
         self.place, self.grads, self.results = place, grads, results
@@ -537,14 +567,73 @@
             self.place.near(core),
         )
 
-    def along_z(self, p, z, sender, core):
+    def order(self):
+        first, second, third = self.place.away()
+        inner = (self.place.z + 1) // 2 % 2
+        return (
+            inner * first + (1 - inner) * third,
+            second,
+            inner * third + (1 - inner) * first,
+            self.place.z,
+        )
+
+    def z_part(self, p, z, core):
         near, far = self.place.sides(core)
         if p in REDUCE_NEAR_LAST:
-            part = self.pair(p, z, far, core)
+            return self.pair(p, z, far, core)
+        return self.block(p, z, near, far, core)
+
+    def along_z(self, p, z, sender, core):
+        sems = self.sems[4].at[p, z], self.sems[5].at[p, sender]
+        target = self.planes[p].at[sender]
+        return remote(self.z_part(p, z, core), target, *sems, self.place.plane(z))
+
+    def to_relay(self, p, core, slot):
+        first, _, third = self.place.away()
+        sems = self.sems[4].at[p, third], self.sems[5].at[p, slot]
+        target = self.planes[p].at[slot]
+        return remote(self.z_part(p, third, core), target, *sems, self.place.plane(first))
+
+    def send_z(self, p, core, index):
+        place = self.place
+        z = self.order()[index]
+        if index == 1:
+            self.along_z(p, z, place.z, core).start()
+        elif p not in REDUCE_RELAYED:
+            if index != 3:
+                self.along_z(p, z, place.z, core).start()
+        elif index == 0:
+            place.when_inner(lambda: self.along_z(p, z, place.z, core).start())
+            place.when_end(lambda: self.to_relay(p, core, place.away()[0]).start())
+        elif index == 2:
+
+            def pass_on():
+                self.to_relay(p, core, place.z).wait_recv()
+                self.add(self.z_part(p, z, core), self.planes[p].at[place.z])
+
+            place.when_inner(pass_on)
+            self.along_z(p, z, place.z, core).start()
+
+    def sum_planes(self, p, core, result):
+        place = self.place
+        first, second, third = place.away()
+        for z in (first, second):
+            self.along_z(p, place.z, z, core).wait_recv()
+        total = self.z_part(p, place.z, core)[...].astype(WIDE)
+        total = total + self.planes[p][first].astype(WIDE) + self.planes[p][second].astype(WIDE)
+
+        def inner():
+            self.along_z(p, place.z, third, core).wait_recv()
+            result[...] = (total + self.planes[p][third].astype(WIDE)).astype(result.dtype)
+
+        def end():
+            result[...] = total.astype(result.dtype)
+
+        if p in REDUCE_RELAYED:
+            place.when_inner(inner)
+            place.when_end(end)
         else:
-            part = self.block(p, z, near, far, core)
-        sems = self.sems[4].at[p, z], self.sems[5].at[p, sender]
-        return remote(part, self.planes[p].at[sender], *sems, self.place.plane(z))
+            inner()
 
     def result(self, p, core):
         piece = PIECES[p]
@@ -569,49 +658,40 @@
 
     def far(self, p):
         def run(core):
-            for step in self.ORDER:
-                self.along_far(p, self.place.turn(step), core).start()
+            for z in self.order():
+                self.along_far(p, z, core).start()
 
         self.place.by_core(run)
 
-    def after_far(self, p):
+    def after_far(self, p, *indices):
         def run(core):
-            for step in self.ORDER:
-                z = self.place.turn(step)
+            for index in indices or range(4):
+                z = self.order()[index]
                 self.along_far(p, z, core).wait_recv()
                 self.add(self.pair(p, z, self.place.sides(core)[1], core), self.far_got[p].at[z])
-                if p not in REDUCE_NEAR_LAST:
+                if p in REDUCE_NEAR_LAST:
+                    self.send_z(p, core, index)
+                else:
                     self.along_near(p, z, core).start()
-                elif step:
-                    self.along_z(p, z, self.place.z, core).start()
 
         self.place.by_core(run)
 
-    def after_near(self, p):
+    def after_near(self, p, *indices):
         place = self.place
 
         def run(core):
             near, far = place.sides(core)
             if p in REDUCE_NEAR_LAST:
-                self.along_z_waits(p, core)
-                total = self.pair(p, place.z, far, core)[...].astype(WIDE)
-                for step in STEPS_AWAY:
-                    total = total + self.planes[p][place.turn(step)].astype(WIDE)
-                self.pair(p, place.z, far, core)[...] = total.astype(LOW)
+                self.sum_planes(p, core, self.pair(p, place.z, far, core))
                 self.along_near(p, place.z, core).start()
                 return
-            for step in self.ORDER:
-                z = place.turn(step)
+            for index in indices or range(4):
+                z = self.order()[index]
                 self.along_near(p, z, core).wait_recv()
                 self.add(self.block(p, z, near, far, core), self.near_got[p].at[z])
-                if step:
-                    self.along_z(p, z, place.z, core).start()
+                self.send_z(p, core, index)
 
         place.by_core(run)
-
-    def along_z_waits(self, p, core):
-        for step in STEPS_AWAY:
-            self.along_z(p, self.place.z, self.place.turn(step), core).wait_recv()
 
     def finish(self, p):
         rows, place = PIECES[p].rows, self.place
@@ -620,14 +700,10 @@
             near, far = place.sides(core)
             if p in REDUCE_NEAR_LAST:
                 self.along_near(p, place.z, core).wait_recv()
-                others = [self.near_got[p].at[place.z]]
+                own = self.block(p, place.z, near, far, core)[...].astype(WIDE)
+                self.final[p][...] = own + self.near_got[p][place.z].astype(WIDE)
             else:
-                self.along_z_waits(p, core)
-                others = [self.planes[p].at[place.turn(step)] for step in STEPS_AWAY]
-            total = self.block(p, place.z, near, far, core)[...].astype(WIDE)
-            for other in others:
-                total = total + other[...].astype(WIDE)
-            self.final[p][...] = total
+                self.sum_planes(p, core, self.final[p])
             self.to_sibling(p, core).start()
             target, columns = self.result(p, core)
             target[...] = self.final[p][pl.ds(rows * core, rows), columns]
@@ -635,30 +711,37 @@
         place.by_core(run)
 
     def drain(self, p):
+        place = self.place
+
         def run(core):
             self.to_sibling(p, 1 - core).wait_recv()
             self.to_sibling(p, core).wait_send()
-            for step in self.ORDER:
-                z = self.place.turn(step)
+            first, second, third = place.away()
+            for z in (first, second):
+                self.along_z(p, z, place.z, core).wait_send()
+            if p in REDUCE_RELAYED:
+                place.when_inner(lambda: self.along_z(p, third, place.z, core).wait_send())
+                place.when_end(lambda: self.to_relay(p, core, first).wait_send())
+            else:
+                self.along_z(p, third, place.z, core).wait_send()
+            for index, z in enumerate((place.z, first, second, third)):
                 self.along_far(p, z, core).wait_send()
-                if p not in REDUCE_NEAR_LAST or step == 0:
+                if p not in REDUCE_NEAR_LAST or index == 0:
                     self.along_near(p, z, core).wait_send()
-                if step:
-                    self.along_z(p, z, self.place.z, core).wait_send()
-
-        self.place.by_core(run)
+
+        place.by_core(run)
 
 
 def tiled(column, count):
     return jnp.concatenate([column] * count, axis=1)
 
 
-def some(index, size=ROWS):
-    return pl.ds(pl.multiple_of(index * size, size), size)
-
-
-def each_block(run, size=ROWS, count=SLOTS):
-    lax.fori_loop(0, count // size, lambda i, _: (run(some(i, size)), 0)[1], 0)
+def each_block(run, size=ROWS):
+    def block(i, carry):
+        run(pl.ds(pl.multiple_of(i * size, size), size))
+        return carry
+
+    lax.fori_loop(0, SLOTS // size, block, 0)
 
 
 def inner(left, right, dims=((1,), (0,))):
@@ -718,7 +801,6 @@
         d_gate=vmem((2, SLOTS, PIECES[1].columns), LOW),
         d_gate_got=vmem((SLOTS, PIECES[1].columns), LOW),
         pre_mix=vmem((SLOTS, MIX), WIDE),
-        glu=vmem((3, SLOTS // 2, CHUNK), WIDE),
         retain=vmem((SLOTS, CH), WIDE),
         drive=vmem(rows, WIDE),
         states=vmem((2, SLOTS + LANES, CH), WIDE),
@@ -841,13 +923,9 @@
         return jnp.concatenate([self.params[2:3, :CH], self.params[2:3, CH:]], axis=0)
 
     def first_norm(self, raw):
-        self.tokens[...] = inner(self.perm[...], raw[...]).astype(LOW)
-
-        def run(rows):
-            values = self.tokens[rows, :].astype(WIDE)
-            self.normed[rows, :] = (values * row_norm(values) * self.params[0:1]).astype(LOW)
-
-        each_block(run)
+        values = inner(self.perm[...], raw[...])
+        self.tokens[...] = values.astype(LOW)
+        self.normed[0:SLOTS] = (values * row_norm(values) * self.params[0:1]).astype(LOW)
 
     def mask_upstream(self, raw):
         striped = inner(self.perm[...], raw[...]) * tiled(self.live[...], D // TILE)
@@ -855,25 +933,21 @@
         self.upstream[1] = striped[:, D // 2 :].astype(LOW)
 
     def mix(self, m):
-        normed, piece = self.normed[0:SLOTS, :], PIECES[m]
-        for half in range(2):
-            skip = piece.overlap * half
-            start = piece.starts[half] + skip
-            product = inner(normed, self.mix_weight(half, m))
-            self.pre_mix[:, start : start + piece.columns - skip] = product[:, skip:]
+        piece = PIECES[m]
+        weight = (self.mix_weight(0, m), self.mix_weight(1, m)[:, piece.overlap :])
+        weight = jnp.concatenate(weight, axis=1)
+        start = piece.starts[0]
+        self.pre_mix[:, start : start + weight.shape[1]] = inner(self.normed[0:SLOTS], weight)
 
     def drives(self):
-        def run(rows):
-            forget = jax.nn.sigmoid(-(self.pre_mix[rows, :CH] + self.params[3:4, :CH]))
-            pre = self.pre_mix[rows, CH : CH + D]
-            driver = pre * jax.nn.sigmoid(pre)
-            opens = tiled(self.opens[rows, :], CH // TILE)
-            decay = jnp.where(opens > 0.5, 1.0, forget).astype(LOW).astype(WIDE)
-            self.retain[rows, :] = 1.0 - decay
-            drive = jnp.concatenate([forget, forget], axis=1) * driver
-            self.drive[rows, :] = drive.astype(LOW).astype(WIDE)
-
-        each_block(run)
+        forget = jax.nn.sigmoid(-(self.pre_mix[:, :CH] + self.params[3:4, :CH]))
+        pre = self.pre_mix[:, CH : CH + D]
+        driver = pre * jax.nn.sigmoid(pre)
+        opens = tiled(self.opens[...], CH // TILE)
+        decay = jnp.where(opens > 0.5, 1.0, forget).astype(LOW).astype(WIDE)
+        self.retain[...] = 1.0 - decay
+        drive = jnp.concatenate([forget, forget], axis=1) * driver
+        self.drive[...] = drive.astype(LOW).astype(WIDE)
 
     def parts(self):
         return self.drive.at[:, pl.ds(0, CH)], self.drive.at[:, pl.ds(CH, CH)]
@@ -914,66 +988,40 @@
         run = whole_forward
         run(self.retain, *self.parts(), self.turn(), self.summaries.at[0], start, self.states)
 
-    def recurrent(self, rows):
-        after = pl.ds(pl.multiple_of(rows.start + LANES, LANES), rows.size)
-        both = jnp.concatenate([self.states[0, after, :], self.states[1, after, :]], axis=1)
+    def recurrent(self):
+        both = jnp.concatenate([self.states[0, LANES:], self.states[1, LANES:]], axis=1)
         return both.astype(LOW).astype(WIDE)
 
     def gate_rows(self):
-        def run(rows):
-            pre = self.pre_mix[rows, CH + D :]
-            masked = self.recurrent(rows) * tiled(self.live[rows, :], D // TILE)
-            self.gated[rows, :] = (masked * (pre * jax.nn.sigmoid(pre))).astype(LOW)
-
-        each_block(run)
+        pre = self.pre_mix[:, CH + D :]
+        masked = self.recurrent() * tiled(self.live[...], D // TILE)
+        self.gated[0:SLOTS] = (masked * (pre * jax.nn.sigmoid(pre))).astype(LOW)
 
     def second_norm(self):
-        self.middle[...] = inner(self.gated[0:SLOTS, :], self.out_weight(0, D))
-
-        def run(rows):
-            middle = self.tokens[rows, :].astype(WIDE) + self.middle[rows, :]
-            self.middle[rows, :] = middle
-            self.normed_two[rows, :] = (middle * row_norm(middle) * self.params[1:2]).astype(LOW)
-
-        each_block(run)
+        mixed = inner(self.gated[0:SLOTS], self.out_weight(0, D))
+        middle = self.tokens[...].astype(WIDE) + mixed
+        self.middle[...] = middle
+        self.total[...] = middle
+        self.normed_two[0:SLOTS] = (middle * row_norm(middle) * self.params[1:2]).astype(LOW)
+
+    def whole_upstream(self):
+        return jnp.concatenate([self.upstream[0], self.upstream[1]], axis=1)
 
     def glu_forward(self, k):
-        weight = self.glu_weight(k)
-        down = self.out_weight(D + CHUNK * k, CHUNK)
-        half = SLOTS // 2
-        for part in range(2):
-            rows = slice(part * half, (part + 1) * half)
-            pre = inner(self.normed_two[rows, :], weight)
-            self.glu[0] = pre[:, :CHUNK]
-            self.glu[1] = pre[:, CHUNK:]
-            upstream = jnp.concatenate([self.upstream[0, rows], self.upstream[1, rows]], axis=1)
-            self.glu[2] = across(upstream, down)
-
-            def run(block):
-                gate, up, d_hidden = (self.glu[i, block, :] for i in range(3))
-                own = pl.ds(pl.multiple_of(block.start + part * half, ROWS), ROWS)
-                logistic = jax.nn.sigmoid(gate)
-                active = gate * logistic
-                slope = logistic * (1.0 + gate * (1.0 - logistic))
-                self.hidden[k, own, :] = (active * up).astype(LOW)
-                self.d_glu[k, 0, own, :] = (d_hidden * up * slope).astype(LOW)
-                self.d_glu[k, 1, own, :] = (d_hidden * active).astype(LOW)
-
-            each_block(run, count=half)
+        pre = inner(self.normed_two[0:SLOTS], self.glu_weight(k))
+        gate, up = pre[:, :CHUNK], pre[:, CHUNK:]
+        d_hidden = across(self.whole_upstream(), self.out_weight(D + CHUNK * k, CHUNK))
+        logistic = jax.nn.sigmoid(gate)
+        active = gate * logistic
+        slope = logistic * (1.0 + gate * (1.0 - logistic))
+        self.hidden[k, 0:SLOTS] = (active * up).astype(LOW)
+        self.d_glu[k, 0] = (d_hidden * up * slope).astype(LOW)
+        self.d_glu[k, 1] = (d_hidden * active).astype(LOW)
 
     def glu_back(self, k):
-        down = self.out_weight(D + CHUNK * k, CHUNK)
-        share = inner(self.hidden[k, 0:SLOTS, :], down)
         d_glu = jnp.concatenate([self.d_glu[k, 0], self.d_glu[k, 1]], axis=1)
         d_share = across(d_glu, self.glu_weight(k))
-        if k == 0:
-            self.total[...] = self.middle[...] + share
-            self.d_normed[...] = d_share
-        else:
-            self.total[...] += share
-            self.d_normed[...] += d_share
-        if k == CHUNKS - 1:
-            self.block_out[...] = self.total[...].astype(LOW)
+        self.d_normed[...] = d_share if k == 0 else self.d_normed[...] + d_share
 
     def own_half(self, ref, got):
         return jnp.concatenate([ref[self.place.core], got], axis=0)
@@ -985,38 +1033,31 @@
         self.put_out(D + CHUNK * k, along(self.hidden[k], upstream))
 
     def add_sum(self, index, values):
-        self.sums[index, :, : values.shape[1]] += eights(values)
+        self.sums[index] += eights(values)
 
     def middle_back(self):
-        def run(rows):
-            middle, d_normed = self.middle[rows, :], self.d_normed[rows, :]
-            scaling = row_norm(middle)
-            self.add_sum(1, d_normed * middle * scaling)
-            scaled = d_normed * self.params[1:2]
-            mean = jnp.mean(middle * scaled, axis=1, keepdims=True)
-            upstream = jnp.concatenate([self.upstream[0, rows], self.upstream[1, rows]], axis=1)
-            d_middle = upstream.astype(WIDE) + scaling * scaled - middle * (scaling**3 * mean)
-            self.middle[rows, :] = d_middle
-            self.d_out[0, rows] = d_middle[:, : D // 2].astype(LOW)
-            self.d_out[1, rows] = d_middle[:, D // 2 :].astype(LOW)
-
-        each_block(run)
+        middle, d_normed = self.middle[...], self.d_normed[...]
+        scaling = row_norm(middle)
+        self.add_sum(1, d_normed * middle * scaling)
+        scaled = d_normed * self.params[1:2]
+        mean = jnp.mean(middle * scaled, axis=1, keepdims=True)
+        upstream = self.whole_upstream().astype(WIDE)
+        d_middle = upstream + scaling * scaled - middle * (scaling**3 * mean)
+        self.middle[...] = d_middle
+        self.d_out[0] = d_middle[:, : D // 2].astype(LOW)
+        self.d_out[1] = d_middle[:, D // 2 :].astype(LOW)
 
     def gate_back(self):
         d_out = jnp.concatenate([self.d_out[0], self.d_out[1]], axis=1)
-        self.total[...] = across(d_out, self.out_weight(0, D))
-
-        def run(rows):
-            pre, d_gated = self.pre_mix[rows, CH + D :], self.total[rows, :]
-            logistic = jax.nn.sigmoid(pre)
-            d_live = d_gated * tiled(self.live[rows, :], D // TILE)
-            self.drive[rows, :] = (d_live * (pre * logistic)).astype(LOW).astype(WIDE)
-            slope = logistic * (1.0 + pre * (1.0 - logistic))
-            d_gate = (d_live * self.recurrent(rows) * slope).astype(LOW)
-            self.d_gate[0, rows, :] = d_gate[:, : D // 2]
-            self.d_gate[1, rows, :] = d_gate[:, D // 2 :]
-
-        each_block(run)
+        d_gated = across(d_out, self.out_weight(0, D))
+        pre = self.pre_mix[:, CH + D :]
+        logistic = jax.nn.sigmoid(pre)
+        d_live = d_gated * tiled(self.live[...], D // TILE)
+        self.drive[...] = (d_live * (pre * logistic)).astype(LOW).astype(WIDE)
+        slope = logistic * (1.0 + pre * (1.0 - logistic))
+        d_gate = (d_live * self.recurrent() * slope).astype(LOW)
+        self.d_gate[0] = d_gate[:, : D // 2]
+        self.d_gate[1] = d_gate[:, D // 2 :]
 
     def mixer_out_grad(self):
         d_out = self.own_half(self.d_out, self.d_out_got[...])
@@ -1073,20 +1114,18 @@
         skip = PIECES[0].overlap
         left = jnp.concatenate([self.d_drive[0], self.d_drive[1][:, skip:]], axis=1)
         right = jnp.concatenate([self.mix_weight(0, 0), self.mix_weight(1, 0)[:, skip:]], axis=1)
-        self.d_normed[...] += across(left, right)
-
-        def run(rows):
-            values, d_normed = self.tokens[rows, :].astype(WIDE), self.d_normed[rows, :]
-            scaling = row_norm(values)
-            self.add_sum(0, d_normed * values * scaling)
-            scaled = d_normed * self.params[0:1]
-            mean = jnp.mean(values * scaled, axis=1, keepdims=True)
-            self.middle[rows, :] += scaling * scaled - values * (scaling**3 * mean)
-
-        each_block(run)
+        d_normed = self.d_normed[...] + across(left, right)
+        values = self.tokens[...].astype(WIDE)
+        scaling = row_norm(values)
+        self.add_sum(0, d_normed * values * scaling)
+        scaled = d_normed * self.params[0:1]
+        mean = jnp.mean(values * scaled, axis=1, keepdims=True)
+        self.middle[...] += scaling * scaled - values * (scaling**3 * mean)
 
     def natural_out(self):
-        self.block_out[...] = along(self.perm[...], self.block_out[...]).astype(LOW)
+        hidden = jnp.concatenate([self.hidden[k, 0:SLOTS] for k in range(CHUNKS)], axis=1)
+        total = self.total[...] + inner(hidden, self.out_weight(D, FF))
+        self.block_out[...] = along(self.perm[...], total.astype(LOW)).astype(LOW)
 
     def natural_tokens(self):
         rest = self.middle[...]
@@ -1160,145 +1199,247 @@
         pltpu.make_async_copy(tokens.at[0], raw_tokens, block.arrivals.at[0]),
         pltpu.make_async_copy(cotangent.at[0], raw_upstream, block.arrivals.at[1]),
     ]
+    leave_out = pltpu.make_async_copy(block.block_out, block_out, block.departures.at[0])
+    leave_tokens = pltpu.make_async_copy(block.d_normed, d_tokens, block.departures.at[1])
     for load in loads:
         load.start()
     block.prepare(padding, opening, vectors)
     entered()
     gather.begin()
+    gather.near_own(0)
+    gather.z_own(0)
+    gather.near_own(2)
+    gather.near_own(5)
+    gather.near_own(3)
+    gather.z_own(3)
+    gather.near_own(4)
+    gather.near_own(1)
+    gather.near_own(6)
+    gather.z_own(2)
+    gather.far_own(0)
+    gather.near(0, 0)
+    gather.far_own(5)
+    gather.near_own(7)
+    gather.far_own(4)
+    gather.far_own(2)
+    gather.far_own(1)
+    gather.far_own(3)
+    gather.z_own(1)
+    gather.far_own(6)
+    gather.near(0, 1)
+    gather.near(3, 0)
+    gather.near(0, 2)
+    gather.z_own(4)
+    gather.near(3, 1)
+    gather.far(0, 1)
+    gather.far_own(7)
     loads[0].wait()
     block.first_norm(raw_tokens)
-
-    out = range(OUT, GLU)
-    for p in (0, 1):
-        gather.near_own(p)
-        gather.z_own(p)
-    for p in range(2, n):
-        gather.near_own(p)
+    gather.near(3, 2)
+    gather.near(2, 0)
+    gather.z_own(5)
+    gather.far(0, 0)
+    gather.near(2, 1)
+    gather.far(1, 0)
+    gather.z_own(6)
     loads[1].wait()
     block.mask_upstream(raw_upstream)
-    block.give("normed", "upstream")
-    gather.far_own(0)
-    gather.far_own(1)
-    gather.near(0)
-    gather.z_own(2)
-    gather.far_own(2)
-    gather.far(0)
-    gather.near(1)
-    gather.z_own(3)
-    gather.far_own(3)
-    gather.chip(0)
-    gather.far(1)
-    gather.near(2)
-    gather.z_own(4)
-    gather.far_own(4)
+    gather.chip(1, 0)
+    gather.near(4, 1)
+    gather.far(3, 0, 1)
+    gather.far(2, 1)
+    gather.near(2, 2)
+    gather.near(5, 1, 0)
+    block.give("normed")
+    gather.near(4, 2)
+    gather.far(3, 2)
+    gather.far(1, 1)
+    gather.far(2, 0)
+    gather.z_own(7)
+    gather.chip(5, 0)
+    gather.chip(6, 0)
+    gather.far(0, 2)
+    gather.chip(0, 2)
+    gather.chip(3, 0)
+    gather.chip(0, 0)
+    gather.far(4, 1)
+    gather.near(4, 0)
+    gather.far(2, 2)
+    gather.near(5, 2)
+    gather.far(4, 2)
+    gather.chip(7, 0)
+    gather.far(6, 1)
+    gather.chip(0, 1)
+    gather.far(1, 2)
+    gather.chip(4, 0)
+    gather.chip(0, 3)
+    gather.chip(2, 1)
+    gather.chip(3, 2)
+    gather.chip(1, 2)
+    gather.far(4, 0)
+    gather.chip(3, 1)
+    gather.chip(2, 3)
+    gather.far(5, 0)
+    gather.chip(4, 3)
+    gather.far(5, 1)
     gather.arrive(0)
+    gather.chip(2, 0)
+    block.give("upstream")
+    gather.chip(1, 1)
+    gather.chip(4, 2)
     block.mix(0)
+    gather.far(6, 0)
+    gather.chip(1, 3)
+    gather.chip(3, 3)
     block.drives()
     block.scan_own(0)
-    gather.chip(1)
-    gather.far(2)
-    gather.near(3)
-    gather.z_own(5)
-    gather.far_own(5)
+    gather.chip(5, 1)
+    gather.far(5, 2)
+    gather.chip(2, 2)
+    gather.chip(6, 2)
+    gather.chip(4, 1)
+    gather.far(6, 2)
+    gather.far(7, 1)
+    gather.chip(6, 1)
+    gather.far(7, 0)
+    gather.arrive(2)
+    gather.chip(5, 2)
+    gather.far(7, 2)
     gather.arrive(1)
+    gather.arrive(3)
     block.mix(1)
-    gather.chip(2)
-    gather.far(3)
-    gather.near(4)
-    gather.far_own(6)
-    gather.z_own(6)
+    gather.chip(5, 3)
     block.scan_states()
+    gather.arrive(4)
     block.gate_rows()
+    gather.chip(6, 3)
     block.give("gated")
-    gather.chip(3)
-    gather.far(4)
-    gather.near(5)
-    gather.far_own(7)
-    gather.z_own(7)
-    gather.chip(4)
-    gather.far(5)
-    for p in out:
-        gather.arrive(p)
     block.second_norm()
+    gather.arrive(5)
+    gather.chip(7, 2)
     block.give("normed_two")
-    gather.chip(5)
-    gather.far(6)
-
-    def glu_chunk(k, beside):
-        gather.arrive(GLU + k)
-        block.glu_forward(k)
-        block.give(("hidden", k), ("d_glu", k))
-        for run, p in beside:
-            run(p)
-        block.glu_back(k)
-        if k == 0:
-            block.take("upstream", "normed_two")
-        block.take(("hidden", k), ("d_glu", k))
-        block.glu_grads(k)
-
-    glu_chunk(0, ((gather.chip, 6), (gather.far, 7)))
-    reduce.far(GLU)
-    glu_chunk(1, ((gather.chip, 7),))
-    reduce.far(GLU + 1)
-    glu_chunk(2, ((reduce.after_far, GLU),))
+    block.glu_forward(0)
+    gather.arrive(6)
+    gather.chip(7, 3)
+    block.take("gated")
+    gather.chip(7, 1)
+    block.give(("d_glu", 0))
+    block.glu_forward(1)
+    block.give(("hidden", 0))
+    gather.arrive(7)
+    block.give(("d_glu", 1))
+    block.glu_forward(2)
+    block.give(("hidden", 2))
+    block.take("normed", "upstream", ("hidden", 0), "normed_two")
+    block.give(("d_glu", 2))
+    block.take(("d_glu", 0))
+    block.glu_grads(0)
+    reduce.far(5)
+    block.glu_back(0)
+    block.take(("d_glu", 2))
+    block.give(("hidden", 1))
+    block.take(("hidden", 2))
+    block.glu_grads(2)
+    reduce.far(7)
+    block.take(("d_glu", 1))
+    block.glu_back(1)
+    block.take(("hidden", 1))
+    reduce.after_far(5, 0)
+    block.glu_grads(1)
+    reduce.after_far(5, 1)
+    block.glu_back(2)
+    reduce.far(6)
     block.middle_back()
+    reduce.after_far(7, 0)
     block.give("d_out")
+    reduce.after_far(5, 2)
     block.gate_back()
+    block.take("d_out")
+    block.mixer_out_grad()
+    reduce.far(4)
+    reduce.far(2)
+    block.give("d_gate")
+    reduce.after_far(6, 0)
     block.scan_own(1)
-    reduce.far(GLU + 2)
-    block.give("d_gate")
-    block.take("gated", "d_out")
-    block.mixer_out_grad()
-    reduce.after_far(GLU + 1)
-    for p in out:
-        reduce.far(p)
-    block.take("normed", "d_gate")
+    block.take("d_gate")
     block.mix_grads(1)
+    reduce.after_far(7, 2)
+    reduce.after_far(4, 0)
     reduce.far(1)
-    block.gate_normed()
-    reduce.after_near(GLU)
-    reduce.after_far(GLU + 2)
+    reduce.far(3)
     block.scan_back()
+    reduce.after_far(7, 1)
+    reduce.after_far(4, 1)
     block.drives_back()
+    reduce.after_far(2, 1)
     block.give("d_drive")
-    reduce.after_far(OUT)
-    reduce.after_near(GLU + 1)
     block.take("d_drive")
     block.mix_grads(0)
+    reduce.after_far(2, 0)
+    reduce.after_far(1, 0)
+    reduce.after_far(4, 2)
     reduce.far(0)
+    reduce.after_near(6, 0)
+    reduce.after_far(1, 2)
+    block.gate_normed()
+    reduce.after_far(7, 3)
+    reduce.after_far(3, 0)
+    reduce.after_far(2, 3)
+    block.first_back()
+    reduce.after_far(1, 1)
+    reduce.after_far(2, 2)
+    reduce.after_far(5, 3)
+    reduce.after_near(1, 0)
+    reduce.after_near(3, 0)
+    reduce.after_far(3, 1)
+    reduce.after_far(0, 0)
     block.natural_out()
-    leave_out = pltpu.make_async_copy(block.block_out, block_out, block.departures.at[0])
     leave_out.start()
-    reduce.after_far(OUT + 1)
-    reduce.after_near(GLU + 2)
-    reduce.finish(GLU)
-    block.first_back()
-    reduce.after_far(OUT + 2)
-    reduce.after_near(OUT)
     block.gather_vector()
+    reduce.after_near(1, 1)
+    reduce.after_far(6, 1)
+    reduce.after_near(3, 1)
     block.vector_step(0)
+    reduce.after_far(0, 1)
+    reduce.after_near(1, 2)
+    block.vector_step(1)
+    reduce.after_near(0, 0)
+    reduce.after_far(0, 2)
+    reduce.after_far(3, 2)
+    reduce.after_near(6, 1)
+    reduce.after_far(4, 3)
+    reduce.after_near(5)
+    reduce.after_far(6, 2)
+    reduce.after_far(1, 3)
+    reduce.after_far(3, 3)
+    reduce.after_near(0, 1)
+    reduce.after_near(2)
+    block.vector_step(2)
+    reduce.after_near(0, 2)
+    reduce.after_far(0, 3)
+    reduce.after_near(7)
+    reduce.after_far(6, 3)
+    reduce.after_near(4)
+    reduce.after_near(3, 2)
+    reduce.after_near(6, 2)
     block.natural_tokens()
-    leave_tokens = pltpu.make_async_copy(block.d_normed, d_tokens, block.departures.at[1])
     leave_tokens.start()
-    reduce.after_far(1)
-    reduce.after_near(OUT + 1)
-    block.vector_step(1)
-    reduce.finish(GLU + 1)
-    reduce.after_near(OUT + 2)
-    reduce.after_far(0)
-    reduce.finish(GLU + 2)
-    reduce.after_near(1)
-    block.vector_step(2)
-    reduce.finish(OUT)
-    reduce.after_near(0)
     block.vector_step(3)
     for step in (1, 2, 3):
         block.vector_plane(planes, step, place.z).start()
     planes[place.z] = block.vector[3]
-    reduce.finish(OUT + 1)
-    reduce.finish(OUT + 2)
+    reduce.after_near(0, 3)
+    reduce.finish(5)
+    reduce.after_near(1, 3)
+    reduce.finish(2)
     reduce.finish(1)
+    reduce.finish(7)
+    reduce.after_near(6, 3)
+    reduce.finish(4)
+    reduce.after_near(3, 3)
     reduce.finish(0)
+    reduce.finish(3)
+    reduce.finish(6)
 
     for step in (1, 2, 3):
         block.vector_plane(planes, step, place.z).wait_send()

time: 139 us -> 127 us (0.914); the launches traced: 138 us -> 125 us
  Pallas kernels: 136 us -> 122 us
    pallas_call x1, Pallas kernels: 130 us -> 116 us  [block_routed(): pl.pallas_call(block_kernel, out_shape=out_shape, in_specs=[anywhere, any...]
where the time goes in v5:
time: 127 us; the launch traced here: 125 us
  Pallas kernels  122 us (96%)
  between operations  1.32 us (1%)
  local copies, waits for them, and re-layouts  1.28 us (1%)
    pallas_call x1, Pallas kernels, block_routed(): pl.pallas_call(block_kernel, out_shape=out_shape, in_specs=[anywhere, any...  116 us
    pallas_call x1, Pallas kernels, update(): pl.pallas_call(update_kernel, grid=(UPDATE_BLOCKS,), out_shape=out_shape,...  5.84 us

profile of v5, /device:TPU:3, one launch (start us, length us, event | category | flops | bytes accessed | tf_op | source)
XLA Modules:
  0.0 124.8 jit_solution(8616838440927734653)
XLA Ops:
  1.3 116.3 %shard_map.269 = (bf16[512,768]{1,0:T(8,128)(2,1)}, f32[512,768]{1,0:T(8,128)}, f32[24,4992]{1,0:T(8,128)}, f32[72,768]{1,0:T(8,128)}, f32[4,24,128]{2,1,0:T(8,128)}) custom-call(bf16[1,512,768]{2,1,0:T(8,128)(2,1)} %tokens.1, bf16[1,512,768]{2,1,0:T(8,128)(2,1)} %cotangent.1, s32[1,512]{1,0:T(1,128)} %padding.1, s32[1,512]{1,0:T(1,128)} %opening.1, ...), custom_call_target="tpu_custom_call" | custom-call | tf_op jit(solution)/shard_map/pallas_call | solution.py:1471
  117.6 5.8 %shard_map.270 = (bf16[512,768]{1,0:T(8,128)(2,1)}, f32[512,768]{1,0:T(8,128)}, f32[24,4992]{1,0:T(8,128)}, f32[24,4992]{1,0:T(8,128)}, f32[24,4992]{1,0:T(8,128...) custom-call(s32[1]{0:T(128)S(6)} %copy.31.counter, ...), custom_call_target="tpu_custom_call" | custom-call | tf_op jit(solution)/shard_map/pallas_call | solution.py:1544
  123.5 1.3 %slice_bitcast_fusion = f32[384]{0:T(512)} fusion(f32[18,128]{1,0:T(8,128)} %get-tuple-element.55), kind=kLoop, calls=%fused_computation | loop fusion | bytes 3072 | tf_op jit(solution)/shard_map/slice | solution.py:1698

commit v6 on v5

--- a/solution.py
+++ b/solution.py
@@ -338,18 +338,18 @@
     )
 
 
-GATHER_SEMS = 4 * 2
-GATHER_NEAR_FIRST = (1, 6, 7)
-REDUCE_NEAR_LAST = (2, 4, 5, 7)
-GATHER_RELAYED = (0, 1, 2, 3, 4, 5)
-REDUCE_RELAYED = (0, 1, 2, 3, 4, 5, 6, 7)
+GATHER_NEAR_FIRST = (4, 6, 7)
+REDUCE_NEAR_LAST = (2, 3, 6, 7)
+GATHER_RELAYED = (0, 2, 4, 5, 6)
+REDUCE_RELAYED = (0, 2, 3, 4, 5, 7)
 
 
 class Gather:
     def __init__(self, place, masters, buffers, staging, sems):
         self.place, self.masters, self.buffers, self.staging = place, masters, buffers, staging
         self.local, self.sent0, self.got0 = sems[:3]
-        self.sems = sems[3:]
+        self.z_sent, self.near_sent, self.far_sent, self.chip_sent, self.chip_got = sems[3:8]
+        self.z_got, self.near_got, self.far_got = sems[8:]
 
     @staticmethod
     def scratch():
@@ -358,8 +358,8 @@
         return (
             [pltpu.VMEM(p.shape(), LOW) for p in PIECES]
             + [pltpu.VMEM((2 * p.rows, p.columns), WIDE) for p in PIECES]
-            + [dma((n,))] * 3
-            + [dma((n, PLANES))] * GATHER_SEMS
+            + [dma((n,))] * 8
+            + [dma((n, PLANES))] * 3
         )
 
     def part(self, p, half):
@@ -385,37 +385,37 @@
             self.part(p, self.place.core), self.own_rows(p), self.local.at[p]
         )
 
-    def along_z(self, p, z, target, core, sent=None):
+    def along_z(self, p, z, target, core):
         place = self.place
         near, far = place.sides(core)
         if p in GATHER_NEAR_FIRST:
             part = pair_of(self.buffers[p], core, z, far)
         else:
             part = block_of(self.buffers[p], core, z, near, far)
-        sems = self.sems[0].at[p, target if sent is None else sent], self.sems[1].at[p, z]
+        sems = self.z_sent.at[p], self.z_got.at[p, z]
         return remote(part, part, *sems, place.plane(target))
 
     def relay(self, p, core):
         place = self.place
         last = place.away()[2]
-        return self.along_z(p, last, 3 - last, core, sent=place.z)
+        return self.along_z(p, last, 3 - last, core)
 
     def along_near(self, p, z, core):
         block = block_of(self.buffers[p], core, z, *self.place.sides(core))
         return remote(
-            block, block, self.sems[2].at[p, z], self.sems[3].at[p, z], self.place.near(core)
+            block, block, self.near_sent.at[p], self.near_got.at[p, z], self.place.near(core)
         )
 
     def along_far(self, p, z, core):
         pair = pair_of(self.buffers[p], core, z, self.place.sides(core)[1])
         return remote(
-            pair, pair, self.sems[4].at[p, z], self.sems[5].at[p, z], self.place.far(core)
+            pair, pair, self.far_sent.at[p], self.far_got.at[p, z], self.place.far(core)
         )
 
-    def in_chip(self, p, z, core):
-        plane = self.buffers[p].at[core, z]
+    def in_chip(self, p, planes, core):
+        part = self.buffers[p].at[core, planes]
         return remote(
-            plane, plane, self.sems[6].at[p, z], self.sems[7].at[p, z], self.place.sibling()
+            part, part, self.chip_sent.at[p], self.chip_got.at[p], self.place.sibling()
         )
 
     def begin(self):
@@ -497,25 +497,32 @@
         self.place.by_core(run)
 
     def arrive(self, p):
-        for z in (self.place.z, *self.place.away()):
-            self.in_chip(p, z, 1 - self.place.core).wait_recv()
+        self.in_chip(p, pl.ds(0, PLANES), 1 - self.place.core).wait_recv()
 
     def drain(self, p):
+        place, ref = self.place, self.buffers[p]
         self.to_sibling(p).wait_send()
 
+        def sent(part, sem):
+            remote(part, part, sem.at[p], sem.at[p], place.sibling()).wait_send()
+
         def run(core):
-            place = self.place
-            for z, when in self.z_targets(p):
-                when(lambda: self.along_z(p, place.z, z, core).wait_send())
+            def sent_z(count):
+                planes = pl.ds(0, count)
+                near_first = p in GATHER_NEAR_FIRST
+                part = ref.at[core, planes, :, 0] if near_first else ref.at[core, planes, 0, 0]
+                sent(part, self.z_sent)
+
             if p in GATHER_RELAYED:
-                place.when_inner(lambda: self.relay(p, core).wait_send())
-            for index, z in enumerate((place.z, *place.away())):
-                if p not in GATHER_NEAR_FIRST or index == 0:
-                    self.along_near(p, z, core).wait_send()
-                self.along_far(p, z, core).wait_send()
-                self.in_chip(p, z, core).wait_send()
-
-        self.place.by_core(run)
+                place.when_inner(lambda: sent_z(4))
+                place.when_end(lambda: sent_z(2))
+            else:
+                sent_z(3)
+            sent(ref.at[core, pl.ds(0, 1 if p in GATHER_NEAR_FIRST else 4), 0, 0], self.near_sent)
+            sent(ref.at[core, :, :, 0], self.far_sent)
+            sent(ref.at[core], self.chip_sent)
+
+        place.by_core(run)
 
 
 class Reduce:
@@ -523,7 +530,9 @@
         n = len(PIECES)
         self.place, self.grads, self.results = place, grads, results
         self.far_got, self.near_got, self.planes, self.final = (refs[k * n : (k + 1) * n] for k in range(4))
-        self.sems = refs[4 * n :]
+        self.far_sem, self.near_sem, self.z_sem = refs[4 * n : 4 * n + 3]
+        self.far_sent, self.near_sent, self.z_sent = refs[4 * n + 3 : 4 * n + 6]
+        self.chip_sent, self.chip_got = refs[4 * n + 6 :]
 
     @staticmethod
     def scratch():
@@ -538,8 +547,8 @@
                 for p, s in enumerate(blocks)
             ]
             + [pltpu.VMEM(s, WIDE) for s in blocks]
-            + [dma((n, PLANES))] * 6
-            + [dma((n,))] * 2
+            + [dma((n, PLANES))] * 3
+            + [dma((n,))] * 5
         )
 
     def block(self, p, z, near, far, core):
@@ -552,8 +561,8 @@
         return remote(
             self.pair(p, z, 1 - self.place.sides(core)[1], core),
             self.far_got[p].at[z],
-            self.sems[0].at[p, z],
-            self.sems[1].at[p, z],
+            self.far_sent.at[p],
+            self.far_sem.at[p, z],
             self.place.far(core),
         )
 
@@ -562,8 +571,8 @@
         return remote(
             self.block(p, z, 1 - near, far, core),
             self.near_got[p].at[z],
-            self.sems[2].at[p, z],
-            self.sems[3].at[p, z],
+            self.near_sent.at[p],
+            self.near_sem.at[p, z],
             self.place.near(core),
         )
 
@@ -584,13 +593,13 @@
         return self.block(p, z, near, far, core)
 
     def along_z(self, p, z, sender, core):
-        sems = self.sems[4].at[p, z], self.sems[5].at[p, sender]
+        sems = self.z_sent.at[p], self.z_sem.at[p, sender]
         target = self.planes[p].at[sender]
         return remote(self.z_part(p, z, core), target, *sems, self.place.plane(z))
 
     def to_relay(self, p, core, slot):
         first, _, third = self.place.away()
-        sems = self.sems[4].at[p, third], self.sems[5].at[p, slot]
+        sems = self.z_sent.at[p], self.z_sem.at[p, slot]
         target = self.planes[p].at[slot]
         return remote(self.z_part(p, third, core), target, *sems, self.place.plane(first))
 
@@ -647,8 +656,8 @@
         return remote(
             self.final[p].at[pl.ds(rows * (1 - core), rows), columns],
             target,
-            self.sems[6].at[p],
-            self.sems[7].at[p],
+            self.chip_sent.at[p],
+            self.chip_got.at[p],
             self.place.sibling(),
         )
 
@@ -713,23 +722,17 @@
     def drain(self, p):
         place = self.place
 
+        def sent(part, sem):
+            remote(part, part, sem.at[p], sem.at[p], place.sibling()).wait_send()
+
         def run(core):
             self.to_sibling(p, 1 - core).wait_recv()
             self.to_sibling(p, core).wait_send()
-            first, second, third = place.away()
-            for z in (first, second):
-                self.along_z(p, z, place.z, core).wait_send()
-            if p in REDUCE_RELAYED:
-                place.when_inner(lambda: self.along_z(p, third, place.z, core).wait_send())
-                place.when_end(lambda: self.to_relay(p, core, first).wait_send())
-            else:
-                self.along_z(p, third, place.z, core).wait_send()
-            for index, z in enumerate((place.z, first, second, third)):
-                self.along_far(p, z, core).wait_send()
-                if p not in REDUCE_NEAR_LAST or index == 0:
-                    self.along_near(p, z, core).wait_send()
 
         place.by_core(run)
+        sent(self.far_got[p], self.far_sent)
+        sent(self.near_got[p].at[pl.ds(0, 1 if p in REDUCE_NEAR_LAST else 4)], self.near_sent)
+        sent(self.planes[p].at[pl.ds(0, 3)], self.z_sent)
 
 
 def tiled(column, count):
@@ -814,8 +817,8 @@
         vector=vmem((8, VEC_ROWS, TILE), WIDE),
         pair_sent=dma((PAIRS,)),
         pair_got=dma((PAIRS,)),
-        carry_sent=dma((2, PLANES * SIDE)),
-        carry_got=dma((2, PLANES * SIDE)),
+        carry_sent=dma((2,)),
+        carry_got=dma((2,)),
         vector_sent=dma((6,)),
         vector_got=dma((6,)),
     )
@@ -823,7 +826,7 @@
 
 VEC_ROWS = 24
 VEC_COUNT = 18
-PAIRS = 16
+PAIRS = 13
 
 
 class Block:
@@ -959,27 +962,31 @@
                 if step or flip:
                     z = place.turn(step)
                     x = 1 - place.x if flip else place.x
-                    yield z * SIDE + x, place.at(z, x, place.y, place.core)
-
-    def carry_copy(self, way, other, device, sender):
+                    yield place.at(z, x, place.y, place.core)
+
+    def carry_copy(self, way, device):
         return remote(
             self.summaries.at[way, pl.ds(24, 8)],
-            self.every.at[way, sender],
-            self.carry_sent.at[way, other],
-            self.carry_got.at[way, sender],
+            self.every.at[way, self.me],
+            self.carry_sent.at[way],
+            self.carry_got.at[way],
             device,
         )
+
+    def all_carries(self, way):
+        part = self.every.at[way, pl.ds(0, PLANES * SIDE - 1)]
+        sems = self.carry_sent.at[way], self.carry_got.at[way]
+        return remote(part, part, *sems, self.place.sibling())
 
     def scan_own(self, way):
         run = local_backward if way else local_forward
         run(self.retain, *self.parts(), self.turn(), self.summaries.at[way])
         self.every[way, self.me] = self.summaries[way, 24:32]
-        for other, device in self.others():
-            self.carry_copy(way, other, device, self.me).start()
+        for device in self.others():
+            self.carry_copy(way, device).start()
 
     def carried(self, way):
-        for other, device in self.others():
-            self.carry_copy(way, other, device, other).wait_recv()
+        self.all_carries(way).wait_recv()
         turn = self.turn()
         return carry_chain(self.every.at[way], turn, self.me, SLOTS, way == 1)
 
@@ -1208,238 +1215,231 @@
     gather.begin()
     gather.near_own(0)
     gather.z_own(0)
-    gather.near_own(2)
-    gather.near_own(5)
+    gather.near_own(4)
     gather.near_own(3)
     gather.z_own(3)
-    gather.near_own(4)
     gather.near_own(1)
+    gather.near_own(5)
+    gather.near_own(7)
     gather.near_own(6)
+    gather.z_own(1)
+    gather.near_own(2)
+    gather.far_own(0)
+    gather.z_own(5)
     gather.z_own(2)
-    gather.far_own(0)
-    gather.near(0, 0)
+    gather.far_own(4)
     gather.far_own(5)
-    gather.near_own(7)
-    gather.far_own(4)
-    gather.far_own(2)
+    gather.near(0, 1, 0)
+    gather.far_own(6)
+    gather.far_own(3)
     gather.far_own(1)
-    gather.far_own(3)
-    gather.z_own(1)
-    gather.far_own(6)
-    gather.near(0, 1)
-    gather.near(3, 0)
+    gather.near(3, 2, 1)
+    gather.far(0, 1)
     gather.near(0, 2)
+    gather.far(0, 0)
+    gather.near(1, 0, 2)
     gather.z_own(4)
-    gather.near(3, 1)
-    gather.far(0, 1)
-    gather.far_own(7)
     loads[0].wait()
     block.first_norm(raw_tokens)
-    gather.near(3, 2)
+    gather.near(1, 1)
+    gather.near(5, 1)
+    gather.z_own(6)
+    gather.near(5, 0)
     gather.near(2, 0)
-    gather.z_own(5)
-    gather.far(0, 0)
+    gather.far(0, 2)
+    gather.far(1, 2)
+    gather.far(3, 1)
+    gather.chip(0, 1)
+    gather.far(1, 0)
     gather.near(2, 1)
-    gather.far(1, 0)
-    gather.z_own(6)
+    gather.far_own(2)
+    gather.near(3, 0)
+    gather.far(5, 1)
+    gather.chip(0, 0)
+    gather.far(1, 1)
+    gather.near(2, 2)
+    gather.far(2, 0)
+    gather.far_own(7)
+    gather.chip(0, 2, 3)
+    gather.chip(6, 0)
+    gather.near(5, 2)
     loads[1].wait()
     block.mask_upstream(raw_upstream)
-    gather.chip(1, 0)
-    gather.near(4, 1)
-    gather.far(3, 0, 1)
+    gather.chip(1, 3)
+    gather.arrive(0)
+    gather.far(3, 2)
+    block.mix(0)
+    gather.far(3, 0)
+    block.drives()
+    gather.chip(3, 2)
+    block.scan_own(0)
+    gather.chip(4, 0)
+    gather.far(5, 0)
+    gather.chip(2, 0)
+    gather.far(4, 2, 1)
+    gather.z_own(7)
+    gather.far(2, 2)
+    gather.chip(5, 0)
+    block.give("upstream")
+    gather.far(6, 1)
+    gather.chip(3, 0)
+    gather.far(5, 2)
+    gather.chip(1, 2)
+    gather.chip(2, 1)
+    gather.chip(1, 1, 0)
+    gather.chip(5, 2)
+    gather.far(4, 0)
+    gather.chip(7, 0)
     gather.far(2, 1)
-    gather.near(2, 2)
-    gather.near(5, 1, 0)
+    gather.chip(3, 3)
+    gather.arrive(1)
     block.give("normed")
-    gather.near(4, 2)
-    gather.far(3, 2)
-    gather.far(1, 1)
-    gather.far(2, 0)
-    gather.z_own(7)
-    gather.chip(5, 0)
-    gather.chip(6, 0)
-    gather.far(0, 2)
-    gather.chip(0, 2)
-    gather.chip(3, 0)
-    gather.chip(0, 0)
-    gather.far(4, 1)
-    gather.near(4, 0)
-    gather.far(2, 2)
-    gather.near(5, 2)
-    gather.far(4, 2)
-    gather.chip(7, 0)
-    gather.far(6, 1)
-    gather.chip(0, 1)
-    gather.far(1, 2)
-    gather.chip(4, 0)
-    gather.chip(0, 3)
-    gather.chip(2, 1)
-    gather.chip(3, 2)
-    gather.chip(1, 2)
-    gather.far(4, 0)
     gather.chip(3, 1)
+    gather.far(6, 0)
+    block.mix(1)
+    gather.far(6, 2)
+    block.take("upstream")
+    gather.chip(5, 3)
     gather.chip(2, 3)
-    gather.far(5, 0)
     gather.chip(4, 3)
-    gather.far(5, 1)
-    gather.arrive(0)
-    gather.chip(2, 0)
-    block.give("upstream")
-    gather.chip(1, 1)
-    gather.chip(4, 2)
-    block.mix(0)
-    gather.far(6, 0)
-    gather.chip(1, 3)
-    gather.chip(3, 3)
-    block.drives()
-    block.scan_own(0)
+    gather.far(7, 0)
+    block.scan_states()
+    gather.chip(4, 2, 1)
+    gather.chip(2, 2)
+    gather.arrive(3)
+    gather.far(7, 2)
+    block.take("normed")
+    gather.chip(6, 2)
     gather.chip(5, 1)
-    gather.far(5, 2)
-    gather.chip(2, 2)
-    gather.chip(6, 2)
-    gather.chip(4, 1)
-    gather.far(6, 2)
+    block.gate_rows()
+    gather.arrive(4)
+    gather.chip(6, 1)
     gather.far(7, 1)
-    gather.chip(6, 1)
-    gather.far(7, 0)
     gather.arrive(2)
-    gather.chip(5, 2)
-    gather.far(7, 2)
-    gather.arrive(1)
-    gather.arrive(3)
-    block.mix(1)
-    gather.chip(5, 3)
-    block.scan_states()
-    gather.arrive(4)
-    block.gate_rows()
+    block.second_norm()
     gather.chip(6, 3)
-    block.give("gated")
-    block.second_norm()
     gather.arrive(5)
-    gather.chip(7, 2)
     block.give("normed_two")
     block.glu_forward(0)
+    gather.chip(7, 1)
     gather.arrive(6)
-    gather.chip(7, 3)
-    block.take("gated")
-    gather.chip(7, 1)
     block.give(("d_glu", 0))
+    block.glu_back(0)
+    gather.chip(7, 3, 2)
     block.glu_forward(1)
+    block.give(("d_glu", 1), ("hidden", 1))
+    block.take("normed_two")
+    block.glu_back(1)
+    gather.arrive(7)
+    block.glu_forward(2)
+    block.give(("d_glu", 2), "gated")
+    block.take(("d_glu", 1))
+    block.give(("hidden", 2))
+    block.take(("hidden", 1), ("d_glu", 0))
+    block.glu_grads(1)
+    reduce.far(6)
+    block.take(("d_glu", 2))
+    block.glu_back(2)
+    block.middle_back()
+    block.gate_back()
+    block.scan_own(1)
     block.give(("hidden", 0))
-    gather.arrive(7)
-    block.give(("d_glu", 1))
-    block.glu_forward(2)
-    block.give(("hidden", 2))
-    block.take("normed", "upstream", ("hidden", 0), "normed_two")
-    block.give(("d_glu", 2))
-    block.take(("d_glu", 0))
-    block.glu_grads(0)
-    reduce.far(5)
-    block.glu_back(0)
-    block.take(("d_glu", 2))
-    block.give(("hidden", 1))
-    block.take(("hidden", 2))
+    block.take("gated", ("hidden", 2))
     block.glu_grads(2)
     reduce.far(7)
-    block.take(("d_glu", 1))
-    block.glu_back(1)
-    block.take(("hidden", 1))
-    reduce.after_far(5, 0)
-    block.glu_grads(1)
-    reduce.after_far(5, 1)
-    block.glu_back(2)
-    reduce.far(6)
-    block.middle_back()
-    reduce.after_far(7, 0)
     block.give("d_out")
-    reduce.after_far(5, 2)
-    block.gate_back()
+    reduce.after_far(6, 1)
+    block.take(("hidden", 0))
+    block.glu_grads(0)
+    reduce.after_far(6, 2)
     block.take("d_out")
     block.mixer_out_grad()
     reduce.far(4)
-    reduce.far(2)
-    block.give("d_gate")
-    reduce.after_far(6, 0)
-    block.scan_own(1)
-    block.take("d_gate")
-    block.mix_grads(1)
-    reduce.after_far(7, 2)
-    reduce.after_far(4, 0)
-    reduce.far(1)
+    reduce.after_far(7, 0)
     reduce.far(3)
     block.scan_back()
-    reduce.after_far(7, 1)
-    reduce.after_far(4, 1)
     block.drives_back()
-    reduce.after_far(2, 1)
+    reduce.after_far(6, 0)
+    reduce.after_far(4, 0)
+    block.give("d_gate")
+    reduce.far(2)
+    reduce.after_far(7, 2)
+    block.gate_normed()
+    block.take("d_gate")
     block.give("d_drive")
     block.take("d_drive")
+    reduce.far(5)
+    reduce.after_far(3, 0)
+    reduce.after_far(6, 3)
+    reduce.after_far(4, 2)
     block.mix_grads(0)
-    reduce.after_far(2, 0)
-    reduce.after_far(1, 0)
-    reduce.after_far(4, 2)
-    reduce.far(0)
-    reduce.after_near(6, 0)
-    reduce.after_far(1, 2)
-    block.gate_normed()
-    reduce.after_far(7, 3)
-    reduce.after_far(3, 0)
-    reduce.after_far(2, 3)
-    block.first_back()
-    reduce.after_far(1, 1)
-    reduce.after_far(2, 2)
-    reduce.after_far(5, 3)
-    reduce.after_near(1, 0)
-    reduce.after_near(3, 0)
-    reduce.after_far(3, 1)
-    reduce.after_far(0, 0)
+    block.mix_grads(1)
+    reduce.after_far(7, 1)
+    reduce.after_far(2, 1)
     block.natural_out()
     leave_out.start()
+    reduce.far(1)
+    reduce.after_far(3, 1)
+    block.first_back()
+    reduce.after_far(2, 0)
     block.gather_vector()
+    reduce.after_far(5, 0)
+    reduce.after_near(4, 0)
+    block.natural_tokens()
+    leave_tokens.start()
+    reduce.after_far(3, 3)
+    reduce.far(0)
+    reduce.after_far(3, 2)
+    reduce.after_far(7, 3)
+    reduce.after_far(1, 0)
+    reduce.after_near(5, 0)
+    reduce.after_far(1, 2)
+    reduce.after_far(2, 2)
+    reduce.after_far(4, 1)
+    reduce.after_far(0, 0)
+    reduce.after_near(4, 2)
+    reduce.after_near(1, 2)
+    reduce.after_far(5, 1)
+    reduce.after_near(4, 1)
+    reduce.after_far(1, 1)
+    reduce.after_far(0, 1)
+    reduce.after_far(2, 3)
+    reduce.after_near(1, 0)
+    reduce.after_far(4, 3)
+    reduce.after_near(0, 0)
+    reduce.after_near(7)
+    block.vector_step(0)
+    reduce.after_far(0, 2)
+    block.vector_step(1)
+    reduce.after_near(5, 1)
+    reduce.after_near(3)
     reduce.after_near(1, 1)
-    reduce.after_far(6, 1)
-    reduce.after_near(3, 1)
-    block.vector_step(0)
-    reduce.after_far(0, 1)
-    reduce.after_near(1, 2)
-    block.vector_step(1)
-    reduce.after_near(0, 0)
-    reduce.after_far(0, 2)
-    reduce.after_far(3, 2)
-    reduce.after_near(6, 1)
-    reduce.after_far(4, 3)
-    reduce.after_near(5)
-    reduce.after_far(6, 2)
+    reduce.after_far(5, 2)
     reduce.after_far(1, 3)
-    reduce.after_far(3, 3)
+    reduce.after_far(0, 3)
     reduce.after_near(0, 1)
     reduce.after_near(2)
+    reduce.after_near(4, 3)
     block.vector_step(2)
     reduce.after_near(0, 2)
-    reduce.after_far(0, 3)
-    reduce.after_near(7)
-    reduce.after_far(6, 3)
-    reduce.after_near(4)
-    reduce.after_near(3, 2)
-    reduce.after_near(6, 2)
-    block.natural_tokens()
-    leave_tokens.start()
+    reduce.after_far(5, 3)
+    reduce.after_near(6)
+    reduce.after_near(5, 2)
+    reduce.after_near(1, 3)
+    reduce.after_near(0, 3)
+    reduce.finish(7)
+    reduce.finish(1)
     block.vector_step(3)
     for step in (1, 2, 3):
         block.vector_plane(planes, step, place.z).start()
     planes[place.z] = block.vector[3]
-    reduce.after_near(0, 3)
-    reduce.finish(5)
-    reduce.after_near(1, 3)
     reduce.finish(2)
-    reduce.finish(1)
-    reduce.finish(7)
-    reduce.after_near(6, 3)
     reduce.finish(4)
-    reduce.after_near(3, 3)
+    reduce.finish(6)
+    reduce.after_near(5, 3)
     reduce.finish(0)
     reduce.finish(3)
-    reduce.finish(6)
+    reduce.finish(5)
 
     for step in (1, 2, 3):
         block.vector_plane(planes, step, place.z).wait_send()
@@ -1447,8 +1447,7 @@
     for stage in range(3):
         block.vector_copy(stage).wait_send()
     for way in range(2):
-        for other, device in block.others():
-            block.carry_copy(way, other, device, block.me).wait_send()
+        block.all_carries(way).wait_send()
     block.settle()
     for p in range(n):
         gather.drain(p)
@@ -1513,11 +1512,14 @@
             ref[...] = value
     master, first, second = (ref[...] for ref in ins[8:])
     results = step(vectors[:VEC_COUNT], master, first, second, 0.0)
-    for ref, value in zip(outs[12:], results, strict=True):
-        ref[...] = value
-
-
-UPDATE_BLOCKS = 3
+    for ref, value in zip(outs[12:16], results, strict=True):
+        for i in range(VEC_COUNT):
+            ref[pl.ds(i * TILE, TILE)] = value[i]
+    for i in range(CH // TILE):
+        outs[16][pl.ds(i * TILE, TILE)] = results[0][VEC_COUNT - CH // TILE + i]
+
+
+UPDATE_BLOCKS = 1
 
 
 def update(counter, planes, block_out, d_tokens, sums, masters, moments, vector_state):
@@ -1537,7 +1539,8 @@
         jax.ShapeDtypeStruct(d_tokens.shape, d_tokens.dtype),
     ]
     out_shape += [jax.ShapeDtypeStruct(shape, kind) for shape in shapes for kind in types]
-    out_shape += [jax.ShapeDtypeStruct((VEC_COUNT, TILE), WIDE)] * 4
+    lines = [(VEC_COUNT * TILE,)] * 4 + [(CH,)]
+    out_shape += [jax.ShapeDtypeStruct(line, WIDE) for line in lines]
     operands = []
     for k in range(2):
         operands += [sums[k], masters[k], *moments[k]]
@@ -1550,7 +1553,7 @@
         + [columns[0]] * 4
         + [columns[1]] * 4
         + [vector] * 3,
-        out_specs=[by_columns(block_out.shape)] * 2 + [columns[0]] * 5 + [columns[1]] * 5 + [vector] * 4,
+        out_specs=[by_columns(block_out.shape)] * 2 + [columns[0]] * 5 + [columns[1]] * 5 + [whole(line) for line in lines],
         compiler_params=pltpu.CompilerParams(vmem_limit_bytes=VMEM_BYTES),
     )(counter, planes, block_out, d_tokens, *operands, *vector_state)
 
@@ -1689,13 +1692,13 @@
             counter, planes, block_out, d_tokens, sums, masters, moments, lines
         )
         block_out, d_tokens = results[:2]
-        grad_vec, update_vec, first_vec, second_vec = (x.reshape(-1) for x in results[12:])
+        grad_vec, update_vec, first_vec, second_vec, grad_bias = results[12:]
         return (
             block_out[None],
             d_tokens[None],
             *results[2:12],
             grad_vec,
-            grad_vec[2 * D + CH :],
+            grad_bias,
             update_vec,
             first_vec,
             second_vec,

time: 127 us -> 120 us (0.945)
  Pallas kernels: 122 us -> 116 us
  local copies, waits for them, and re-layouts: 1.28 us -> 0 us
    pallas_call x1, Pallas kernels: 116 us -> 111 us  [block_routed(): pl.pallas_call(block_kernel, out_shape=out_shape, in_specs=[anywhere, any...]
    slice x1 -> x0, local copies, waits for them, and re-layouts: 1.28 us -> none  [body(): grad_vec[2 * D + CH:]]
where the time goes in v6:
time: 120 us; the launch traced here: 118 us
  Pallas kernels  116 us (97%)
  between operations  1.51 us (1%)
    pallas_call x1, Pallas kernels, block_routed(): pl.pallas_call(block_kernel, out_shape=out_shape, in_specs=[anywhere, any...  111 us
    pallas_call x1, Pallas kernels, update(): pl.pallas_call(update_kernel, grid=(UPDATE_BLOCKS,), out_shape=out_shape,...  5.15 us

profile of v6, /device:TPU:3, one launch (start us, length us, event | category | flops | bytes accessed | tf_op | source)
XLA Modules:
  0.0 117.8 jit_solution(13488887412379827310)
XLA Ops:
  1.3 111.1 %shard_map.269 = (bf16[512,768]{1,0:T(8,128)(2,1)}, f32[512,768]{1,0:T(8,128)}, f32[24,4992]{1,0:T(8,128)}, f32[72,768]{1,0:T(8,128)}, f32[4,24,128]{2,1,0:T(8,128)}) custom-call(bf16[1,512,768]{2,1,0:T(8,128)(2,1)} %tokens.1, bf16[1,512,768]{2,1,0:T(8,128)(2,1)} %cotangent.1, s32[1,512]{1,0:T(1,128)} %padding.1, s32[1,512]{1,0:T(1,128)} %opening.1, ...), custom_call_target="tpu_custom_call" | custom-call | tf_op jit(solution)/shard_map/pallas_call | solution.py:1470
  112.4 5.1 %shard_map.270 = (bf16[512,768]{1,0:T(8,128)(2,1)}, f32[512,768]{1,0:T(8,128)}, f32[24,4992]{1,0:T(8,128)}, f32[24,4992]{1,0:T(8,128)}, f32[24,4992]{1,0:T(8,128...) custom-call(s32[1]{0:T(128)S(6)} %copy.31.counter, ...), custom_call_target="tpu_custom_call" | custom-call | tf_op jit(solution)/shard_map/pallas_call | solution.py:1547

commit v7 on v6

--- a/solution.py
+++ b/solution.py
@@ -340,8 +340,8 @@
 
 GATHER_NEAR_FIRST = (4, 6, 7)
 REDUCE_NEAR_LAST = (2, 3, 6, 7)
-GATHER_RELAYED = (0, 2, 4, 5, 6)
-REDUCE_RELAYED = (0, 2, 3, 4, 5, 7)
+GATHER_RELAYED = (0, 1, 2, 3, 4, 5)
+REDUCE_RELAYED = (0, 1, 3, 4, 5, 6, 7)
 
 
 class Gather:
@@ -1215,231 +1215,232 @@
     gather.begin()
     gather.near_own(0)
     gather.z_own(0)
+    gather.near_own(3)
+    gather.near_own(1)
+    gather.near_own(2)
+    gather.near_own(6)
     gather.near_own(4)
-    gather.near_own(3)
-    gather.z_own(3)
-    gather.near_own(1)
-    gather.near_own(5)
-    gather.near_own(7)
-    gather.near_own(6)
     gather.z_own(1)
-    gather.near_own(2)
-    gather.far_own(0)
-    gather.z_own(5)
     gather.z_own(2)
-    gather.far_own(4)
-    gather.far_own(5)
-    gather.near(0, 1, 0)
-    gather.far_own(6)
-    gather.far_own(3)
-    gather.far_own(1)
-    gather.near(3, 2, 1)
-    gather.far(0, 1)
-    gather.near(0, 2)
-    gather.far(0, 0)
-    gather.near(1, 0, 2)
-    gather.z_own(4)
     loads[0].wait()
     block.first_norm(raw_tokens)
-    gather.near(1, 1)
-    gather.near(5, 1)
-    gather.z_own(6)
+    gather.near_own(7)
+    gather.near_own(5)
+    gather.far_own(0)
+    gather.far_own(3)
+    gather.z_own(3)
+    gather.far_own(2)
+    gather.near(0, 1)
+    gather.z_own(5)
+    loads[1].wait()
+    block.mask_upstream(raw_upstream)
+    gather.near(1, 0)
+    gather.near(0, 0)
+    block.give("normed")
+    gather.far_own(7)
+    gather.far_own(5)
+    gather.far_own(4)
+    gather.far_own(6)
+    gather.near(0, 2)
+    gather.far(0, 1)
+    gather.near(1, 2)
+    gather.near(2, 0)
+    gather.z_own(4)
+    gather.near(3, 0)
+    gather.far(0, 0)
+    gather.far(1, 0)
+    gather.near(3, 1)
     gather.near(5, 0)
-    gather.near(2, 0)
+    gather.near(2, 1)
+    gather.chip(2, 0)
     gather.far(0, 2)
     gather.far(1, 2)
+    gather.near(3, 2)
+    gather.z_own(6)
+    gather.chip(6, 0)
+    gather.far(5, 0)
+    gather.near(1, 1)
+    gather.near(2, 2)
+    gather.far(3, 2)
+    gather.chip(0, 0)
+    gather.far_own(1)
+    gather.far(2, 0)
+    gather.near(5, 2)
+    gather.far(4, 1)
+    gather.far(1, 1)
+    gather.far(4, 2)
+    gather.chip(7, 0)
+    gather.chip(0, 3)
+    gather.z_own(7)
+    gather.chip(1, 0)
+    gather.near(5, 1)
+    gather.chip(0, 1)
+    gather.far(3, 0)
+    gather.chip(4, 0)
+    gather.far(2, 1)
+    gather.chip(0, 2)
     gather.far(3, 1)
-    gather.chip(0, 1)
-    gather.far(1, 0)
-    gather.near(2, 1)
-    gather.far_own(2)
-    gather.near(3, 0)
-    gather.far(5, 1)
-    gather.chip(0, 0)
-    gather.far(1, 1)
-    gather.near(2, 2)
-    gather.far(2, 0)
-    gather.far_own(7)
-    gather.chip(0, 2, 3)
-    gather.chip(6, 0)
-    gather.near(5, 2)
-    loads[1].wait()
-    block.mask_upstream(raw_upstream)
     gather.chip(1, 3)
+    gather.far(6, 1)
     gather.arrive(0)
-    gather.far(3, 2)
+    gather.far(2, 2)
+    gather.chip(4, 2)
+    gather.chip(1, 2)
+    block.take("normed")
+    block.give("upstream")
+    gather.far(5, 1, 2)
     block.mix(0)
-    gather.far(3, 0)
+    gather.chip(5, 1)
+    gather.chip(3, 2)
+    gather.chip(2, 1)
+    gather.chip(3, 0, 1)
+    gather.far(4, 0)
+    gather.chip(2, 2)
     block.drives()
-    gather.chip(3, 2)
+    gather.chip(1, 1)
     block.scan_own(0)
-    gather.chip(4, 0)
-    gather.far(5, 0)
-    gather.chip(2, 0)
-    gather.far(4, 2, 1)
-    gather.z_own(7)
-    gather.far(2, 2)
-    gather.chip(5, 0)
-    block.give("upstream")
-    gather.far(6, 1)
-    gather.chip(3, 0)
-    gather.far(5, 2)
-    gather.chip(1, 2)
-    gather.chip(2, 1)
-    gather.chip(1, 1, 0)
-    gather.chip(5, 2)
-    gather.far(4, 0)
-    gather.chip(7, 0)
-    gather.far(2, 1)
-    gather.chip(3, 3)
-    gather.arrive(1)
-    block.give("normed")
-    gather.chip(3, 1)
-    gather.far(6, 0)
-    block.mix(1)
-    gather.far(6, 2)
-    block.take("upstream")
-    gather.chip(5, 3)
     gather.chip(2, 3)
     gather.chip(4, 3)
+    gather.far(6, 2)
+    gather.chip(3, 3)
+    gather.far(6, 0)
+    gather.chip(5, 0, 2)
+    gather.chip(4, 1)
+    gather.far(7, 1, 2)
+    gather.arrive(3)
+    gather.chip(5, 3)
     gather.far(7, 0)
+    gather.arrive(1)
+    block.mix(1)
+    gather.chip(6, 2)
+    block.take("upstream")
+    gather.arrive(2)
+    gather.arrive(4)
     block.scan_states()
-    gather.chip(4, 2, 1)
-    gather.chip(2, 2)
-    gather.arrive(3)
-    gather.far(7, 2)
-    block.take("normed")
-    gather.chip(6, 2)
-    gather.chip(5, 1)
+    gather.arrive(5)
     block.gate_rows()
-    gather.arrive(4)
-    gather.chip(6, 1)
-    gather.far(7, 1)
-    gather.arrive(2)
     block.second_norm()
-    gather.chip(6, 3)
-    gather.arrive(5)
+    gather.chip(6, 1, 3)
     block.give("normed_two")
     block.glu_forward(0)
+    gather.chip(7, 3)
+    gather.arrive(6)
+    gather.chip(7, 2)
+    block.glu_forward(1)
     gather.chip(7, 1)
-    gather.arrive(6)
-    block.give(("d_glu", 0))
+    block.give(("d_glu", 1), ("hidden", 1))
     block.glu_back(0)
-    gather.chip(7, 3, 2)
-    block.glu_forward(1)
-    block.give(("d_glu", 1), ("hidden", 1))
-    block.take("normed_two")
-    block.glu_back(1)
+    block.give(("hidden", 0))
     gather.arrive(7)
     block.glu_forward(2)
-    block.give(("d_glu", 2), "gated")
+    block.give(("hidden", 2))
     block.take(("d_glu", 1))
-    block.give(("hidden", 2))
-    block.take(("hidden", 1), ("d_glu", 0))
+    block.give(("d_glu", 2), ("d_glu", 0))
+    block.take(("hidden", 1), "normed_two")
     block.glu_grads(1)
     reduce.far(6)
-    block.take(("d_glu", 2))
+    block.glu_back(1)
+    block.take(("hidden", 2), ("d_glu", 2))
+    block.glu_grads(2)
+    block.take(("hidden", 0))
+    reduce.far(7)
     block.glu_back(2)
+    reduce.after_far(6, 0)
+    block.take(("d_glu", 0))
     block.middle_back()
     block.gate_back()
     block.scan_own(1)
-    block.give(("hidden", 0))
-    block.take("gated", ("hidden", 2))
-    block.glu_grads(2)
-    reduce.far(7)
+    block.give("gated")
+    block.glu_grads(0)
+    reduce.far(5)
     block.give("d_out")
     reduce.after_far(6, 1)
-    block.take(("hidden", 0))
-    block.glu_grads(0)
+    block.give("d_gate")
+    block.take("gated")
+    block.gate_normed()
+    block.take("d_out")
+    reduce.after_far(7, 1)
+    block.mixer_out_grad()
+    block.scan_back()
+    reduce.after_far(7, 3)
+    reduce.after_far(5, 0)
+    reduce.far(3)
+    reduce.far(2)
+    reduce.after_far(7, 0)
+    block.drives_back()
+    block.take("d_gate")
     reduce.after_far(6, 2)
-    block.take("d_out")
-    block.mixer_out_grad()
+    block.first_back()
+    block.mix_grads(1)
+    reduce.after_far(3, 0)
+    reduce.after_far(7, 2)
+    reduce.after_far(5, 1)
+    block.give("d_drive")
+    block.natural_tokens()
+    leave_tokens.start()
+    block.gather_vector()
+    block.vector_step(0)
+    reduce.far(1)
+    block.take("d_drive")
+    reduce.after_far(5, 2)
+    reduce.after_far(2, 0)
+    reduce.after_near(5, 0)
+    block.mix_grads(0)
     reduce.far(4)
-    reduce.after_far(7, 0)
-    reduce.far(3)
-    block.scan_back()
-    block.drives_back()
-    reduce.after_far(6, 0)
-    reduce.after_far(4, 0)
-    block.give("d_gate")
-    reduce.far(2)
-    reduce.after_far(7, 2)
-    block.gate_normed()
-    block.take("d_gate")
-    block.give("d_drive")
-    block.take("d_drive")
-    reduce.far(5)
-    reduce.after_far(3, 0)
-    reduce.after_far(6, 3)
-    reduce.after_far(4, 2)
-    block.mix_grads(0)
-    block.mix_grads(1)
-    reduce.after_far(7, 1)
-    reduce.after_far(2, 1)
+    reduce.after_far(2, 2)
+    reduce.after_far(3, 2, 1)
+    reduce.far(0)
     block.natural_out()
     leave_out.start()
-    reduce.far(1)
-    reduce.after_far(3, 1)
-    block.first_back()
-    reduce.after_far(2, 0)
-    block.gather_vector()
-    reduce.after_far(5, 0)
+    reduce.after_far(1, 1)
+    block.vector_step(1)
+    reduce.after_far(1, 0)
+    reduce.after_near(1, 0)
+    reduce.after_far(1, 2)
+    reduce.after_near(5, 1)
+    reduce.after_far(2, 1, 3)
+    reduce.after_near(1, 1)
+    reduce.after_far(6, 3)
+    reduce.after_far(4, 0)
+    reduce.after_far(5, 3)
+    reduce.after_far(0, 0)
+    reduce.after_far(4, 1)
     reduce.after_near(4, 0)
-    block.natural_tokens()
-    leave_tokens.start()
+    reduce.after_far(0, 1)
     reduce.after_far(3, 3)
-    reduce.far(0)
-    reduce.after_far(3, 2)
-    reduce.after_far(7, 3)
-    reduce.after_far(1, 0)
-    reduce.after_near(5, 0)
-    reduce.after_far(1, 2)
-    reduce.after_far(2, 2)
-    reduce.after_far(4, 1)
-    reduce.after_far(0, 0)
+    reduce.after_near(5, 2)
+    reduce.after_near(1, 2)
+    reduce.after_near(0, 0)
+    reduce.after_far(4, 2)
+    reduce.after_far(1, 3)
+    reduce.after_near(4, 1)
+    reduce.after_far(0, 2)
+    reduce.after_near(2)
+    reduce.after_near(0, 1)
+    reduce.after_near(5, 3)
+    reduce.finish(5)
+    reduce.after_near(6)
+    reduce.after_far(4, 3)
+    block.vector_step(2)
+    reduce.after_near(3)
+    reduce.after_near(1, 3)
+    reduce.after_far(0, 3)
     reduce.after_near(4, 2)
-    reduce.after_near(1, 2)
-    reduce.after_far(5, 1)
-    reduce.after_near(4, 1)
-    reduce.after_far(1, 1)
-    reduce.after_far(0, 1)
-    reduce.after_far(2, 3)
-    reduce.after_near(1, 0)
-    reduce.after_far(4, 3)
-    reduce.after_near(0, 0)
+    reduce.after_near(0, 2)
     reduce.after_near(7)
-    block.vector_step(0)
-    reduce.after_far(0, 2)
-    block.vector_step(1)
-    reduce.after_near(5, 1)
-    reduce.after_near(3)
-    reduce.after_near(1, 1)
-    reduce.after_far(5, 2)
-    reduce.after_far(1, 3)
-    reduce.after_far(0, 3)
-    reduce.after_near(0, 1)
-    reduce.after_near(2)
-    reduce.after_near(4, 3)
-    block.vector_step(2)
-    reduce.after_near(0, 2)
-    reduce.after_far(5, 3)
-    reduce.after_near(6)
-    reduce.after_near(5, 2)
-    reduce.after_near(1, 3)
-    reduce.after_near(0, 3)
-    reduce.finish(7)
-    reduce.finish(1)
+    reduce.finish(6)
     block.vector_step(3)
     for step in (1, 2, 3):
         block.vector_plane(planes, step, place.z).start()
     planes[place.z] = block.vector[3]
+    reduce.finish(1)
     reduce.finish(2)
+    reduce.after_near(0, 3)
+    reduce.after_near(4, 3)
     reduce.finish(4)
-    reduce.finish(6)
-    reduce.after_near(5, 3)
+    reduce.finish(7)
+    reduce.finish(3)
     reduce.finish(0)
-    reduce.finish(3)
-    reduce.finish(5)
 
     for step in (1, 2, 3):
         block.vector_plane(planes, step, place.z).wait_send()

time: 120 us -> 118 us (0.983)
  Pallas kernels: 116 us -> 114 us
    pallas_call x1, Pallas kernels: 111 us -> 109 us  [block_routed(): pl.pallas_call(block_kernel, out_shape=out_shape, in_specs=[anywhere, any...]
where the time goes in v7:
time: 118 us; the launch traced here: 116 us
  Pallas kernels  114 us (97%)
  between operations  1.51 us (1%)
    pallas_call x1, Pallas kernels, block_routed(): pl.pallas_call(block_kernel, out_shape=out_shape, in_specs=[anywhere, any...  109 us
    pallas_call x1, Pallas kernels, update(): pl.pallas_call(update_kernel, grid=(UPDATE_BLOCKS,), out_shape=out_shape,...  5.13 us

profile of v7, /device:TPU:3, one launch (start us, length us, event | category | flops | bytes accessed | tf_op | source)
XLA Modules:
  0.0 115.9 jit_solution(8354073570682682832)
XLA Ops:
  1.3 109.3 %shard_map.269 = (bf16[512,768]{1,0:T(8,128)(2,1)}, f32[512,768]{1,0:T(8,128)}, f32[24,4992]{1,0:T(8,128)}, f32[72,768]{1,0:T(8,128)}, f32[4,24,128]{2,1,0:T(8,128)}) custom-call(bf16[1,512,768]{2,1,0:T(8,128)(2,1)} %tokens.1, bf16[1,512,768]{2,1,0:T(8,128)(2,1)} %cotangent.1, s32[1,512]{1,0:T(1,128)} %padding.1, s32[1,512]{1,0:T(1,128)} %opening.1, ...), custom_call_target="tpu_custom_call" | custom-call | tf_op jit(solution)/shard_map/pallas_call | solution.py:1471
  110.6 5.1 %shard_map.270 = (bf16[512,768]{1,0:T(8,128)(2,1)}, f32[512,768]{1,0:T(8,128)}, f32[24,4992]{1,0:T(8,128)}, f32[24,4992]{1,0:T(8,128)}, f32[24,4992]{1,0:T(8,128...) custom-call(s32[1]{0:T(128)S(6)} %copy.31.counter, ...), custom_call_target="tpu_custom_call" | custom-call | tf_op jit(solution)/shard_map/pallas_call | solution.py:1548

commit v8 on v7

--- a/solution.py
+++ b/solution.py
@@ -663,7 +663,7 @@
 
     @staticmethod
     def add(target, source):
-        target[...] = (target[...].astype(WIDE) + source[...].astype(WIDE)).astype(LOW)
+        target[...] = target[...] + source[...]
 
     def far(self, p):
         def run(core):

time: 118 us -> 118 us (level)
  no operation moved by 1% of the time
where the time goes in v8:
time: 118 us; the launch traced here: 116 us
  Pallas kernels  114 us (97%)
  between operations  1.51 us (1%)
    pallas_call x1, Pallas kernels, block_routed(): pl.pallas_call(block_kernel, out_shape=out_shape, in_specs=[anywhere, any...  109 us
    pallas_call x1, Pallas kernels, update(): pl.pallas_call(update_kernel, grid=(UPDATE_BLOCKS,), out_shape=out_shape,...  5.13 us

profile of v8, /device:TPU:3, one launch (start us, length us, event | category | flops | bytes accessed | tf_op | source)
XLA Modules:
  0.0 115.9 jit_solution(2491619725824870586)
XLA Ops:
  1.3 109.2 %shard_map.269 = (bf16[512,768]{1,0:T(8,128)(2,1)}, f32[512,768]{1,0:T(8,128)}, f32[24,4992]{1,0:T(8,128)}, f32[72,768]{1,0:T(8,128)}, f32[4,24,128]{2,1,0:T(8,128)}) custom-call(bf16[1,512,768]{2,1,0:T(8,128)(2,1)} %tokens.1, bf16[1,512,768]{2,1,0:T(8,128)(2,1)} %cotangent.1, s32[1,512]{1,0:T(1,128)} %padding.1, s32[1,512]{1,0:T(1,128)} %opening.1, ...), custom_call_target="tpu_custom_call" | custom-call | tf_op jit(solution)/shard_map/pallas_call | solution.py:1471
  110.5 5.1 %shard_map.270 = (bf16[512,768]{1,0:T(8,128)(2,1)}, f32[512,768]{1,0:T(8,128)}, f32[24,4992]{1,0:T(8,128)}, f32[24,4992]{1,0:T(8,128)}, f32[24,4992]{1,0:T(8,128...) custom-call(s32[1]{0:T(128)S(6)} %copy.31.counter, ...), custom_call_target="tpu_custom_call" | custom-call | tf_op jit(solution)/shard_map/pallas_call | solution.py:1548
